TPU v7x, 32 devices: a whole 2x2x4 slice. The times are simulated.
32 devices in a mesh: chan: 4 (over x, core), space: 8 (over z, y).
Axes of the slice: x: 2, y: 2, z: 4, core: 2. Of those that a mesh axis runs over, the one named last changes fastest.
Arguments:
- velocity: float32 [2, 4, 256, 256], P(None, None, 'space'), may hold values from -6 to 6
- w_first: bfloat16 [3, 3, 2, 64], P(None, None, None, 'chan'), may hold values from -2 to 2
- b_first: bfloat16 [64], P('chan'), may hold values from -3 to 3
- w_mid: bfloat16 [5, 3, 3, 64, 64], P(None, None, None, None, 'chan'), may hold values from -0.375 to 0.375
- b_mid: bfloat16 [5, 64], P(None, 'chan'), may hold values from -3 to 3
- w_last: bfloat16 [3, 3, 64, 32], P(None, None, None, 'chan'), may hold values from -0.1875 to 0.1875
- b_last: bfloat16 [32], P('chan'), may hold values from -3 to 3
- offsets: int32 [2, 16], replicated, may hold values from 0 to 15, each once within a row
- cotangent: float32 [2, 4, 256, 256], P(None, None, 'space'), may hold values from -6 to 6
Outputs:
- new_velocity: float32 [2, 4, 256, 256], P(None, None, 'space')
- velocity_grad: float32 [2, 4, 256, 256], P(None, 'chan', 'space')
- w_first_grad: float32 [3, 3, 2, 64], P(None, None, None, 'chan')
- b_first_grad: float32 [64], P('chan')
- w_mid_grad: float32 [5, 3, 3, 64, 64], P(None, None, None, None, 'chan')
- b_mid_grad: float32 [5, 64], P(None, 'chan')
- w_last_grad: float32 [3, 3, 64, 32], P(None, None, None, 'chan')
- b_last_grad: float32 [32], P('chan')
- rms_stats: float32 [4], replicated
Inputs may be any that keep to these rules, and one draw needn't show every extreme that they name: `offsets`: each row names every stencil point 0 to 15 once.
All inputs are finite; a program needn't handle non-finite values.
Results may differ from a plain program's by a relative error of at most 0.015.
The roundings to bfloat16 on the way count: a program that leaves them out, or rounds other values in their place, can miss the bound.
Values may be sent and summed in bfloat16 or wider, within the bound.
No kernel may reach another device: no remote copies, remote signals or barrier semaphores. Data moves between devices by JAX's collectives and lax.ppermute only.
A program may use at most 704 MiB of HBM per device.

v0:
```python
import jax
import jax.numpy as jnp
from jax import lax
from jax.sharding import PartitionSpec as P

highest = lax.Precision.HIGHEST
time_step = 0.2
viscosity = 0.256


def with_halo(array, sides, width):
    for axis, dim in sides:
        peers, length = (lax.axis_size(axis), array.shape[dim])
        up = [(i, (i + 1) % peers) for i in range(peers)]
        down = [(j, i) for i, j in up]
        last = lax.slice_in_dim(array, length - width, length, axis=dim)
        initial = lax.slice_in_dim(array, 0, width, axis=dim)
        before = lax.ppermute(last, axis, up)
        after = lax.ppermute(initial, axis, down)
        array = jnp.concatenate([before, array, after], axis=dim)
    return array


def shifted_2(block, axis, distance):
    devices = range(lax.axis_size(axis))
    route = [((i - distance) % len(devices), i) for i in devices]
    return lax.ppermute(block, axis, route)


def wide_rim(values):
    return with_halo(values, (("space", 2),), 2)


def narrow_rim(values):
    return with_halo(values, (("space", 2),), 1)


def gather_channels(values):
    return lax.all_gather(values, "chan", axis=0, tiled=True)


def spread_channels(values):
    return gather_channels(narrow_rim(values))


def reduce_channels(values):
    return lax.psum_scatter(values, "chan", scatter_dimension=0, tiled=True)


def chan_slice(values, axis_number):
    portion = values.shape[axis_number] // lax.axis_size("chan")
    return lax.dynamic_slice_in_dim(values, lax.axis_index("chan") * portion, portion, axis_number)


def conv_forward(padded_in, weight):
    height = padded_in.shape[2] - 2
    summed = None
    for row_tap in range(3):
        window = padded_in[:, :, row_tap : row_tap + height, :]
        for col_tap in range(3):
            shifted = jnp.roll(window, 1 - col_tap, axis=3)
            product = jnp.einsum(
                "co,cbrx->obrx",
                weight[row_tap, col_tap],
                shifted,
                preferred_element_type=jnp.float32,
            )
            summed = product if summed is None else summed + product
    return summed


def conv_backward(padded_in, weight, grad_low):
    height = grad_low.shape[2]
    grad_pad = narrow_rim(grad_low)
    weight_taps = []
    input_grad = None
    for row_tap in range(3):
        window_in = padded_in[:, :, row_tap : row_tap + height, :]
        window_out = grad_pad[:, :, 2 - row_tap : 2 - row_tap + height, :]
        tap_row = []
        for col_tap in range(3):
            shifted_in = jnp.roll(window_in, 1 - col_tap, axis=3)
            tap_row.append(
                jnp.einsum(
                    "cbrx,obrx->co", shifted_in, grad_low, preferred_element_type=jnp.float32
                )
            )
            shifted_out = jnp.roll(window_out, col_tap - 1, axis=3)
            product = jnp.einsum(
                "co,obrx->cbrx",
                weight[row_tap, col_tap],
                shifted_out,
                preferred_element_type=jnp.float32,
            )
            input_grad = product if input_grad is None else input_grad + product
        weight_taps.append(jnp.stack(tap_row))
    bias_grad = jnp.sum(grad_low, axis=(1, 2, 3), dtype=jnp.float32)
    return (input_grad, jnp.stack(weight_taps), bias_grad)


def gelu_back(preact, upstream):
    return jax.vjp(jax.nn.gelu, preact)[1](upstream)[0].astype(jnp.bfloat16)


def cnn_forward(first_pad, weights, spread):
    w_first, b_first, w_mid, b_mid, w_last, b_last = weights
    preact = conv_forward(first_pad, w_first) + b_first[:, None, None, None]
    stored = [(first_pad, preact)]
    for depth_index in range(w_mid.shape[0]):
        padded_in = spread(jax.nn.gelu(preact).astype(jnp.bfloat16))
        preact = (
            conv_forward(padded_in, w_mid[depth_index]) + b_mid[depth_index][:, None, None, None]
        )
        stored.append((padded_in, preact))
    padded_in = spread(jax.nn.gelu(preact).astype(jnp.bfloat16))
    stencil = conv_forward(padded_in, w_last) + b_last[:, None, None, None]
    stored.append((padded_in, stencil))
    return (stored, stencil)


def cnn_backward(stored, weights, stencil_low, collect):
    w_first, b_first, w_mid, b_mid, w_last, b_last = weights
    input_grad, last_w_grad, last_b_grad = conv_backward(stored[-1][0], w_last, stencil_low)
    mid_w_grads = []
    mid_b_grads = []
    for depth_index in range(w_mid.shape[0], 0, -1):
        upstream = gelu_back(stored[depth_index][1], collect(input_grad))
        input_grad, tap_grad, bias_grad = conv_backward(
            stored[depth_index][0], w_mid[depth_index - 1], upstream
        )
        mid_w_grads.insert(0, tap_grad)
        mid_b_grads.insert(0, bias_grad)
    upstream = gelu_back(stored[0][1], collect(input_grad))
    first_grad, first_w_grad, first_b_grad = conv_backward(stored[0][0], w_first, upstream)
    return (
        (
            first_w_grad,
            first_b_grad,
            jnp.stack(mid_w_grads),
            jnp.stack(mid_b_grads),
            last_w_grad,
            last_b_grad,
        ),
        first_grad,
    )


def face_values(padded_vel, stencil, offsets):
    points = offsets.shape[1]
    height = stencil.shape[2]
    onehot = (offsets[:, :, None] == jnp.arange(points, dtype=jnp.int32)[None, None, :]).astype(
        jnp.float32
    )
    second = jnp.array([[6], [9]], dtype=jnp.int32)
    base_weight = 0.5 * (
        (offsets == 5).astype(jnp.float32) + (offsets == second).astype(jnp.float32)
    )
    grouped = stencil.reshape((2, points) + stencil.shape[1:])
    stencil_mix = (
        grouped - jnp.mean(grouped, axis=1, keepdims=True) + base_weight[:, :, None, None, None]
    )
    by_point = jnp.einsum("ckp,ckbrx->cpbrx", onehot, stencil_mix, precision=highest)
    components = []
    for component in range(2):
        summed = None
        for stencil_point in range(points):
            row_shift = stencil_point // 4 - 1
            col_shift = stencil_point % 4 - 1
            rows_taken = padded_vel[component, :, 2 + row_shift : 2 + row_shift + height, :]
            shifted = jnp.roll(rows_taken, -col_shift, axis=2)
            product = by_point[component, stencil_point] * shifted
            summed = product if summed is None else summed + product
        components.append(summed)
    return jnp.stack(components)


def solver_local(padded_vel, face_vals, vn_prev):
    height = face_vals.shape[2]
    center = padded_vel[:, :, 2 : height + 2]
    north_row = padded_vel[:, :, 3 : height + 3]
    south_row = padded_vel[:, :, 1 : height + 1]
    east_col = jnp.roll(center, -1, axis=3)
    west_col = jnp.roll(center, 1, axis=3)
    laplace = east_col + west_col + north_row + south_row - 4.0 * center
    flux_east = face_vals[0][None] * (center + east_col) * 0.5
    flux_north = face_vals[1][None] * (center + north_row) * 0.5
    below_flux = vn_prev[None, :, None, :] * (padded_vel[:, :, 1:2] + padded_vel[:, :, 2:3]) * 0.5
    flux_south = jnp.concatenate([below_flux, flux_north[:, :, : height - 1]], axis=2)
    advect = flux_east - jnp.roll(flux_east, 1, axis=3) + flux_north - flux_south
    return center + time_step * (viscosity * laplace - advect)


def dft_tables(length):
    positions = jnp.arange(length, dtype=jnp.int32)
    angles = jnp.mod(positions[:, None] * positions[None, :], length).astype(jnp.float32) * (
        2.0 * jnp.pi / length
    )
    return (jnp.cos(angles), jnp.sin(angles))


def wavenumber(positions, length):
    signed = jnp.where(positions >= length // 2, positions - length, positions).astype(jnp.float32)
    return signed * (2.0 * jnp.pi / length)


def along_y(table, values):
    return jnp.einsum("zy,kbyc->kbzc", table, values, precision=highest)


def project(field_vals):
    extent = field_vals.shape[3]
    cos_x, sin_x = dft_tables(extent)
    real_part = jnp.einsum("kbrx,xm->kbrm", field_vals, cos_x, precision=highest)
    imag_part = -jnp.einsum("kbrx,xm->kbrm", field_vals, sin_x, precision=highest)
    column_block = lax.all_to_all(
        jnp.stack([real_part, imag_part]), "space", split_axis=4, concat_axis=3, tiled=True
    )
    length = column_block.shape[3]
    width_cols = column_block.shape[4]
    cos_y, sin_y = dft_tables(length)
    column_ids = lax.axis_index("space") * width_cols + jnp.arange(width_cols, dtype=jnp.int32)
    wave_x = wavenumber(column_ids, extent)[None, :]
    wave_y = wavenumber(jnp.arange(length, dtype=jnp.int32), length)[:, None]
    wave_sq = wave_x * wave_x + wave_y * wave_y
    reciprocal = jnp.where(wave_sq > 0, 1.0 / jnp.where(wave_sq > 0, wave_sq, 1.0), 0.0)

    def remove(spectral):
        divergence = (wave_x * spectral[0] + wave_y * spectral[1]) * reciprocal
        return jnp.stack([spectral[0] - wave_x * divergence, spectral[1] - wave_y * divergence])

    forward_re = along_y(cos_y, column_block[0]) + along_y(sin_y, column_block[1])
    forward_im = along_y(cos_y, column_block[1]) - along_y(sin_y, column_block[0])
    forward_re = remove(forward_re)
    forward_im = remove(forward_im)
    inverse_re = (along_y(cos_y, forward_re) - along_y(sin_y, forward_im)) / length
    inverse_im = (along_y(cos_y, forward_im) + along_y(sin_y, forward_re)) / length
    mixed = lax.all_to_all(
        jnp.stack([inverse_re, inverse_im]), "space", split_axis=3, concat_axis=4, tiled=True
    )
    real_back = jnp.einsum("kbrm,mx->kbrx", mixed[0], cos_x, precision=highest)
    imag_back = jnp.einsum("kbrm,mx->kbrx", mixed[1], sin_x, precision=highest)
    return (real_back - imag_back) / extent


def per_device(velocity, w_first, b_first, w_mid, b_mid, w_last, b_last, offsets, cotangent):
    height = velocity.shape[2]
    extent = velocity.shape[3]
    cell_count = 2 * velocity.shape[1] * height * extent * lax.axis_size("space")
    padded = wide_rim(velocity)

    def faces_of(pad_arg, stencil_arg):
        return face_values(pad_arg, stencil_arg, offsets)

    weights = (w_first, b_first, w_mid, b_mid, w_last, b_last)
    stored, local_stencil = cnn_forward(
        padded[:, :, 1 : height + 3].astype(jnp.bfloat16), weights, spread_channels
    )
    stencil = lax.all_gather(local_stencil, "chan", axis=0, tiled=True)
    face_vals, face_pull = jax.vjp(faces_of, padded, stencil)
    vn_prev = shifted_2(face_vals[1][:, height - 1, :], "space", 1)
    provisional, solver_pull = jax.vjp(solver_local, padded, face_vals, vn_prev)
    new_velocity = project(provisional)
    update = provisional - velocity
    squares = jnp.stack(
        [
            jnp.sum(velocity * velocity),
            jnp.sum(face_vals * face_vals),
            jnp.sum(update * update),
            jnp.sum(new_velocity * new_velocity),
        ]
    )
    padded_grad, faces_grad, prev_grad = solver_pull(project(cotangent))
    from_next = shifted_2(prev_grad, "space", -1)
    faces_grad = faces_grad.at[1, :, height - 1, :].add(from_next)
    stencil_pad_grad, stencil_grad = face_pull(faces_grad)
    own_grad = chan_slice(padded_grad + stencil_pad_grad, 1)
    gradients, partial_first = cnn_backward(
        stored, weights, chan_slice(stencil_grad, 0).astype(jnp.bfloat16), reduce_channels
    )
    first_grad = lax.psum_scatter(partial_first, "chan", scatter_dimension=1, tiled=True)
    summed = lax.psum(
        (
            gradients[0],
            gradients[1],
            gradients[2],
            gradients[3],
            gradients[4],
            gradients[5],
            squares,
        ),
        "space",
    )
    weight_grads = (summed[0], summed[1], summed[2], summed[3], summed[4], summed[5])
    rim_rows = jnp.concatenate(
        [own_grad[:, :, 0:2], own_grad[:, :, height + 2 : height + 4]], axis=2
    )
    beside_all = wide_rim(rim_rows)
    interior = own_grad[:, :, 2 : height + 2] + first_grad
    interior = interior.at[:, :, 0:2].add(beside_all[:, :, 0:2])
    interior = interior.at[:, :, height - 2 : height].add(beside_all[:, :, 6:8])
    rms_stats = jnp.sqrt(summed[6] / cell_count)
    return (
        new_velocity,
        interior,
        weight_grads[0],
        weight_grads[1],
        weight_grads[2],
        weight_grads[3],
        weight_grads[4],
        weight_grads[5],
        rms_stats,
    )


def solution(mesh):
    return jax.shard_map(
        per_device,
        mesh=mesh,
        in_specs=(
            P(None, None, "space", None),
            P(None, None, None, "chan"),
            P("chan"),
            P(None, None, None, None, "chan"),
            P(None, "chan"),
            P(None, None, None, "chan"),
            P("chan"),
            P(),
            P(None, None, "space", None),
        ),
        out_specs=(
            P(None, None, "space", None),
            P(None, "chan", "space", None),
            P(None, None, None, "chan"),
            P("chan"),
            P(None, None, None, None, "chan"),
            P(None, "chan"),
            P(None, None, None, "chan"),
            P("chan"),
            P(),
        ),
        check_vma=False,
    )
```

profile of v0, /device:TPU:0, one launch (start us, length us, event | category | flops | bytes accessed | tf_op | source)
XLA Modules:
  0.0 1795.7 jit_solution(17300739114544885889)
XLA Ops:
  38.5 36.3 %all-gather.8.cloned.1.call-done = bf16[64,4,34,256]{3,0,2,1:T(8,128)(2,1)} async-done(((bf16[16,4,34,256]{3,0,2,1:T(8,128)(2,1)}), bf16[64,4,34,256]{3,0,2,1:T(8,128)(2,1)}) %all-gather.8.cloned.1.call-update) | async-done | bytes 4456464 | tf_op jit(solution)/shard_map/all_gather | solution.py:39
  83.5 19.3 %fusion.996 = (bf16[64,4,32,255]{3,0,2,1:T(8,128)(2,1)}, bf16[64,4,32,255]{3,0,2,1:T(8,128)(2,1)}, bf16[64,4,32,255]{3,0,2,1:T(8,128)(2,1)}, bf16[64,4,32,255]{3...) fusion(bf16[64,4,34,256]{3,0,2,1:T(8,128)(2,1)} %all-gather.8.cloned.1.call-done), kind=kLoop, calls=%fused_computation.1596 | loop fusion | bytes 50135040 | tf_op jit(solution)/shard_map/jit(_roll_static)/slice | solution.py:61
  132.7 36.6 %all-gather.10.cloned.1.call-done = bf16[64,4,34,256]{3,0,2,1:T(8,128)(2,1)} async-done(((bf16[16,4,34,256]{3,0,2,1:T(8,128)(2,1)}), bf16[64,4,34,256]{3,0,2,1:T(8,128)(2,1)}) %all-gather.10.cloned.1.call-update) | async-done | bytes 4456464 | tf_op jit(solution)/shard_map/all_gather | solution.py:39
  169.2 19.9 %fusion.995 = (bf16[64,4,32,1]{3,0,2,1:T(8,128)(2,1)S(1)}, bf16[64,4,32,1]{3,0,2,1:T(8,128)(2,1)}, bf16[64,4,32,1]{3,0,2,1:T(8,128)(2,1)}, bf16[64,4,32,1]{3,0,2...) fusion(bf16[64,4,34,256]{3,0,2,1:T(8,128)(2,1)} %all-gather.10.cloned.1.call-done), kind=kLoop, calls=%fused_computation.1595 | loop fusion | bytes 196608 | tf_op jit(solution)/shard_map/jit(_roll_static)/slice | solution.py:61
  189.1 19.0 %fusion.994 = (bf16[64,4,32,255]{3,0,2,1:T(8,128)(2,1)}, bf16[64,4,32,255]{3,0,2,1:T(8,128)(2,1)}, bf16[64,4,32,255]{3,0,2,1:T(8,128)(2,1)}, bf16[64,4,32,255]{3...) fusion(bf16[64,4,34,256]{3,0,2,1:T(8,128)(2,1)} %all-gather.10.cloned.1.call-done), kind=kLoop, calls=%fused_computation.1594 | loop fusion | bytes 50135040 | tf_op jit(solution)/shard_map/jit(_roll_static)/slice | solution.py:61
  237.9 36.6 %all-gather.12.cloned.1.call-done = bf16[64,4,34,256]{3,0,2,1:T(8,128)(2,1)} async-done(((bf16[16,4,34,256]{3,0,2,1:T(8,128)(2,1)}), bf16[64,4,34,256]{3,0,2,1:T(8,128)(2,1)}) %all-gather.12.cloned.1.call-update) | async-done | bytes 4456464 | tf_op jit(solution)/shard_map/all_gather | solution.py:39
  283.3 19.0 %fusion.992 = (bf16[64,4,32,255]{3,0,2,1:T(8,128)(2,1)}, bf16[64,4,32,255]{3,0,2,1:T(8,128)(2,1)}, bf16[64,4,32,255]{3,0,2,1:T(8,128)(2,1)}, bf16[64,4,32,255]{3...) fusion(bf16[64,4,34,256]{3,0,2,1:T(8,128)(2,1)} %all-gather.12.cloned.1.call-done), kind=kLoop, calls=%fused_computation.1592 | loop fusion | bytes 50135040 | tf_op jit(solution)/shard_map/jit(_roll_static)/slice | solution.py:61
  332.2 36.6 %all-gather.14.cloned.1.call-done = bf16[64,4,34,256]{3,0,2,1:T(8,128)(2,1)} async-done(((bf16[16,4,34,256]{3,0,2,1:T(8,128)(2,1)}), bf16[64,4,34,256]{3,0,2,1:T(8,128)(2,1)}) %all-gather.14.cloned.1.call-update) | async-done | bytes 4456464 | tf_op jit(solution)/shard_map/all_gather | solution.py:39
  377.2 19.0 %fusion.990 = (bf16[64,4,32,255]{3,0,2,1:T(8,128)(2,1)}, bf16[64,4,32,255]{3,0,2,1:T(8,128)(2,1)}, bf16[64,4,32,255]{3,0,2,1:T(8,128)(2,1)}, bf16[64,4,32,255]{3...) fusion(bf16[64,4,34,256]{3,0,2,1:T(8,128)(2,1)} %all-gather.14.cloned.1.call-done), kind=kLoop, calls=%fused_computation.1590 | loop fusion | bytes 50135040 | tf_op jit(solution)/shard_map/jit(_roll_static)/slice | solution.py:61
  426.1 36.6 %all-gather.16.cloned.1.call-done = bf16[64,4,34,256]{3,0,2,1:T(8,128)(2,1)} async-done(((bf16[16,4,34,256]{3,0,2,1:T(8,128)(2,1)}), bf16[64,4,34,256]{3,0,2,1:T(8,128)(2,1)}) %all-gather.16.cloned.1.call-update) | async-done | bytes 4456464 | tf_op jit(solution)/shard_map/all_gather | solution.py:39
  471.6 19.0 %fusion.988 = (bf16[64,4,32,255]{3,0,2,1:T(8,128)(2,1)}, bf16[64,4,32,255]{3,0,2,1:T(8,128)(2,1)}, bf16[64,4,32,255]{3,0,2,1:T(8,128)(2,1)}, bf16[64,4,32,255]{3...) fusion(bf16[64,4,34,256]{3,0,2,1:T(8,128)(2,1)} %all-gather.16.cloned.1.call-done), kind=kLoop, calls=%fused_computation.1588 | loop fusion | bytes 50135040 | tf_op jit(solution)/shard_map/jit(_roll_static)/slice | solution.py:61
  565.7 19.2 %fusion.987 = (bf16[64,4,32,255]{3,0,2,1:T(8,128)(2,1)}, bf16[64,4,32,255]{3,0,2,1:T(8,128)(2,1)}, bf16[64,4,32,255]{3,0,2,1:T(8,128)(2,1)}, bf16[64,4,32,255]{3...) fusion(bf16[64,4,34,256]{3,0,2,1:T(8,128)(2,1)} %all-gather.18.cloned.1.call-done), kind=kLoop, calls=%fused_computation.1587 | loop fusion | bytes 50135040 | tf_op jit(solution)/shard_map/jit(_roll_static)/slice | solution.py:61
  783.8 25.8 %add_bitcast_fusion.5 = f32[64,4,32,256]{3,0,2,1:T(8,128)} fusion(f32[4,32,256,64]{2,3,1,0:T(8,128)} %fusion.453, f32[4,32,256,64]{2,3,1,0:T(8,128)} %fusion.449, f32[4,32,256,64]{2,3,1,0:T(8,128)} %fusion.445, f32[4,32,256,64]{2,3,1,0:T(8,128)} %fusion.679, f32[4,32,256,64]{2,3,1,0:T(8,128)} %fusion.441, f32[4,32,256,64]{2,3,1,0:T(8,128)} %fusion.437, ...), kind=kOutput, calls=%fused_computation.5 | convolution fusion | flops 51412992 | bytes 76040192 | tf_op jit(solution)/shard_map/co,obrx->cbrx/dot_general | solution.py:89
  809.7 70.5 %reduce-scatter.8.cloned.1.call-done = f32[16,4,32,256]{3,0,2,1:T(8,128)} async-done(((f32[64,4,32,256]{3,0,2,1:T(8,128)}), f32[16,4,32,256]{3,0,2,1:T(8,128)}) %reduce-scatter.8.cloned.1.call-update) | async-done | bytes 2097168 | tf_op jit(solution)/shard_map/reduce_scatter | solution.py:47
  929.1 25.8 %add_bitcast_fusion.4 = f32[64,4,32,256]{3,0,2,1:T(8,128)} fusion(f32[4,32,256,64]{2,3,1,0:T(8,128)} %fusion.269, f32[4,32,256,64]{2,3,1,0:T(8,128)} %fusion.265, f32[4,32,256,64]{2,3,1,0:T(8,128)} %fusion.261, f32[4,32,256,64]{2,3,1,0:T(8,128)} %fusion.669, f32[4,32,256,64]{2,3,1,0:T(8,128)} %fusion.257, f32[4,32,256,64]{2,3,1,0:T(8,128)} %fusion.253, ...), kind=kOutput, calls=%fused_computation.4 | convolution fusion | flops 86048768 | bytes 76582912 | tf_op jit(solution)/shard_map/co,obrx->cbrx/dot_general | solution.py:89
  955.2 70.1 %reduce-scatter.10.cloned.1.call-done = f32[16,4,32,256]{3,0,2,1:T(8,128)} async-done(((f32[64,4,32,256]{3,0,2,1:T(8,128)}), f32[16,4,32,256]{3,0,2,1:T(8,128)}) %reduce-scatter.10.cloned.1.call-update) | async-done | bytes 2097168 | tf_op jit(solution)/shard_map/reduce_scatter | solution.py:47
  1073.9 25.8 %add_bitcast_fusion.3 = f32[64,4,32,256]{3,0,2,1:T(8,128)} fusion(f32[4,32,256,64]{2,3,1,0:T(8,128)} %fusion.293, f32[4,32,256,64]{2,3,1,0:T(8,128)} %fusion.289, f32[4,32,256,64]{2,3,1,0:T(8,128)} %fusion.285, f32[4,32,256,64]{2,3,1,0:T(8,128)} %fusion.668, f32[4,32,256,64]{2,3,1,0:T(8,128)} %fusion.281, f32[4,32,256,64]{2,3,1,0:T(8,128)} %fusion.277, ...), kind=kOutput, calls=%fused_computation.3 | convolution fusion | flops 86048768 | bytes 76582912 | tf_op jit(solution)/shard_map/co,obrx->cbrx/dot_general | solution.py:89
  1100.2 69.9 %reduce-scatter.12.cloned.1.call-done = f32[16,4,32,256]{3,0,2,1:T(8,128)} async-done(((f32[64,4,32,256]{3,0,2,1:T(8,128)}), f32[16,4,32,256]{3,0,2,1:T(8,128)}) %reduce-scatter.12.cloned.1.call-update) | async-done | bytes 2097168 | tf_op jit(solution)/shard_map/reduce_scatter | solution.py:47
  1218.7 25.8 %add_bitcast_fusion.2 = f32[64,4,32,256]{3,0,2,1:T(8,128)} fusion(f32[4,32,256,64]{2,3,1,0:T(8,128)} %fusion.317, f32[4,32,256,64]{2,3,1,0:T(8,128)} %fusion.313, f32[4,32,256,64]{2,3,1,0:T(8,128)} %fusion.309, f32[4,32,256,64]{2,3,1,0:T(8,128)} %fusion.667, f32[4,32,256,64]{2,3,1,0:T(8,128)} %fusion.305, f32[4,32,256,64]{2,3,1,0:T(8,128)} %fusion.301, ...), kind=kOutput, calls=%fused_computation.2 | convolution fusion | flops 86048768 | bytes 76582912 | tf_op jit(solution)/shard_map/co,obrx->cbrx/dot_general | solution.py:89
  1244.8 70.1 %reduce-scatter.14.cloned.1.call-done = f32[16,4,32,256]{3,0,2,1:T(8,128)} async-done(((f32[64,4,32,256]{3,0,2,1:T(8,128)}), f32[16,4,32,256]{3,0,2,1:T(8,128)}) %reduce-scatter.14.cloned.1.call-update) | async-done | bytes 2097168 | tf_op jit(solution)/shard_map/reduce_scatter | solution.py:47
  1363.5 26.2 %add_bitcast_fusion.1 = f32[64,4,32,256]{3,0,2,1:T(8,128)} fusion(f32[4,32,256,64]{2,3,1,0:T(8,128)} %fusion.341, f32[4,32,256,64]{2,3,1,0:T(8,128)} %fusion.337, f32[4,32,256,64]{2,3,1,0:T(8,128)} %fusion.333, f32[4,32,256,64]{2,3,1,0:T(8,128)} %fusion.666, f32[4,32,256,64]{2,3,1,0:T(8,128)} %fusion.329, f32[4,32,256,64]{2,3,1,0:T(8,128)} %fusion.325, ...), kind=kOutput, calls=%fused_computation.1 | convolution fusion | flops 86048768 | bytes 76582912 | tf_op jit(solution)/shard_map/co,obrx->cbrx/dot_general | solution.py:89
  1549.7 25.8 %add_bitcast_fusion = f32[64,4,32,256]{3,0,2,1:T(8,128)} fusion(f32[4,32,256,64]{2,3,1,0:T(8,128)} %fusion.365, f32[4,32,256,64]{2,3,1,0:T(8,128)} %fusion.361, f32[4,32,256,64]{2,3,1,0:T(8,128)} %fusion.357, f32[4,32,256,64]{2,3,1,0:T(8,128)} %fusion.665, f32[4,32,256,64]{2,3,1,0:T(8,128)} %fusion.353, f32[4,32,256,64]{2,3,1,0:T(8,128)} %fusion.349, ...), kind=kOutput, calls=%fused_computation | convolution fusion | flops 86048768 | bytes 76582912 | tf_op jit(solution)/shard_map/co,obrx->cbrx/dot_general | solution.py:89
  1701.6 34.0 %all-reduce.126 = (f32[3,3,2,16]{3,2,1,0:T(2,128)}, f32[16]{0:T(128)}, f32[5,16]{1,0:T(8,128)}, f32[3,3,64,8]{2,3,1,0:T(8,128)}, f32[8]{0:T(128)}, /*index=5*/f32[4]{0:T(128)S(1)}) all-reduce(f32[3,3,2,16]{3,2,1,0:T(2,128)S(1)} %pad_maximum_fusion.256, f32[16]{0:T(128)S(1)} %get-tuple-element.113, ...), channel_id=1, replica_groups=mesh['chan'=4,'space'=8] {'space'}, use_global_device_ids=true, to_apply=%region_12.13 | all-reduce | flops 5004 | bytes 40032 | tf_op jit(solution)/shard_map/psum | solution.py:281
  1739.1 47.9 %all-reduce.129.cloned.1.call-done = f32[5,3,3,64,16]{3,4,2,1,0:T(8,128)} async-done(((f32[5,3,3,64,16]{3,4,2,1,0:T(8,128)}), f32[5,3,3,64,16]{3,4,2,1,0:T(8,128)}) %all-reduce.129.cloned.1.call-update) | async-done | bytes 184336 | tf_op jit(solution)/shard_map/psum | solution.py:281
  (1529 shorter events, 940.3 us)
Async XLA Ops:
  7.2 67.6 %all-gather.8.cloned.1.call-start = ((), (), s32[]{:S(2)}) async-start(), calls=%async_computation.11 | async-start | bytes 5570560 | tf_op jit(solution)/shard_map/all_gather | solution.py:39
  9.1 9.0 collective-permute-start.1
  37.1 132.1 %all-gather.10.cloned.1.call-start = ((), (), s32[]{:S(2)}) async-start(), calls=%async_computation.12 | async-start | bytes 5570560 | tf_op jit(solution)/shard_map/all_gather | solution.py:39
  132.6 141.9 %all-gather.12.cloned.1.call-start = ((), (), s32[]{:S(2)}) async-start(), calls=%async_computation.13 | async-start | bytes 5570560 | tf_op jit(solution)/shard_map/all_gather | solution.py:39
  237.9 130.8 %all-gather.14.cloned.1.call-start = ((), (), s32[]{:S(2)}) async-start(), calls=%async_computation.14 | async-start | bytes 5570560 | tf_op jit(solution)/shard_map/all_gather | solution.py:39
  332.1 130.5 %all-gather.16.cloned.1.call-start = ((), (), s32[]{:S(2)}) async-start(), calls=%async_computation.15 | async-start | bytes 5570560 | tf_op jit(solution)/shard_map/all_gather | solution.py:39
  426.1 131.0 %all-gather.18.cloned.1.call-start = ((), (), s32[]{:S(2)}) async-start(), calls=%async_computation.16 | async-start | bytes 5570560 | tf_op jit(solution)/shard_map/all_gather | solution.py:39
  526.7 107.2 %all-to-all-start.2 = ((f32[8,1,16384]{2,1,0:T(1,128)}), f32[8,1,16384]{2,1,0:T(1,128)}, u32[]{:S(2)}, u32[]{:S(2)}) async-start(f32[8,1,16384]{2,1,0:T(1,128)} %reshape.2325), calls=%async_computation.2 | async-start | bytes 1048576 | tf_op jit(solution)/shard_map/all_to_all | solution.py:215
  532.8 159.0 %all-gather.20.cloned.1.call-start = ((), (), s32[]{:S(2)}) async-start(), calls=%async_computation.17 | async-start | bytes 5242880 | tf_op jit(solution)/shard_map/all_gather | solution.py:258
  662.2 20.4 %all-to-all-start.3 = ((f32[8,1,16384]{2,1,0:T(1,128)}), f32[8,1,16384]{2,1,0:T(1,128)S(1)}, u32[]{:S(2)}, u32[]{:S(2)}) async-start(f32[8,1,16384]{2,1,0:T(1,128)} %reshape.2327), calls=%async_computation.3 | async-start | bytes 1048576 | tf_op jit(solution)/shard_map/all_to_all | solution.py:237
  667.7 212.5 %reduce-scatter.8.cloned.1.call-start = ((), (), s32[]{:S(2)}) async-start(), calls=%async_computation.18 | async-start | bytes 10485760 | tf_op jit(solution)/shard_map/reduce_scatter | solution.py:47
  707.8 12.1 collective-permute-start.14
  809.7 215.7 %reduce-scatter.10.cloned.1.call-start = ((), (), s32[]{:S(2)}) async-start(), calls=%async_computation.19 | async-start | bytes 10485760 | tf_op jit(solution)/shard_map/reduce_scatter | solution.py:47
  883.9 9.3 collective-permute-start.18
  955.0 215.1 %reduce-scatter.12.cloned.1.call-start = ((), (), s32[]{:S(2)}) async-start(), calls=%async_computation.20 | async-start | bytes 10485760 | tf_op jit(solution)/shard_map/reduce_scatter | solution.py:47
  1099.8 215.1 %reduce-scatter.14.cloned.1.call-start = ((), (), s32[]{:S(2)}) async-start(), calls=%async_computation.21 | async-start | bytes 10485760 | tf_op jit(solution)/shard_map/reduce_scatter | solution.py:47
  1244.5 257.8 %reduce-scatter.16.cloned.1.call-start = ((), (), s32[]{:S(2)}) async-start(), calls=%async_computation.22 | async-start | bytes 10485760 | tf_op jit(solution)/shard_map/reduce_scatter | solution.py:47
  1403.4 35.0 %all-to-all-start = ((f32[8,1,16384]{2,1,0:T(1,128)}), f32[8,1,16384]{2,1,0:T(1,128)S(1)}, u32[]{:S(2)}, u32[]{:S(2)}) async-start(f32[8,1,16384]{2,1,0:T(1,128)} %reshape.2321), calls=%async_computation | async-start | bytes 1048576 | tf_op jit(solution)/shard_map/all_to_all | solution.py:215
  1419.3 318.4 %collective-permute-start.31 = (f32[2,1,2,256]{3,1,2,0:T(1,128)}, f32[2,1,2,256]{3,1,2,0:T(1,128)}, u32[]{:S(2)}, u32[]{:S(2)}) collective-permute-start(f32[2,1,2,256]{3,1,2,0:T(1,128)} %get-tuple-element.589), channel_id=1, source_target_pairs={{1,0},{2,1},{3,2},{4,3},{5,4},{6,5},{7,6},{0,7},{9,8},{10,9},{11,1... | collective-permute-start | bytes 12296 | tf_op jit(solution)/shard_map/ppermute | solution.py:19
  1424.0 313.0 %collective-permute-start.30 = (f32[2,1,2,256]{3,1,2,0:T(1,128)}, f32[2,1,2,256]{3,1,2,0:T(1,128)}, u32[]{:S(2)}, u32[]{:S(2)}) collective-permute-start(f32[2,1,2,256]{3,1,2,0:T(1,128)} %get-tuple-element.590), channel_id=1, source_target_pairs={{0,1},{1,2},{2,3},{3,4},{4,5},{5,6},{6,7},{7,0},{8,9},{9,10},{10,1... | collective-permute-start | bytes 12296 | tf_op jit(solution)/shard_map/ppermute | solution.py:18
  1459.4 19.0 %all-to-all-start.1 = ((f32[8,1,16384]{2,1,0:T(1,128)}), f32[8,1,16384]{2,1,0:T(1,128)S(1)}, u32[]{:S(2)}, u32[]{:S(2)}) async-start(f32[8,1,16384]{2,1,0:T(1,128)} %reshape.2323), calls=%async_computation.1 | async-start | bytes 1048576 | tf_op jit(solution)/shard_map/all_to_all | solution.py:237
  1465.3 210.2 %reduce-scatter.18.cloned.1.call-start = ((), (), s32[]{:S(2)}) async-start(), calls=%async_computation.23 | async-start | bytes 10485760 | tf_op jit(solution)/shard_map/reduce_scatter | solution.py:47
  1575.5 160.6 %reduce-scatter.20.cloned.1.call-start = ((), (), s32[]{:S(2)}) async-start(), calls=%async_computation.24 | async-start | bytes 327680 | tf_op jit(solution)/shard_map/reduce_scatter | solution.py:280
  1695.0 92.0 %all-reduce.129.cloned.1.call-start = ((), (), s32[]{:S(2)}) async-start(), calls=%async_computation.25 | async-start | bytes 737280 | tf_op jit(solution)/shard_map/psum | solution.py:281
  (466 other events, 5073.9 us)
Sparse Core Ops, SparseCore 0:
  37.2 37.5 all-gather.7
  132.8 36.4 all-gather.9
  238.0 36.4 all-gather.11
  332.2 36.4 all-gather.13
  426.2 36.4 all-gather.15
  520.4 36.5 all-gather.17
  606.0 34.4 all-gather.19
  809.8 70.3 reduce-scatter.7
  955.1 70.2 reduce-scatter.9
  1099.9 70.1 reduce-scatter.11
  1244.6 70.2 reduce-scatter.13
  1389.9 70.1 reduce-scatter.15
  1575.7 70.3 reduce-scatter.17
  1695.1 16.4 reduce-scatter.19
  1715.8 71.1 all-reduce.128
where the time goes:
time: 1800 us
  matrix products  630 us (35%)
  waiting for transfers between devices  567 us (32%)
  local copies, waits for them, and re-layouts  343 us (19%)
  other arithmetic  109 us (6%)
  starting transfers between devices  92.8 us (5%)
  blocking collectives  34 us (2%)
  between operations  20.6 us (1%)
    dot_general x63, matrix products, conv_backward(): jnp.einsum('co,obrx->cbrx', weight[row_tap, col_tap], shifted_out, prefer...  379 us
    reduce_scatter x6, waiting for transfers between devices, reduce_channels(): return lax.psum_scatter(values, 'chan', scatter_dimension=0, tiled=True)  281 us
    all_gather x6, waiting for transfers between devices, gather_channels(): return lax.all_gather(values, 'chan', axis=0, tiled=True)  194 us
    slice x12, local copies, waits for them, and re-layouts, conv_forward(): shifted = jnp.roll(window, 1 - col_tap, axis=3)  178 us
    dot_general x63, matrix products, conv_forward(): jnp.einsum('co,cbrx->obrx', weight[row_tap, col_tap], shifted, preferred_...  106 us
    dot_general x63, matrix products, conv_backward(): jnp.einsum('cbrx,obrx->co', shifted_in, grad_low, preferred_element_type=...  99.2 us
    unnamed x892, local copies, waits for them, and re-layouts  87.2 us
    ppermute x15, starting transfers between devices, with_halo(): after = lax.ppermute(initial, axis, down)  52.9 us
  transfers between devices with their start and end apart: 51, of which 27 were waited for; matrix products, arithmetic and copies ran while one was open for 23% of the time, Pallas kernels for 0%

commit v1 on v0

v1 whole, which is shorter than its diff:
```python
import functools

import jax
import jax.numpy as jnp
import numpy as np
from jax import lax
from jax.experimental import pallas as pl
from jax.experimental.pallas import tpu as pltpu
from jax.sharding import PartitionSpec as P

f32 = jnp.float32
bf16 = jnp.bfloat16
highest = lax.Precision.HIGHEST
time_step = 0.2
viscosity = 0.256
HALO = 16
DEEP = 12
GPH = 8
C = 64
NL = 5
KW = 256
MIDROWS = NL * 3 * 16
A0 = 0.7978845608028654
A1 = 0.044715 * A0


def basis(length):
    half = length // 2
    pos = np.arange(length)[:, None]
    table = np.zeros((length, length))
    m = np.arange(half + 1)[None, :]
    table[:, : half + 1] = np.cos(2 * np.pi * ((pos * m) % length) / length) * np.sqrt(2.0 / length)
    table[:, 0] = np.sqrt(1.0 / length)
    table[:, half] = np.cos(np.pi * pos[:, 0]) * np.sqrt(1.0 / length)
    m = np.arange(1, half)[None, :]
    table[:, half + 1 :] = np.sin(2 * np.pi * ((pos * m) % length) / length) * np.sqrt(2.0 / length)
    return table


def multipliers(ny, nx):
    def modes(n):
        half = n // 2
        index = np.arange(n)
        wave = np.where(index <= half, index, index - half) * (2 * np.pi / n)
        return wave, index <= half

    ky, cy = modes(ny)
    kx, cx = modes(nx)
    ky, cy = ky[:, None], cy[:, None]
    kx, cx = kx[None, :], cx[None, :]
    sq = kx * kx + ky * ky
    inv = np.where(sq > 0, 1.0 / np.where(sq > 0, sq, 1.0), 0.0)
    sign = np.where(cx == cy, 1.0, -1.0)
    edge_x = (kx == 0) | (kx >= np.pi - 1e-9)
    edge_y = (ky == 0) | (ky >= np.pi - 1e-9)
    mxy = np.where(edge_x | edge_y, 0.0, sign * kx * ky * inv)
    mxx = 1.0 - kx * kx * inv
    myy = 1.0 - ky * ky * inv
    return mxx, myy, mxy


def split(table):
    high = table.astype(np.float32)
    return jnp.asarray(high)


def project_spectral(u, v, mxx, myy, mxy):
    half_y, half_x = u.shape[0] // 2, u.shape[1] // 2

    def swap(a):
        a = jnp.concatenate([a[:, half_x:], a[:, :half_x]], axis=1)
        return jnp.concatenate([a[half_y:], a[:half_y]], axis=0)

    rows = lax.broadcasted_iota(jnp.int32, u.shape, 0)
    cols = lax.broadcasted_iota(jnp.int32, u.shape, 1)
    corner = jnp.where((rows == half_y) & (cols == half_x), -0.5, 0.0)
    return (
        mxx * u + mxy * swap(v) + corner * v,
        myy * v + mxy * swap(u) + corner * u,
    )


def dot3(a, b):
    return jnp.dot(a, b, preferred_element_type=f32, precision=highest)


def gelu_both(z):
    z2 = z * z
    t = jnp.tanh(z * (A0 + A1 * z2))
    h = 0.5 * t + 0.5
    a = z * h
    return a, h + a * (1.0 - h) * (2.0 * A0 + 6.0 * A1 * z2)


def lroll(x, s):
    return pltpu.roll(x, s % x.shape[1], 1)


def shifts(x):
    return jnp.concatenate([lroll(x, 1), x, lroll(x, -1)], axis=0)


def unshifts(x):
    return jnp.concatenate([lroll(x, -1), x, lroll(x, 1)], axis=0)


def spread(ref, first, values):
    for k in range(ref.shape[0]):
        ref[k, pl.ds(first, values.shape[0], stride=8), :] = values[:, k * 128 : k * 128 + 128]


def collect(ref, first, count):
    planes = [ref[k, pl.ds(first, count, stride=8), :] for k in range(ref.shape[0])]
    return jnp.concatenate(planes, axis=1)


def rows_of(ref, first, count):
    at = pl.ds(first if isinstance(first, int) else pl.multiple_of(first, 8), count)
    return jnp.concatenate([ref[k, at, :] for k in range(ref.shape[0])], axis=1)


def put_rows(ref, first, values):
    at = pl.ds(
        first if isinstance(first, int) else pl.multiple_of(first, 8), values.shape[0]
    )
    for k in range(ref.shape[0]):
        ref[k, at, :] = values[:, k * 128 : k * 128 + 128]


def group4(s):
    i = lax.broadcasted_iota(jnp.int32, s.shape, 0)
    s = s + jnp.where(i % 2 == 0, pltpu.roll(s, 7, 0), pltpu.roll(s, 1, 0))
    return s + jnp.where((i // 2) % 2 == 0, pltpu.roll(s, 6, 0), pltpu.roll(s, 2, 0))


def point_order(offs):
    row = lax.broadcasted_iota(jnp.int32, (32, 16), 0)
    point = (row // 8) * 4 + row % 4
    comp = (row // 4) % 2
    parts = [
        jnp.where((comp == c) & (offs[c : c + 1, :] == point), 1.0, 0.0).astype(f32)
        for c in range(2)
    ]
    return jnp.concatenate(parts, axis=1)


def blocks(n, most=17):
    count = -(-n // most)
    return count, -(-n // count)


def forward_kernel(
    h, me_ref, vel_ref, up_ref, down_ref, w0, w1, w2, w3, offs_ref,
    prov_ref, vp_ref, vs_ref, face_ref, mix_ref, x_out, g_out, wk_ref, w7_ref, wf_ref, perm_ref, sq_ref,
    xb, gb, w7k, f8, xsem, gsem,
):
    rows = h + 2 * HALO
    me = me_ref[0]
    for k, piece in enumerate((w0, w1, w2, w3)):
        slot = jnp.bitwise_xor(me, k)
        at16 = pl.ds(pl.multiple_of(slot * 16, 16), 16)
        at8 = pl.ds(pl.multiple_of(slot * 8, 8), 8)
        for n in range(NL * 3):
            wk_ref[n, at16, :] = piece[n * 16 : n * 16 + 16]
        for j in range(3):
            block = piece[MIDROWS + j * 16 : MIDROWS + j * 16 + 16].astype(f32)
            w7k[j, at8, :] = block[0:8]
        wf_ref[at16, :] = piece[MIDROWS + 48 : MIDROWS + 64]
    perm = point_order(offs_ref[...])
    perm_ref[...] = perm
    perm_low = perm.astype(bf16)
    for i in range(3):
        w7_ref[i] = jnp.dot(perm_low, w7k[i].astype(bf16), preferred_element_type=f32).astype(bf16)

    vp_ref[:, 0:HALO] = up_ref[...]
    vp_ref[:, HALO : HALO + h] = vel_ref[...]
    vp_ref[:, HALO + h :] = down_ref[...]
    for c in range(2):
        plane = vp_ref[c]
        for d in range(4):
            spread(vs_ref, c * 4 + d, lroll(plane, 1 - d))

    def vs_rows(y, n):
        return rows_of(vs_ref, (y + HALO) * 8, 8 * n)

    def copies(l):
        return (
            pltpu.make_async_copy(xb.at[l, pl.ds(DEEP - 1, h + 2)], x_out.at[l], xsem.at[l]),
            pltpu.make_async_copy(
                gb.at[l, pl.ds(DEEP - l - 1, h + 2 * (l + 1))],
                g_out.at[l, pl.ds(0, h + 2 * (l + 1))],
                gsem.at[l],
            ),
        )

    wfirst = wf_ref[:, 0:24]
    bias = jnp.broadcast_to(wf_ref[:, 24:25].astype(f32), (C, KW))
    n = h + 2 * (DEEP - 1)
    count, size = blocks(n)

    def first_block(k, _):
        top = jnp.minimum(k * size, n - size) - (DEEP - 1)
        for r in range(size):
            y = top + r
            x = vs_rows(y - 1, 3).astype(bf16)
            z = jnp.dot(wfirst, x, preferred_element_type=f32)
            a, d = gelu_both(z + bias)
            xb[0, y + DEEP] = a.astype(bf16)
            gb[0, y + DEEP] = d.astype(bf16)
        return 0

    lax.fori_loop(0, count, first_block, 0)
    for copy in copies(0):
        copy.start()

    for l in range(1, NL + 1):
        weight = wk_ref[3 * (l - 1) : 3 * l].reshape(192, KW)
        bias = jnp.broadcast_to(weight[0:C, 192:193].astype(f32), (C, KW))
        weight = weight[:, 0:192]
        n = h + 2 * (DEEP - 1 - l)
        count, size = blocks(n)

        def block(k, _, l=l, weight=weight, bias=bias, n=n, size=size):
            top = jnp.minimum(k * size, n - size) - (DEEP - 1 - l) + DEEP
            p0 = p1 = None
            for r in range(-1, size + 1):
                o = jnp.dot(weight, shifts(xb[l - 1, top + r]), preferred_element_type=f32)
                if r >= 1:
                    a, d = gelu_both(p1 + o[128:192] + bias)
                    xb[l, top + r - 1] = a.astype(bf16)
                    gb[l, top + r - 1] = d.astype(bf16)
                p1 = o[64:128] if p0 is None else p0 + o[64:128]
                p0 = o[0:64]
            return 0

        lax.fori_loop(0, count, block, 0)
        for copy in copies(l):
            copy.start()

    weight = w7_ref[...].reshape(96, KW)
    bias = jnp.broadcast_to(weight[0:32, 192:193].astype(f32), (32, KW))
    weight = weight[:, 0:192]
    row = lax.broadcasted_iota(jnp.int32, (32, KW), 0)
    point = (row // 8) * 4 + row % 4
    second = jnp.where((row // 4) % 2 == 0, 6, 9)
    base = jnp.where((point == 5) | (point == second), 0.5, 0.0).astype(f32)
    n = h + 4
    count, size = blocks(n, 12)

    def last_block(k, _):
        top = jnp.minimum(k * size, n - size) - 2
        p0 = p1 = None
        for r in range(-1, size + 1):
            o = jnp.dot(weight, shifts(xb[NL, top + r + DEEP]), preferred_element_type=f32)
            if r >= 1:
                y = top + r - 1
                s = p1 + o[64:96] + bias
                mean = group4(s[0:8] + s[8:16] + s[16:24] + s[24:32]) * (1.0 / 16.0)
                mix = s - jnp.concatenate([mean] * 4, axis=0) + base
                mix_ref[pl.ds(pl.multiple_of((y + 2) * 32, 32), 32), :] = mix
                m = mix * vs_rows(y - 1, 4)
                m = group4(m[0:8] + m[8:16] + m[16:24] + m[24:32])
                put_rows(f8, (y + 2) * 8, m)
            p1 = o[32:64] if p0 is None else p0 + o[32:64]
            p0 = o[0:32]
        return 0

    lax.fori_loop(0, count, last_block, 0)
    for c in range(2):
        face_ref[c] = collect(f8, c * 4, h + 4)
    ue = face_ref[0, 2 : 2 + h]
    vn = face_ref[1, 2 : 2 + h]
    vn_south = face_ref[1, 1 : 1 + h]
    total = [jnp.sum(ue * ue) + jnp.sum(vn * vn)]
    own = update = 0.0
    for c in range(2):
        q = vp_ref[c, HALO : HALO + h]
        north = vp_ref[c, HALO + 1 : HALO + 1 + h]
        south = vp_ref[c, HALO - 1 : HALO - 1 + h]
        east, west = lroll(q, -1), lroll(q, 1)
        lap = east + west + north + south - 4.0 * q
        fx = ue * (q + east) * 0.5
        adv = fx - lroll(fx, 1) + vn * (q + north) * 0.5 - vn_south * (south + q) * 0.5
        new = q + time_step * (viscosity * lap - adv)
        prov_ref[c] = new
        own = own + jnp.sum(q * q)
        update = update + jnp.sum((new - q) * (new - q))
    lane = lax.broadcasted_iota(jnp.int32, (8, KW), 1)
    sq_ref[...] = jnp.where(
        lane == 0, own, jnp.where(lane == 1, total[0], jnp.where(lane == 2, update, 0.0))
    )
    for l in range(NL + 1):
        for copy in copies(l):
            copy.wait()


def backward_kernel(
    h, me_ref, cot_ref, t_ref, tt_ref, t2_ref, trow_ref, mxx_ref, myy_ref, mxy_ref,
    vp_ref, vs_ref, face_ref, mix_ref, x_in, g_in, wk_ref, w7_ref, wf_ref, perm_ref, sq_ref,
    vel_grad_ref, pack_ref,
    xb, gb, gz7, gz6, gz5, gz4, gz3, gz2, gz1, f8, adv_ref, acc_ref, gp_ref, near8, xsem, gsem,
):
    me_chan = me_ref[0]
    me_space = me_ref[1]

    def copies(l):
        return (
            pltpu.make_async_copy(x_in.at[l], xb.at[l], xsem.at[l]),
            pltpu.make_async_copy(
                g_in.at[l, pl.ds(0, h + 2 * (l + 1))],
                gb.at[l, pl.ds(0, h + 2 * (l + 1))],
                gsem.at[l],
            ),
        )

    for l in range(NL, -1, -1):
        for copy in copies(l):
            copy.start()

    n = h + 2 * GPH
    spectra = dot3(t2_ref[...], dot3(cot_ref[...], t_ref[...]))
    half = spectra.shape[0] // 2
    u, v = project_spectral(spectra[:half], spectra[half:], mxx_ref[...], myy_ref[...], mxy_ref[...])
    trow = trow_ref[me_space]
    gp_ref[0] = dot3(dot3(trow, u), tt_ref[...])
    gp_ref[1] = dot3(dot3(trow, v), tt_ref[...])

    m = n - 1
    fields = []
    gue = gvn = 0.0
    for c in range(2):
        g = -time_step * gp_ref[c, 0:m]
        g_north = -time_step * gp_ref[c, 1 : m + 1]
        q = vp_ref[c, HALO - GPH : HALO - GPH + m]
        q_north = vp_ref[c, HALO - GPH + 1 : HALO - GPH + 1 + m]
        gfx = g - lroll(g, -1)
        gfy = g - g_north
        gue = gue + gfx * (q + lroll(q, -1)) * 0.5
        gvn = gvn + gfy * (q + q_north) * 0.5
        adv_ref[c, 0:m] = gfy
        fields.append(gfx[GPH : GPH + h])
    for d in range(4):
        spread(f8, d, gue)
        spread(f8, 4 + d, gvn)
    ue = face_ref[0, 2 : 2 + h]
    vn = face_ref[1, 2 : 2 + h]
    vn_south = face_ref[1, 1 : 1 + h]
    for c in range(2):
        g = gp_ref[c, GPH : GPH + h]
        lap = (
            lroll(g, -1) + lroll(g, 1) + gp_ref[c, GPH + 1 : GPH + 1 + h]
            + gp_ref[c, GPH - 1 : GPH - 1 + h] - 4.0 * g
        )
        ex = fields[c] * ue
        ny = adv_ref[c, GPH : GPH + h] * vn
        sy = adv_ref[c, GPH - 1 : GPH - 1 + h] * vn_south
        vel_grad_ref[c] = g + time_step * viscosity * lap + 0.5 * (ex + lroll(ex, 1) + ny + sy)

    def f8_row(y):
        return rows_of(f8, (y + GPH) * 8, 8)

    def vs_rows(y, count):
        return rows_of(vs_ref, (y + HALO) * 8, 8 * count)

    def stencil_row(k, _):
        for r in range(2):
            y = 2 * k + r - 7
            face = f8_row(y)
            near = vs_rows(y - 1, 4)
            s = near[0:8] + near[8:16] + near[16:24] + near[24:32]
            mean = group4(s) * (1.0 / 16.0)
            gm = (near - jnp.concatenate([mean] * 4, axis=0)) * jnp.concatenate([face] * 4, axis=0)
            gz7[y + 7] = gm.astype(bf16)
        return 0

    lax.fori_loop(0, (h + 14) // 2, stencil_row, 0, unroll=4 if h >= 16 else 1)

    ones = jnp.ones((16, KW), bf16)

    def wgrad(columns, inputs):
        return lax.dot_general(
            jnp.concatenate(columns, axis=1),
            jnp.concatenate(inputs, axis=1),
            (((1,), (1,)), ((), ())),
            preferred_element_type=f32,
        )

    gzs = {7: gz7, 6: gz6, 5: gz5, 4: gz4, 3: gz3, 2: gz2, 1: gz1}
    for l in range(7, 1, -1):
        for copy in copies(l - 2):
            copy.wait()
        source, target = gzs[l], gzs[l - 1]
        xs, gs = xb.at[l - 2], gb.at[l - 2]
        if l == 7:
            parts = [w7_ref[i][:, 0:192].astype(f32) for i in range(3)]
            width = 32
        else:
            parts = [wk_ref[3 * (l - 2) + i][:, 0:192].astype(f32) for i in range(3)]
            width = C
        weight = jnp.concatenate(
            [
                jnp.concatenate([p[:, j * C : (j + 1) * C].T for j in range(3)], axis=1)
                for p in parts
            ],
            axis=0,
        ).astype(bf16)
        p0 = p1 = None
        acc = None
        for ys in (range(-l, h // 2), range(h // 2, h + l)):
            columns = {y: unshifts(source[y + l]) for y in ys}
            for y in ys:
                o = jnp.dot(weight, columns[y], preferred_element_type=f32)
                if y >= 2 - l:
                    ga = p1 + o[0:64]
                    target[y - 1 + l - 1] = (ga * gs[y - 1 + l - 1].astype(f32)).astype(bf16)
                p1 = o[64:128] if p0 is None else p0 + o[64:128]
                p0 = o[128:192]
            own = [y for y in ys if 0 <= y < h]
            part = wgrad(
                [columns[y] for y in own],
                [
                    jnp.concatenate([xs[y : y + 3].reshape(192, KW), ones], axis=0)
                    for y in own
                ],
            )
            acc = part if acc is None else acc + part
        if l == 7:
            back = perm_ref[...]
            acc = jnp.concatenate(
                [
                    lax.dot_general(
                        back, acc[j * 32 : j * 32 + 32], (((0,), (0,)), ((), ())),
                        preferred_element_type=f32, precision=highest,
                    )
                    for j in range(3)
                ],
                axis=0,
            )
        acc_ref[l - 1, 0 : 3 * width, 0:208] = acc

    wfirst = wf_ref[:, 0:32].astype(f32).T.astype(bf16)
    source = gz1
    outs = {}
    for y in range(-1, h + 1):
        outs[y] = jnp.dot(wfirst[0:24], source[y + 1], preferred_element_type=f32)
    acc_ref[0, 0:64, 0:40] = wgrad(
        [source[y + 1] for y in range(h)],
        [
            jnp.concatenate(
                [vs_rows(y - 1, 3), jnp.ones((16, KW), f32)], axis=0
            ).astype(bf16)
            for y in range(h)
        ],
    )
    for y in range(h):
        total = outs[y + 1][0:8] + outs[y][8:16] + outs[y - 1][16:24]
        for k in range(4):
            at = y + 1 - k
            total = total + f8_row(at) * mix_ref[pl.ds((at + 2) * 32 + k * 8, 8), :]
        put_rows(near8, y * 8, total)
    for c in range(2):
        total = vel_grad_ref[c]
        for d in range(4):
            total = total + lroll(collect(near8, c * 4 + d, h), d - 1)
        vel_grad_ref[c] = total

    for k, other in enumerate((0, 2, 1, 3)):
        slot = jnp.bitwise_xor(me_chan, other)
        for l in range(NL):
            for j in range(3):
                piece = acc_ref[l + 1, pl.ds(pl.multiple_of(j * 64 + slot * 16, 16), 16), :]
                pack_ref[k, (3 * l + j) * 16 : (3 * l + j) * 16 + 16, :] = piece.astype(bf16)
        last = [
            acc_ref[6, pl.ds(pl.multiple_of(j * 32 + slot * 8, 8), 8), :] for j in range(3)
        ]
        pack_ref[k, MIDROWS : MIDROWS + 32, :] = jnp.concatenate(
            last + [sq_ref[...]], axis=0
        ).astype(bf16)
        pack_ref[k, MIDROWS + 32 : MIDROWS + 48, :] = acc_ref[
            0, pl.ds(pl.multiple_of(slot * 16, 16), 16), :
        ].astype(bf16)


def project_kernel(h, me_ref, prov_ref, t_ref, tt_ref, t2_ref, trow_ref, mxx_ref, myy_ref, mxy_ref, out_ref, sq_ref):
    me_space = me_ref[1]
    trow = trow_ref[me_space][GPH : GPH + h]
    total = 0.0
    for t in range(prov_ref.shape[1]):
        field = prov_ref[:, t].reshape(-1, KW)
        spectra = dot3(t2_ref[...], dot3(field, t_ref[...]))
        half = spectra.shape[0] // 2
        u, v = project_spectral(
            spectra[:half], spectra[half:], mxx_ref[...], myy_ref[...], mxy_ref[...]
        )
        total = total + jnp.sum(u * u) + jnp.sum(v * v)
        out_ref[0, t] = dot3(dot3(trow, u), tt_ref[...])
        out_ref[1, t] = dot3(dot3(trow, v), tt_ref[...])
    sq_ref[...] = jnp.full((8, 128), total, f32)


def moved(x, axis, step):
    n = lax.axis_size(axis)
    return lax.ppermute(x, axis, [(i, (i + step) % n) for i in range(n)])


def swapped(x, axis, bit):
    n = lax.axis_size(axis)
    return lax.ppermute(x, axis, [(i, i ^ bit) for i in range(n)])


def halos(own, width):
    height = own.shape[1]
    if height >= width:
        return (
            moved(own[:, height - width :], "space", 1),
            moved(own[:, :width], "space", -1),
        )
    hops = -(-width // height)
    up = jnp.concatenate([moved(own, "space", k) for k in range(hops, 0, -1)], axis=1)
    down = jnp.concatenate([moved(own, "space", -k) for k in range(1, hops + 1)], axis=1)
    return up[:, up.shape[1] - width :], down[:, :width]


def packed_weights(w_first, b_first, w_mid, b_mid, w_last, b_last):
    mid = jnp.transpose(w_mid, (0, 1, 4, 2, 3)).reshape(NL, 3, 16, 192)
    bias = jnp.broadcast_to(b_mid[:, None, :, None], (NL, 3, 16, 64))
    mid = jnp.concatenate([mid, bias], axis=3).reshape(MIDROWS, KW)
    last = jnp.transpose(w_last, (0, 3, 1, 2)).reshape(3, 8, 192)
    last = jnp.concatenate([last, jnp.broadcast_to(b_last[None, :, None], (3, 8, 64))], axis=2)
    last = jnp.pad(last, ((0, 0), (0, 8), (0, 0))).reshape(48, KW)
    first = jnp.pad(jnp.transpose(w_first, (3, 0, 2, 1)), ((0, 0), (0, 0), (0, 0), (0, 1)))
    first = first.reshape(16, 24)
    first = jnp.concatenate([first, jnp.broadcast_to(b_first[:, None], (16, KW - 24))], axis=1)
    return jnp.concatenate([mid, last, first], axis=0)


def vmem(count):
    return [pl.BlockSpec(memory_space=pltpu.VMEM)] * count


def per_device(velocity, w_first, b_first, w_mid, b_mid, w_last, b_last, offsets, cotangent):
    traj, h, nx = velocity.shape[1:]
    space = lax.axis_size("space")
    ny = h * space
    me_chan = lax.axis_index("chan")
    me_space = lax.axis_index("space")
    me = jnp.stack([me_chan, me_space]).astype(jnp.int32)
    rows = h + 2 * HALO
    own = lax.dynamic_index_in_dim(velocity, me_chan, 1, keepdims=False)
    own_cot = lax.dynamic_index_in_dim(cotangent, me_chan, 1, keepdims=False)

    packed = packed_weights(w_first, b_first, w_mid, b_mid, w_last, b_last)
    across = swapped(packed, "chan", 2)
    up, down = halos(own, HALO)
    beside = swapped(packed, "chan", 1)
    diagonal = swapped(across, "chan", 1)
    cot_full = lax.all_to_all(
        jnp.broadcast_to(own_cot[None], (space,) + own_cot.shape), "space", 0, 0, tiled=True
    ).reshape(space * 2 * h, nx)

    any_space = pl.BlockSpec(memory_space=pl.ANY)
    smem = pl.BlockSpec(memory_space=pltpu.SMEM)
    shape = jax.ShapeDtypeStruct
    deep = h + 2 * DEEP
    prov, vp, vs, face, mix, x_all, g_all, wk, w7, wf, perm, squares = pl.pallas_call(
        functools.partial(forward_kernel, h),
        out_shape=[
            shape((2, h, nx), f32),
            shape((2, rows, nx), f32),
            shape((nx // 128, rows * 8, 128), f32),
            shape((2, h + 4, nx), f32),
            shape(((h + 4) * 32, nx), f32),
            shape((NL + 1, h + 2, C, nx), bf16),
            shape((NL + 1, h + 2 * (NL + 1), C, nx), bf16),
            shape((NL * 3, C, KW), bf16),
            shape((3, 32, KW), bf16),
            shape((C, KW), bf16),
            shape((32, 32), f32),
            shape((8, KW), f32),
        ],
        in_specs=[smem] + vmem(8),
        out_specs=vmem(5) + [any_space, any_space] + vmem(5),
        scratch_shapes=[
            pltpu.VMEM((NL + 1, deep, C, nx), bf16),
            pltpu.VMEM((NL + 1, deep, C, nx), bf16),
            pltpu.VMEM((3, 32, KW), f32),
            pltpu.VMEM((nx // 128, (h + 4) * 8, 128), f32),
            pltpu.SemaphoreType.DMA((NL + 1,)),
            pltpu.SemaphoreType.DMA((NL + 1,)),
        ],
        compiler_params=pltpu.CompilerParams(vmem_limit_bytes=56 * 2**20),
        name="forward",
    )(me, own, up, down, packed, beside, across, diagonal, offsets)

    everywhere = lax.all_gather(prov, ("space", "chan"), axis=0, tiled=False)

    ty = basis(ny)
    tx = basis(nx)
    t_full = jnp.asarray(tx.astype(np.float32))
    t_back = jnp.asarray(np.ascontiguousarray(tx.T).astype(np.float32))
    wide = np.zeros((2 * ny, space, 2, h))
    for c in range(2):
        wide[c * ny : (c + 1) * ny, :, c, :] = ty.T.reshape(ny, space, h)
    t_wide = jnp.asarray(wide.reshape(2 * ny, 2 * ny).astype(np.float32))
    ring = (np.arange(space)[:, None] * h + np.arange(h + 2 * GPH)[None, :] - GPH) % ny
    t_rows = jnp.asarray(ty[ring].astype(np.float32))
    spectral = [jnp.asarray(m.astype(np.float32)) for m in multipliers(ny, nx)]

    vel_grad, pack = pl.pallas_call(
        functools.partial(backward_kernel, h),
        out_shape=[shape((2, h, nx), f32), shape((4, MIDROWS + 48, KW), bf16)],
        in_specs=[smem] + vmem(12) + [any_space, any_space] + vmem(5),
        out_specs=vmem(2),
        scratch_shapes=[
            pltpu.VMEM((NL + 1, h + 2, C, nx), bf16),
            pltpu.VMEM((NL + 1, h + 2 * (NL + 1), C, nx), bf16),
            pltpu.VMEM((h + 14, 32, nx), bf16),
        ]
        + [pltpu.VMEM((h + 2 * l, C, nx), bf16) for l in range(6, 0, -1)]
        + [
            pltpu.VMEM((nx // 128, (h + 2 * GPH) * 8, 128), f32),
            pltpu.VMEM((2, h + 2 * GPH, nx), f32),
            pltpu.VMEM((7, 192, KW), f32),
            pltpu.VMEM((2, h + 2 * GPH, nx), f32),
            pltpu.VMEM((nx // 128, h * 8, 128), f32),
            pltpu.SemaphoreType.DMA((NL + 1,)),
            pltpu.SemaphoreType.DMA((NL + 1,)),
        ],
        compiler_params=pltpu.CompilerParams(vmem_limit_bytes=60 * 2**20),
        name="backward",
    )(
        me, cot_full, t_full, t_back, t_wide, t_rows, *spectral,
        vp, vs, face, mix, x_all, g_all, wk, w7, wf, perm, squares,
    )

    pair = (pack[0:2].astype(f32) + swapped(pack[2:4], "chan", 1).astype(f32)).astype(bf16)
    total = pair[0].astype(f32) + swapped(pair[1], "chan", 2).astype(f32)
    bit = 1
    while bit < space:
        low = total.astype(bf16)
        total = low.astype(f32) + swapped(low, "space", bit).astype(f32)
        bit *= 2

    new_velocity, new_sq = pl.pallas_call(
        functools.partial(project_kernel, h),
        out_shape=[shape((2, traj, h, nx), f32), shape((8, 128), f32)],
        in_specs=[smem] + vmem(8),
        out_specs=vmem(2),
        compiler_params=pltpu.CompilerParams(vmem_limit_bytes=56 * 2**20),
        name="project",
    )(
        me, everywhere.reshape(space, traj, 2 * h, nx), t_full, t_back, t_wide, t_rows, *spectral
    )

    mid = total[:MIDROWS].reshape(NL, 3, 16, KW)
    w_mid_grad = jnp.transpose(mid[..., :192].reshape(NL, 3, 16, 3, C), (0, 3, 1, 4, 2))
    b_mid_grad = mid[:, 0, :, 192]
    last = total[MIDROWS : MIDROWS + 24].reshape(3, 8, KW)
    w_last_grad = jnp.transpose(last[..., :192].reshape(3, 8, 3, C), (2, 0, 3, 1))
    b_last_grad = last[0, :, 192]
    first = total[MIDROWS + 32 :]
    w_first_grad = jnp.transpose(first[:, :24].reshape(16, 3, 2, 4)[..., :3], (1, 3, 2, 0))
    b_first_grad = first[:, 24]
    sums = jnp.concatenate([total[MIDROWS + 24, 0:3], new_sq[0, 0:1]])
    rms_stats = jnp.sqrt(sums / (2 * traj * ny * nx))
    return (
        new_velocity,
        vel_grad[:, None],
        w_first_grad,
        b_first_grad,
        w_mid_grad,
        b_mid_grad,
        w_last_grad,
        b_last_grad,
        rms_stats,
    )


def solution(mesh):
    return jax.shard_map(
        per_device,
        mesh=mesh,
        in_specs=(
            P(None, None, "space", None),
            P(None, None, None, "chan"),
            P("chan"),
            P(None, None, None, None, "chan"),
            P(None, "chan"),
            P(None, None, None, "chan"),
            P("chan"),
            P(),
            P(None, None, "space", None),
        ),
        out_specs=(
            P(None, None, "space", None),
            P(None, "chan", "space", None),
            P(None, None, None, "chan"),
            P("chan"),
            P(None, None, None, None, "chan"),
            P(None, "chan"),
            P(None, None, None, "chan"),
            P("chan"),
            P(),
        ),
        check_vma=False,
    )
```

time: 1800 us -> 157 us (0.09)
  matrix products: 630 us -> 0 us
  waiting for transfers between devices: 567 us -> 25.8 us
  local copies, waits for them, and re-layouts: 343 us -> 14.2 us
  other arithmetic: 109 us -> 3.22 us
  starting transfers between devices: 92.8 us -> 13.2 us
  Pallas kernels: 0 us -> 64.9 us
    dot_general x215 -> x0, matrix products: 630 us -> none  [the longest x63 379 us: conv_backward(): jnp.einsum('co,obrx->cbrx', weight[row_tap, col_tap], shifted_out, prefer...]
    reduce_scatter x7 -> x0, waiting for transfers between devices: 281 us -> none  [the longest x6 281 us: reduce_channels(): return lax.psum_scatter(values, 'chan', scatter_dimension=0, tiled=True)]
    all_gather x7 -> x1, waiting for transfers between devices: 194 us -> 0.01 us  [per_device(): everywhere = lax.all_gather(prov, ('space', 'chan'), axis=0, tiled=False)]
    slice x58 -> x9, local copies, waits for them, and re-layouts: 191 us -> 3.17 us  [the longest x1 1.25 us: per_device(): sums = jnp.concatenate([total[MIDROWS + 24, 0:3], new_sq[0, 0:1]])]
    unnamed x892 -> x22, local copies, waits for them, and re-layouts: 87.2 us -> 5.29 us
    pallas_call x0 -> x3, Pallas kernels: none -> 64.9 us  [the longest x1 23.7 us: per_device(): pl.pallas_call(functools.partial(backward_kernel, h), out_shape=[shape((2...]
    ppermute x32 -> x10, starting transfers between devices: 69.1 us -> 13.2 us  [the longest x8 8.28 us: swapped(): return lax.ppermute(x, axis, [(i, i ^ bit) for i in range(n)])]
    psum x1 -> x0, waiting for transfers between devices: 47.9 us -> none  [per_device(): lax.psum((gradients[0], gradients[1], gradients[2], gradients[3], gradien...]
  transfers between devices with their start and end apart: 51 -> 11, of which waited for: 27 -> 7; matrix products, arithmetic and copies ran while one was open for 23% -> 5% of each run, Pallas kernels for 0% -> 15%
where the time goes in v1:
time: 157 us
  Pallas kernels  64.9 us (41%)
  waiting for transfers between devices  25.8 us (16%)
  blocking collectives  21.1 us (13%)
  local copies, waits for them, and re-layouts  14.2 us (9%)
  between operations  14.2 us (9%)
  starting transfers between devices  13.2 us (8%)
  other arithmetic  3.22 us (2%)
    ppermute x8, waiting for transfers between devices, swapped(): return lax.ppermute(x, axis, [(i, i ^ bit) for i in range(n)])  24.4 us
    pallas_call x1, Pallas kernels, per_device(): pl.pallas_call(functools.partial(backward_kernel, h), out_shape=[shape((2...  23.7 us
    pallas_call x1, Pallas kernels, per_device(): pl.pallas_call(functools.partial(forward_kernel, h), out_shape=[shape((2,...  23.3 us
    all_to_all x1, blocking collectives, per_device(): lax.all_to_all(jnp.broadcast_to(own_cot[None], (space,) + own_cot.shape),...  21.1 us
    pallas_call x1, Pallas kernels, per_device(): pl.pallas_call(functools.partial(project_kernel, h), out_shape=[shape((2,...  17.9 us
    ppermute x8, starting transfers between devices, swapped(): return lax.ppermute(x, axis, [(i, i ^ bit) for i in range(n)])  8.28 us
    unnamed x22, local copies, waits for them, and re-layouts  5.29 us
    ppermute x2, starting transfers between devices, moved(): return lax.ppermute(x, axis, [(i, (i + step) % n) for i in range(n)])  4.92 us
  transfers between devices with their start and end apart: 11, of which 7 were waited for; matrix products, arithmetic and copies ran while one was open for 5% of the time, Pallas kernels for 15%

profile of v1, /device:TPU:0, one launch (start us, length us, event | category | flops | bytes accessed | tf_op | source)
XLA Modules:
  0.0 156.6 jit_solution(16849755741915734595)
XLA Ops:
  7.2 1.1 copy.42
  12.6 3.0 %collective-permute-start.3 = (bf16[304,256]{1,0:T(8,128)(2,1)S(1)}, bf16[304,256]{1,0:T(8,128)(2,1)S(1)}, u32[]{:S(2)}, u32[]{:S(2)}) collective-permute-start(bf16[304,256]{1,0:T(8,128)(2,1)S(1)} %maximum_maximum_fusion.w0), channel_id=1, source_target_pairs={{0,16},{8,24},{16,0},{24,8},{1,17},{9,25},{17,1},{25,9},{2,18},{10... | collective-permute-start | bytes 466952 | tf_op jit(solution)/shard_map/ppermute | solution.py:508
  15.7 4.0 %collective-permute-done.3.w2 = bf16[304,256]{1,0:T(8,128)(2,1)S(1)} collective-permute-done((bf16[304,256]{1,0:T(8,128)(2,1)S(1)}, bf16[304,256]{1,0:T(8,128)(2,1)S(1)}, u32[]{:S(2)}, u32[]{:S(2)}) %collective-permute-start.3) | collective-permute-done | bytes 155680 | tf_op jit(solution)/shard_map/ppermute | solution.py:508
  19.7 1.8 %collective-permute-start = (f32[2,16,256]{2,1,0:T(8,128)S(1)}, f32[2,16,256]{2,1,0:T(8,128)S(1)}, u32[]{:S(2)}, u32[]{:S(2)}) collective-permute-start(f32[2,16,256]{2,1,0:T(8,128)S(1)} %get-tuple-element.69), channel_id=1, source_target_pairs={{0,1},{1,2},{2,3},{3,4},{4,5},{5,6},{6,7},{7,0},{8,9},{9,10},{10,1... | collective-permute-start | bytes 98312 | tf_op jit(solution)/shard_map/ppermute | solution.py:503
  21.5 3.1 %collective-permute-start.1 = (f32[2,16,256]{2,1,0:T(8,128)S(1)}, f32[2,16,256]{2,1,0:T(8,128)S(1)}, u32[]{:S(2)}, u32[]{:S(2)}) collective-permute-start(f32[2,16,256]{2,1,0:T(8,128)S(1)} %get-tuple-element.68), channel_id=1, source_target_pairs={{0,7},{1,0},{2,1},{3,2},{4,3},{5,4},{6,5},{7,6},{8,15},{9,8},{10,9... | collective-permute-start | bytes 98312 | tf_op jit(solution)/shard_map/ppermute | solution.py:503
  25.3 1.3 collective-permute-done.up_ref
  27.9 23.3 %forward.1 = (f32[2,32,256]{2,1,0:T(8,128)}, f32[2,64,256]{2,1,0:T(8,128)}, f32[2,512,128]{2,1,0:T(8,128)}, f32[2,36,256]{2,1,0:T(8,128)}, f32[1152,256]{1,0:T(8...) custom-call(s32[2]{0:T(128)} %pad_add_fusion.me_ref, ...), custom_call_target="tpu_custom_call" | custom-call | tf_op jit(solution)/shard_map/forward/pallas_call | solution.py:565
  51.3 0.9 dynamic-slice_bitcast_fusion
  52.2 21.1 %all_to_all.5 = f32[8,2,32,256]{3,2,1,0:T(8,128)} all-to-all(f32[8,2,32,256]{3,2,1,0:T(8,128)S(1)} %broadcast_in_dim.39), channel_id=1, replica_groups=mesh['chan'=4,'space'=8] {'space'}, dimensions={0} | all-to-all | bytes 1048576 | tf_op jit(solution)/shard_map/all_to_all | solution.py:557
  73.3 23.7 %backward.1 = (f32[2,32,256]{2,1,0:T(8,128)}, bf16[4,288,256]{2,1,0:T(8,128)(2,1)}) custom-call(s32[2]{0:T(128)} %pad_add_fusion.me_ref, f32[512,256]{1,0:T(8,128)} %bitcast.41, f32[256,256]{1,0:T(8,128)} %constant.36.clone.t_ref, f32[256,256]{1,0:T(8,128)} %constant.37.clone.tt_ref, f32[512,512]{1,0:T(8,128)} %constant.38.clone.t2_ref, ...), custom_call_target="tpu_custom_call" | custom-call | tf_op jit(solution)/shard_map/backward/pallas_call | solution.py:609
  96.9 1.0 slice.57
  98.0 1.6 %collective-permute-done.5 = bf16[2,288,256]{2,1,0:T(8,128)(2,1)S(1)} collective-permute-done((bf16[2,288,256]{2,1,0:T(8,128)(2,1)S(1)}, bf16[2,288,256]{2,1,0:T(8,128)(2,1)S(1)}, u32[]{:S(2)}, u32[]{:S(2)}) %collective-permute-start.5) | collective-permute-done | bytes 294944 | tf_op jit(solution)/shard_map/ppermute | solution.py:508
  99.6 1.0 add_convert_fusion
  100.6 1.6 %collective-permute-start.6 = (bf16[288,256]{1,0:T(8,128)(2,1)S(1)}, bf16[288,256]{1,0:T(8,128)(2,1)S(1)}, u32[]{:S(2)}, u32[]{:S(2)}) collective-permute-start(bf16[288,256]{1,0:T(8,128)(2,1)S(1)} %slice_bitcast_fusion), channel_id=1, source_target_pairs={{0,16},{8,24},{16,0},{24,8},{1,17},{9,25},{17,1},{25,9},{2,18},{10... | collective-permute-start | bytes 442376 | tf_op jit(solution)/shard_map/ppermute | solution.py:508
  102.2 4.4 %collective-permute-done.6 = bf16[288,256]{1,0:T(8,128)(2,1)S(1)} collective-permute-done((bf16[288,256]{1,0:T(8,128)(2,1)S(1)}, bf16[288,256]{1,0:T(8,128)(2,1)S(1)}, u32[]{:S(2)}, u32[]{:S(2)}) %collective-permute-start.6) | collective-permute-done | bytes 147488 | tf_op jit(solution)/shard_map/ppermute | solution.py:508
  106.6 1.6 %collective-permute-start.7 = (bf16[288,256]{1,0:T(8,128)(2,1)S(1)}, bf16[288,256]{1,0:T(8,128)(2,1)S(1)}, u32[]{:S(2)}, u32[]{:S(2)}) collective-permute-start(bf16[288,256]{1,0:T(8,128)(2,1)S(1)} %fusion), channel_id=1, source_target_pairs={{0,1},{1,0},{2,3},{3,2},{4,5},{5,4},{6,7},{7,6},{8,9},{9,8},{10,11... | collective-permute-start | bytes 442376 | tf_op jit(solution)/shard_map/ppermute | solution.py:508
  108.2 3.6 %collective-permute-done.7 = bf16[288,256]{1,0:T(8,128)(2,1)S(1)} collective-permute-done((bf16[288,256]{1,0:T(8,128)(2,1)S(1)}, bf16[288,256]{1,0:T(8,128)(2,1)S(1)}, u32[]{:S(2)}, u32[]{:S(2)}) %collective-permute-start.7) | collective-permute-done | bytes 147488 | tf_op jit(solution)/shard_map/ppermute | solution.py:508
  111.9 1.1 collective-permute-start.8
  113.0 4.1 %collective-permute-done.8 = bf16[288,256]{1,0:T(8,128)(2,1)S(1)} collective-permute-done((bf16[288,256]{1,0:T(8,128)(2,1)S(1)}, bf16[288,256]{1,0:T(8,128)(2,1)S(1)}, u32[]{:S(2)}, u32[]{:S(2)}) %collective-permute-start.8) | collective-permute-done | bytes 147488 | tf_op jit(solution)/shard_map/ppermute | solution.py:508
  117.1 0.9 collective-permute-start.9
  118.1 6.7 %collective-permute-done.9 = bf16[288,256]{1,0:T(8,128)(2,1)S(1)} collective-permute-done((bf16[288,256]{1,0:T(8,128)(2,1)S(1)}, bf16[288,256]{1,0:T(8,128)(2,1)S(1)}, u32[]{:S(2)}, u32[]{:S(2)}) %collective-permute-start.9) | collective-permute-done | bytes 147488 | tf_op jit(solution)/shard_map/ppermute | solution.py:508
  129.4 17.9 %project.1 = (f32[2,4,32,256]{3,2,1,0:T(8,128)}, f32[8,128]{1,0:T(8,128)}) custom-call(s32[2]{0:T(128)} %pad_add_fusion.me_ref, f32[8,4,64,256]{3,2,1,0:T(8,128)} %bitcast.40, f32[256,256]{1,0:T(8,128)} %constant.36.clone.t_ref, f32[256,256]{1,0:T(8,128)} %constant.37.clone.tt_ref, f32[512,512]{1,0:T(8,128)} %constant.38.clone.t2_ref, ...), custom_call_target="tpu_custom_call" | custom-call | tf_op jit(solution)/shard_map/project/pallas_call | solution.py:644
  147.3 1.3 slice.70
  148.5 1.2 fusion.4
  (63 shorter events, 11.1 us)
Async XLA Ops:
  7.2 8.5 %copy-start = (f32[2,4,32,256]{3,2,1,0:T(8,128)S(1)}, f32[2,4,32,256]{3,2,1,0:T(8,128)}, u32[]{:S(2)}) copy-start(f32[2,4,32,256]{3,2,1,0:T(8,128)} %param.16) | copy-start | bytes 786436
  7.2 122.2 %all-gather.3.cloned.1.call-start = ((), (), s32[]{:S(2)}) async-start(), calls=%async_computation.1 | async-start | bytes 2162688 | tf_op jit(solution)/shard_map/all_gather | solution.py:595
  12.6 14.0 %copy-start.1 = (bf16[304,256]{1,0:T(8,128)(2,1)}, bf16[304,256]{1,0:T(8,128)(2,1)S(1)}, u32[]{:S(2)}) copy-start(bf16[304,256]{1,0:T(8,128)(2,1)S(1)} %maximum_maximum_fusion.w0) | copy-start | bytes 466948
  12.6 7.0 %collective-permute-start.3 = (bf16[304,256]{1,0:T(8,128)(2,1)S(1)}, bf16[304,256]{1,0:T(8,128)(2,1)S(1)}, u32[]{:S(2)}, u32[]{:S(2)}) collective-permute-start(bf16[304,256]{1,0:T(8,128)(2,1)S(1)} %maximum_maximum_fusion.w0), channel_id=1, source_target_pairs={{0,16},{8,24},{16,0},{24,8},{1,17},{9,25},{17,1},{25,9},{2,18},{10... | collective-permute-start | bytes 466952 | tf_op jit(solution)/shard_map/ppermute | solution.py:508
  15.7 10.9 %collective-permute-start.2 = (bf16[304,256]{1,0:T(8,128)(2,1)S(1)}, bf16[304,256]{1,0:T(8,128)(2,1)S(1)}, u32[]{:S(2)}, u32[]{:S(2)}) collective-permute-start(bf16[304,256]{1,0:T(8,128)(2,1)S(1)} %maximum_maximum_fusion.w0), channel_id=1, source_target_pairs={{0,8},{8,0},{16,24},{24,16},{1,9},{9,1},{17,25},{25,17},{2,10},{10... | collective-permute-start | bytes 466952 | tf_op jit(solution)/shard_map/ppermute | solution.py:508
  15.7 10.9 %copy-start.2 = (f32[2,32,256]{2,1,0:T(8,128)}, f32[2,32,256]{2,1,0:T(8,128)S(1)}, u32[]{:S(2)}) copy-start(f32[2,32,256]{2,1,0:T(8,128)S(1)} %dynamic-slice_bitcast_fusion.1.vel_ref) | copy-start | bytes 196612
  19.7 6.9 %copy-start.3 = (bf16[304,256]{1,0:T(8,128)(2,1)}, bf16[304,256]{1,0:T(8,128)(2,1)S(1)}, u32[]{:S(2)}) copy-start(bf16[304,256]{1,0:T(8,128)(2,1)S(1)} %collective-permute-done.3.w2) | copy-start | bytes 466948
  19.7 6.9 %collective-permute-start.4 = (bf16[304,256]{1,0:T(8,128)(2,1)S(1)}, bf16[304,256]{1,0:T(8,128)(2,1)S(1)}, u32[]{:S(2)}, u32[]{:S(2)}) collective-permute-start(bf16[304,256]{1,0:T(8,128)(2,1)S(1)} %collective-permute-done.3.w2), channel_id=1, source_target_pairs={{0,8},{8,0},{16,24},{24,16},{1,9},{9,1},{17,25},{25,17},{2,10},{10... | collective-permute-start | bytes 466952 | tf_op jit(solution)/shard_map/ppermute | solution.py:508
  19.7 6.9 %collective-permute-start = (f32[2,16,256]{2,1,0:T(8,128)S(1)}, f32[2,16,256]{2,1,0:T(8,128)S(1)}, u32[]{:S(2)}, u32[]{:S(2)}) collective-permute-start(f32[2,16,256]{2,1,0:T(8,128)S(1)} %get-tuple-element.69), channel_id=1, source_target_pairs={{0,1},{1,2},{2,3},{3,4},{4,5},{5,6},{6,7},{7,0},{8,9},{9,10},{10,1... | collective-permute-start | bytes 98312 | tf_op jit(solution)/shard_map/ppermute | solution.py:503
  21.5 5.0 %collective-permute-start.1 = (f32[2,16,256]{2,1,0:T(8,128)S(1)}, f32[2,16,256]{2,1,0:T(8,128)S(1)}, u32[]{:S(2)}, u32[]{:S(2)}) collective-permute-start(f32[2,16,256]{2,1,0:T(8,128)S(1)} %get-tuple-element.68), channel_id=1, source_target_pairs={{0,7},{1,0},{2,1},{3,2},{4,3},{5,4},{6,5},{7,6},{8,15},{9,8},{10,9... | collective-permute-start | bytes 98312 | tf_op jit(solution)/shard_map/ppermute | solution.py:503
  26.6 0.6 copy-start.6
  26.6 0.6 copy-start.7
  26.6 0.7 copy-start.4
  27.2 0.7 copy-start.5
  97.9 1.6 %collective-permute-start.5 = (bf16[2,288,256]{2,1,0:T(8,128)(2,1)S(1)}, bf16[2,288,256]{2,1,0:T(8,128)(2,1)S(1)}, u32[]{:S(2)}, u32[]{:S(2)}) collective-permute-start(bf16[2,288,256]{2,1,0:T(8,128)(2,1)S(1)} %slice.57), channel_id=1, source_target_pairs={{0,8},{8,0},{16,24},{24,16},{1,9},{9,1},{17,25},{25,17},{2,10},{10... | collective-permute-start | bytes 884744 | tf_op jit(solution)/shard_map/ppermute | solution.py:508
  100.6 6.0 %collective-permute-start.6 = (bf16[288,256]{1,0:T(8,128)(2,1)S(1)}, bf16[288,256]{1,0:T(8,128)(2,1)S(1)}, u32[]{:S(2)}, u32[]{:S(2)}) collective-permute-start(bf16[288,256]{1,0:T(8,128)(2,1)S(1)} %slice_bitcast_fusion), channel_id=1, source_target_pairs={{0,16},{8,24},{16,0},{24,8},{1,17},{9,25},{17,1},{25,9},{2,18},{10... | collective-permute-start | bytes 442376 | tf_op jit(solution)/shard_map/ppermute | solution.py:508
  106.6 5.2 %collective-permute-start.7 = (bf16[288,256]{1,0:T(8,128)(2,1)S(1)}, bf16[288,256]{1,0:T(8,128)(2,1)S(1)}, u32[]{:S(2)}, u32[]{:S(2)}) collective-permute-start(bf16[288,256]{1,0:T(8,128)(2,1)S(1)} %fusion), channel_id=1, source_target_pairs={{0,1},{1,0},{2,3},{3,2},{4,5},{5,4},{6,7},{7,6},{8,9},{9,8},{10,11... | collective-permute-start | bytes 442376 | tf_op jit(solution)/shard_map/ppermute | solution.py:508
  111.9 5.2 %collective-permute-start.8 = (bf16[288,256]{1,0:T(8,128)(2,1)S(1)}, bf16[288,256]{1,0:T(8,128)(2,1)S(1)}, u32[]{:S(2)}, u32[]{:S(2)}) collective-permute-start(bf16[288,256]{1,0:T(8,128)(2,1)S(1)} %add_convert_fusion.2), channel_id=1, source_target_pairs={{0,2},{1,3},{2,0},{3,1},{4,6},{5,7},{6,4},{7,5},{8,10},{9,11},{10,... | collective-permute-start | bytes 442376 | tf_op jit(solution)/shard_map/ppermute | solution.py:508
  117.1 7.7 %collective-permute-start.9 = (bf16[288,256]{1,0:T(8,128)(2,1)S(1)}, bf16[288,256]{1,0:T(8,128)(2,1)S(1)}, u32[]{:S(2)}, u32[]{:S(2)}) collective-permute-start(bf16[288,256]{1,0:T(8,128)(2,1)S(1)} %add_convert_fusion.1), channel_id=1, source_target_pairs={{0,4},{1,5},{2,6},{3,7},{4,0},{5,1},{6,2},{7,3},{8,12},{9,13},{10,... | collective-permute-start | bytes 442376 | tf_op jit(solution)/shard_map/ppermute | solution.py:508
Sparse Core Ops, SparseCore 0:
  51.4 59.0 all-gather.2

commit v2 on v1

--- a/solution.py
+++ b/solution.py
@@ -59,11 +59,6 @@
     return mxx, myy, mxy
 
 
-def split(table):
-    high = table.astype(np.float32)
-    return jnp.asarray(high)
-
-
 def project_spectral(u, v, mxx, myy, mxy):
     half_y, half_x = u.shape[0] // 2, u.shape[1] // 2
 
@@ -80,8 +75,40 @@
     )
 
 
-def dot3(a, b):
-    return jnp.dot(a, b, preferred_element_type=f32, precision=highest)
+def halves(x):
+    high = x.astype(bf16)
+    return high, (x - high.astype(f32)).astype(bf16)
+
+
+def product(a, b):
+    def dot(x, y):
+        return jnp.dot(x, y, preferred_element_type=f32)
+
+    return dot(a[0], b[0]) + (dot(a[1], b[0]) + dot(a[0], b[1]))
+
+
+def both(ref):
+    return ref[0], ref[1]
+
+
+def spectrum(h, field_ref, tx_ref, ty_ref):
+    ny = field_ref.shape[0] * h if h % 8 == 0 else field_ref.shape[0] // 2
+    if h % 8 == 0:
+        fields = [field_ref[:, c].reshape(ny, KW) for c in range(2)]
+        field = jnp.concatenate(fields, axis=0)
+    else:
+        field = field_ref[...]
+    along = product(halves(field), both(tx_ref))
+    table = both(ty_ref)
+    if h % 8 == 0:
+        return [product(table, halves(along[c * ny : (c + 1) * ny])) for c in range(2)]
+    out = product(table, halves(along))
+    return out[:ny], out[ny:]
+
+
+def project_back(trow, u, back_ref):
+    back = both(back_ref)
+    return product(halves(product(trow, halves(u))), back)
 
 
 def gelu_both(z):
@@ -144,7 +171,7 @@
     return jnp.concatenate(parts, axis=1)
 
 
-def blocks(n, most=17):
+def blocks(n, most=27):
     count = -(-n // most)
     return count, -(-n // count)
 
@@ -282,7 +309,8 @@
         fx = ue * (q + east) * 0.5
         adv = fx - lroll(fx, 1) + vn * (q + north) * 0.5 - vn_south * (south + q) * 0.5
         new = q + time_step * (viscosity * lap - adv)
-        prov_ref[c] = new
+        for k in range(prov_ref.shape[0]):
+            prov_ref[k, c] = new
         own = own + jnp.sum(q * q)
         update = update + jnp.sum((new - q) * (new - q))
     lane = lax.broadcasted_iota(jnp.int32, (8, KW), 1)
@@ -295,9 +323,9 @@
 
 
 def backward_kernel(
-    h, me_ref, cot_ref, t_ref, tt_ref, t2_ref, trow_ref, mxx_ref, myy_ref, mxy_ref,
+    h, me_ref, cot_ref, tx_ref, ty_ref, back_ref, trow_ref, mxx_ref, myy_ref, mxy_ref,
     vp_ref, vs_ref, face_ref, mix_ref, x_in, g_in, wk_ref, w7_ref, wf_ref, perm_ref, sq_ref,
-    vel_grad_ref, pack_ref,
+    vel_grad_ref, keep_ref, send_ref,
     xb, gb, gz7, gz6, gz5, gz4, gz3, gz2, gz1, f8, adv_ref, acc_ref, gp_ref, near8, xsem, gsem,
 ):
     me_chan = me_ref[0]
@@ -318,12 +346,11 @@
             copy.start()
 
     n = h + 2 * GPH
-    spectra = dot3(t2_ref[...], dot3(cot_ref[...], t_ref[...]))
-    half = spectra.shape[0] // 2
-    u, v = project_spectral(spectra[:half], spectra[half:], mxx_ref[...], myy_ref[...], mxy_ref[...])
-    trow = trow_ref[me_space]
-    gp_ref[0] = dot3(dot3(trow, u), tt_ref[...])
-    gp_ref[1] = dot3(dot3(trow, v), tt_ref[...])
+    u, v = spectrum(h, cot_ref, tx_ref, ty_ref)
+    u, v = project_spectral(u, v, mxx_ref[...], myy_ref[...], mxy_ref[...])
+    trow = (trow_ref[0, me_space], trow_ref[1, me_space])
+    gp_ref[0] = project_back(trow, u, back_ref)
+    gp_ref[1] = project_back(trow, v, back_ref)
 
     m = n - 1
     fields = []
@@ -466,6 +493,8 @@
 
     for k, other in enumerate((0, 2, 1, 3)):
         slot = jnp.bitwise_xor(me_chan, other)
+        pack_ref = (keep_ref, send_ref)[k // 2]
+        k = k % 2
         for l in range(NL):
             for j in range(3):
                 piece = acc_ref[l + 1, pl.ds(pl.multiple_of(j * 64 + slot * 16, 16), 16), :]
@@ -481,21 +510,96 @@
         ].astype(bf16)
 
 
-def project_kernel(h, me_ref, prov_ref, t_ref, tt_ref, t2_ref, trow_ref, mxx_ref, myy_ref, mxy_ref, out_ref, sq_ref):
+def project_kernel(h, me_ref, prov_ref, tx_ref, ty_ref, back_ref, trow_ref, mxx_ref, myy_ref, mxy_ref, out_ref):
     me_space = me_ref[1]
-    trow = trow_ref[me_space][GPH : GPH + h]
-    total = 0.0
-    for t in range(prov_ref.shape[1]):
-        field = prov_ref[:, t].reshape(-1, KW)
-        spectra = dot3(t2_ref[...], dot3(field, t_ref[...]))
-        half = spectra.shape[0] // 2
-        u, v = project_spectral(
-            spectra[:half], spectra[half:], mxx_ref[...], myy_ref[...], mxy_ref[...]
-        )
-        total = total + jnp.sum(u * u) + jnp.sum(v * v)
-        out_ref[0, t] = dot3(dot3(trow, u), tt_ref[...])
-        out_ref[1, t] = dot3(dot3(trow, v), tt_ref[...])
-    sq_ref[...] = jnp.full((8, 128), total, f32)
+    trow = tuple(trow_ref[k, me_space][GPH : GPH + h] for k in range(2))
+    u, v = spectrum(h, prov_ref, tx_ref, ty_ref)
+    u, v = project_spectral(u, v, mxx_ref[...], myy_ref[...], mxy_ref[...])
+    out_ref[0:h] = project_back(trow, u, back_ref)
+    out_ref[h : 2 * h] = project_back(trow, v, back_ref)
+    out_ref[2 * h :] = jnp.full((8, KW), jnp.sum(u * u) + jnp.sum(v * v), f32)
+
+
+def prepare_kernel(h, me_ref, vel_ref, cot_ref, wm_ref, wl_ref, wf_ref, bm_ref, bf_ref, bl_ref, pack_ref, own_ref, top_ref, bottom_ref, cot_all_ref, tall, wide):
+    me = me_ref[0]
+    own = vel_ref[:, me]
+    own_ref[...] = own
+    if h >= HALO:
+        top_ref[...] = own[:, :HALO]
+        bottom_ref[...] = own[:, h - HALO :]
+    cot = cot_ref[:, me]
+    for k in range(cot_all_ref.shape[0]):
+        cot_all_ref[k] = cot
+    wide[...] = jnp.zeros_like(wide)
+    wide[0:NL, 0:16] = bm_ref[...].astype(f32)
+    wide[NL : NL + 1, 0:16] = bf_ref[...].astype(f32)
+    wide[NL + 1 : NL + 2, 0:8] = bl_ref[...].astype(f32)
+    columns = wide[...].T
+
+    def column(k, count, width):
+        return jnp.broadcast_to(columns[0:count, k : k + 1], (count, width))
+
+    for l in range(NL):
+        for i in range(3):
+            parts = [wm_ref[l, i, j] for j in range(3)] + [column(l, 16, 64).astype(bf16)]
+            at = (3 * l + i) * 16
+            pack_ref[at : at + 16, :] = jnp.concatenate(parts, axis=1)
+    for i in range(3):
+        parts = [wl_ref[i, j].astype(f32) for j in range(3)] + [column(NL + 1, 8, 64)]
+        block = jnp.concatenate(parts, axis=1)
+        at = MIDROWS + i * 16
+        pack_ref[at : at + 16, :] = jnp.concatenate([block, jnp.zeros_like(block)], axis=0).astype(bf16)
+    tall[...] = jnp.zeros_like(tall)
+    for i in range(3):
+        for j in range(3):
+            taps = wf_ref[i, j].astype(f32)
+            for c in range(2):
+                at = i * 8 + c * 4 + j
+                tall[at : at + 1, 0:16] = taps[c : c + 1]
+    tall[24:25, 0:16] = bf_ref[...].astype(f32)
+    first = tall[...].T[0:16]
+    pack_ref[MIDROWS + 48 :, :] = jnp.concatenate([first, jnp.zeros_like(first)], axis=1).astype(bf16)
+
+
+def finish_kernel(h, cells, me_ref, low_ref, other_ref, n0, n1, n2, n3, new_ref, wf_ref, bf_ref, wm_ref, bm_ref, wl_ref, bl_ref, rms_ref, parts):
+    me = me_ref[0]
+    for k, piece in enumerate((n0, n1, n2, n3)):
+        slot = jnp.bitwise_xor(me, k)
+        new_ref[0, slot] = piece[0:h]
+        new_ref[1, slot] = piece[h : 2 * h]
+        parts[slot] = piece[2 * h :]
+
+    def total(at, count):
+        return low_ref[at : at + count, :].astype(f32) + other_ref[at : at + count, :].astype(f32)
+
+    def turned(block):
+        return jnp.concatenate([block, jnp.zeros((128 - block.shape[0], 128), f32)], axis=0).T
+
+    for l in range(NL):
+        for j in range(3):
+            block = total((3 * l + j) * 16, 16)
+            for i in range(3):
+                wm_ref[l, i, j] = block[:, i * 64 : i * 64 + 64]
+            if j == 0:
+                bm_ref[l : l + 1, :] = turned(block[:, 128:256])[64:65, 0:16]
+    tail = total(MIDROWS, 32)
+    for j in range(3):
+        block = tail[j * 8 : j * 8 + 8]
+        for i in range(3):
+            wl_ref[i, j] = block[:, i * 64 : i * 64 + 64]
+        if j == 0:
+            bl_ref[...] = turned(block[:, 128:256])[64:65, 0:8]
+    first = turned(total(MIDROWS + 32, 16)[:, 0:128])
+    for i in range(3):
+        for j in range(3):
+            for c in range(2):
+                at = i * 8 + c * 4 + j
+                wf_ref[i, j, c : c + 1, :] = first[at : at + 1, 0:16]
+    bf_ref[...] = first[24:25, 0:16]
+    news = (parts[0] + parts[1]) + (parts[2] + parts[3])
+    lane = lax.broadcasted_iota(jnp.int32, (8, 128), 1)
+    sums = jnp.where(lane == 3, news[:, 0:128], tail[24:32, 0:128])
+    rms_ref[...] = jnp.sqrt(sums * (1.0 / cells))[0:1, 0:4]
 
 
 def moved(x, axis, step):
@@ -508,30 +612,34 @@
     return lax.ppermute(x, axis, [(i, i ^ bit) for i in range(n)])
 
 
-def halos(own, width):
+def halos(own, top, bottom, width):
     height = own.shape[1]
     if height >= width:
-        return (
-            moved(own[:, height - width :], "space", 1),
-            moved(own[:, :width], "space", -1),
-        )
+        return moved(bottom, "space", 1), moved(top, "space", -1)
     hops = -(-width // height)
     up = jnp.concatenate([moved(own, "space", k) for k in range(hops, 0, -1)], axis=1)
     down = jnp.concatenate([moved(own, "space", -k) for k in range(1, hops + 1)], axis=1)
     return up[:, up.shape[1] - width :], down[:, :width]
 
 
-def packed_weights(w_first, b_first, w_mid, b_mid, w_last, b_last):
-    mid = jnp.transpose(w_mid, (0, 1, 4, 2, 3)).reshape(NL, 3, 16, 192)
-    bias = jnp.broadcast_to(b_mid[:, None, :, None], (NL, 3, 16, 64))
-    mid = jnp.concatenate([mid, bias], axis=3).reshape(MIDROWS, KW)
-    last = jnp.transpose(w_last, (0, 3, 1, 2)).reshape(3, 8, 192)
-    last = jnp.concatenate([last, jnp.broadcast_to(b_last[None, :, None], (3, 8, 64))], axis=2)
-    last = jnp.pad(last, ((0, 0), (0, 8), (0, 0))).reshape(48, KW)
-    first = jnp.pad(jnp.transpose(w_first, (3, 0, 2, 1)), ((0, 0), (0, 0), (0, 0), (0, 1)))
-    first = first.reshape(16, 24)
-    first = jnp.concatenate([first, jnp.broadcast_to(b_first[:, None], (16, KW - 24))], axis=1)
-    return jnp.concatenate([mid, last, first], axis=0)
+def tables(h, space, nx):
+    ny = h * space
+    ty, tx = basis(ny), basis(nx)
+
+    def two(table):
+        high = table.astype(np.float32).astype(jnp.bfloat16)
+        low = (table - high.astype(np.float64)).astype(np.float32).astype(jnp.bfloat16)
+        return jnp.asarray(np.stack([high, low]))
+
+    back_y = ty.T
+    if h % 8:
+        wide = np.zeros((2, ny, space, 2, h))
+        for c in range(2):
+            wide[c, :, :, c, :] = ty.T.reshape(ny, space, h)
+        back_y = wide.reshape(2 * ny, 2 * ny)
+    ring = (np.arange(space)[:, None] * h + np.arange(h + 2 * GPH)[None, :] - GPH) % ny
+    spectral = [jnp.asarray(m.astype(np.float32)) for m in multipliers(ny, nx)]
+    return [two(tx), two(back_y), two(tx.T), two(ty[ring])] + spectral
 
 
 def vmem(count):
@@ -546,26 +654,42 @@
     me_space = lax.axis_index("space")
     me = jnp.stack([me_chan, me_space]).astype(jnp.int32)
     rows = h + 2 * HALO
-    own = lax.dynamic_index_in_dim(velocity, me_chan, 1, keepdims=False)
-    own_cot = lax.dynamic_index_in_dim(cotangent, me_chan, 1, keepdims=False)
-
-    packed = packed_weights(w_first, b_first, w_mid, b_mid, w_last, b_last)
+    shape = jax.ShapeDtypeStruct
+    smem = pl.BlockSpec(memory_space=pltpu.SMEM)
+    limit = pltpu.CompilerParams(vmem_limit_bytes=56 * 2**20)
+    packed, own, top, bottom, cot_all = pl.pallas_call(
+        functools.partial(prepare_kernel, h),
+        out_shape=[
+            shape((MIDROWS + 64, KW), bf16),
+            shape((2, h, nx), f32),
+            shape((2, min(h, HALO), nx), f32),
+            shape((2, min(h, HALO), nx), f32),
+            shape((space, 2, h, nx), f32),
+        ],
+        in_specs=[smem] + vmem(8),
+        out_specs=vmem(5),
+        scratch_shapes=[pltpu.VMEM((128, 128), f32), pltpu.VMEM((8, 128), f32)],
+        compiler_params=limit,
+        name="prepare",
+    )(
+        me, velocity, cotangent, jnp.swapaxes(w_mid, 3, 4), jnp.swapaxes(w_last, 2, 3), w_first,
+        b_mid, b_first[None], b_last[None],
+    )
     across = swapped(packed, "chan", 2)
-    up, down = halos(own, HALO)
+    up, down = halos(own, top, bottom, HALO)
+    across, up, down, cot_all = lax.optimization_barrier((across, up, down, cot_all))
     beside = swapped(packed, "chan", 1)
     diagonal = swapped(across, "chan", 1)
-    cot_full = lax.all_to_all(
-        jnp.broadcast_to(own_cot[None], (space,) + own_cot.shape), "space", 0, 0, tiled=True
-    ).reshape(space * 2 * h, nx)
+    cot_full = lax.all_to_all(cot_all, "space", 0, 0, tiled=True)
+    if h % 8:
+        cot_full = cot_full.reshape(space * 2 * h, nx)
 
     any_space = pl.BlockSpec(memory_space=pl.ANY)
-    smem = pl.BlockSpec(memory_space=pltpu.SMEM)
-    shape = jax.ShapeDtypeStruct
     deep = h + 2 * DEEP
     prov, vp, vs, face, mix, x_all, g_all, wk, w7, wf, perm, squares = pl.pallas_call(
         functools.partial(forward_kernel, h),
         out_shape=[
-            shape((2, h, nx), f32),
+            shape((space, 2, h, nx), f32),
             shape((2, rows, nx), f32),
             shape((nx // 128, rows * 8, 128), f32),
             shape((2, h + 4, nx), f32),
@@ -588,29 +712,22 @@
             pltpu.SemaphoreType.DMA((NL + 1,)),
             pltpu.SemaphoreType.DMA((NL + 1,)),
         ],
-        compiler_params=pltpu.CompilerParams(vmem_limit_bytes=56 * 2**20),
+        compiler_params=limit,
+        cost_estimate=pl.CostEstimate(
+            flops=2 * 7 * deep * nx * 9 * C * C, bytes_accessed=2**25, transcendentals=6 * deep * nx * C
+        ),
         name="forward",
     )(me, own, up, down, packed, beside, across, diagonal, offsets)
 
-    everywhere = lax.all_gather(prov, ("space", "chan"), axis=0, tiled=False)
-
-    ty = basis(ny)
-    tx = basis(nx)
-    t_full = jnp.asarray(tx.astype(np.float32))
-    t_back = jnp.asarray(np.ascontiguousarray(tx.T).astype(np.float32))
-    wide = np.zeros((2 * ny, space, 2, h))
-    for c in range(2):
-        wide[c * ny : (c + 1) * ny, :, c, :] = ty.T.reshape(ny, space, h)
-    t_wide = jnp.asarray(wide.reshape(2 * ny, 2 * ny).astype(np.float32))
-    ring = (np.arange(space)[:, None] * h + np.arange(h + 2 * GPH)[None, :] - GPH) % ny
-    t_rows = jnp.asarray(ty[ring].astype(np.float32))
-    spectral = [jnp.asarray(m.astype(np.float32)) for m in multipliers(ny, nx)]
-
-    vel_grad, pack = pl.pallas_call(
+    everywhere = lax.all_to_all(prov, "space", 0, 0, tiled=True)
+    if h % 8:
+        everywhere = everywhere.reshape(space * 2 * h, nx)
+    constants = tables(h, space, nx)
+    vel_grad, keep, send = pl.pallas_call(
         functools.partial(backward_kernel, h),
-        out_shape=[shape((2, h, nx), f32), shape((4, MIDROWS + 48, KW), bf16)],
+        out_shape=[shape((2, h, nx), f32)] + [shape((2, MIDROWS + 48, KW), bf16)] * 2,
         in_specs=[smem] + vmem(12) + [any_space, any_space] + vmem(5),
-        out_specs=vmem(2),
+        out_specs=vmem(3),
         scratch_shapes=[
             pltpu.VMEM((NL + 1, h + 2, C, nx), bf16),
             pltpu.VMEM((NL + 1, h + 2 * (NL + 1), C, nx), bf16),
@@ -626,53 +743,60 @@
             pltpu.SemaphoreType.DMA((NL + 1,)),
             pltpu.SemaphoreType.DMA((NL + 1,)),
         ],
-        compiler_params=pltpu.CompilerParams(vmem_limit_bytes=60 * 2**20),
+        compiler_params=limit,
+        cost_estimate=pl.CostEstimate(
+            flops=4 * 7 * deep * nx * 9 * C * C, bytes_accessed=2**25, transcendentals=0
+        ),
         name="backward",
-    )(
-        me, cot_full, t_full, t_back, t_wide, t_rows, *spectral,
-        vp, vs, face, mix, x_all, g_all, wk, w7, wf, perm, squares,
-    )
-
-    pair = (pack[0:2].astype(f32) + swapped(pack[2:4], "chan", 1).astype(f32)).astype(bf16)
-    total = pair[0].astype(f32) + swapped(pair[1], "chan", 2).astype(f32)
+    )(me, cot_full, *constants, vp, vs, face, mix, x_all, g_all, wk, w7, wf, perm, squares)
+
+    new_own = pl.pallas_call(
+        functools.partial(project_kernel, h),
+        out_shape=shape((2 * h + 8, nx), f32),
+        in_specs=[smem] + vmem(8),
+        out_specs=vmem(1)[0],
+        compiler_params=limit,
+        cost_estimate=pl.CostEstimate(flops=2**31, bytes_accessed=2**22, transcendentals=0),
+        name="project",
+    )(me, everywhere, *constants)
+
+    pair = (keep.astype(f32) + swapped(send, "chan", 1).astype(f32)).astype(bf16)
+    low = (pair[0].astype(f32) + swapped(pair[1], "chan", 2).astype(f32)).astype(bf16)
     bit = 1
-    while bit < space:
-        low = total.astype(bf16)
-        total = low.astype(f32) + swapped(low, "space", bit).astype(f32)
+    while 2 * bit < space:
+        low = (low.astype(f32) + swapped(low, "space", bit).astype(f32)).astype(bf16)
         bit *= 2
-
-    new_velocity, new_sq = pl.pallas_call(
-        functools.partial(project_kernel, h),
-        out_shape=[shape((2, traj, h, nx), f32), shape((8, 128), f32)],
-        in_specs=[smem] + vmem(8),
-        out_specs=vmem(2),
-        compiler_params=pltpu.CompilerParams(vmem_limit_bytes=56 * 2**20),
-        name="project",
-    )(
-        me, everywhere.reshape(space, traj, 2 * h, nx), t_full, t_back, t_wide, t_rows, *spectral
-    )
-
-    mid = total[:MIDROWS].reshape(NL, 3, 16, KW)
-    w_mid_grad = jnp.transpose(mid[..., :192].reshape(NL, 3, 16, 3, C), (0, 3, 1, 4, 2))
-    b_mid_grad = mid[:, 0, :, 192]
-    last = total[MIDROWS : MIDROWS + 24].reshape(3, 8, KW)
-    w_last_grad = jnp.transpose(last[..., :192].reshape(3, 8, 3, C), (2, 0, 3, 1))
-    b_last_grad = last[0, :, 192]
-    first = total[MIDROWS + 32 :]
-    w_first_grad = jnp.transpose(first[:, :24].reshape(16, 3, 2, 4)[..., :3], (1, 3, 2, 0))
-    b_first_grad = first[:, 24]
-    sums = jnp.concatenate([total[MIDROWS + 24, 0:3], new_sq[0, 0:1]])
-    rms_stats = jnp.sqrt(sums / (2 * traj * ny * nx))
+    other = swapped(low, "space", bit)
+    news = [new_own] + [swapped(new_own, "chan", k) for k in (1, 2, 3)]
+
+    new_velocity, w_first_grad, b_first_grad, w_mid_grad, b_mid_grad, w_last_grad, b_last_grad, rms_stats = pl.pallas_call(
+        functools.partial(finish_kernel, h, 2 * traj * ny * nx),
+        out_shape=[
+            shape((2, traj, h, nx), f32),
+            shape((3, 3, 2, 16), f32),
+            shape((1, 16), f32),
+            shape((NL, 3, 3, 16, C), f32),
+            shape((NL, 16), f32),
+            shape((3, 3, 8, C), f32),
+            shape((1, 8), f32),
+            shape((1, 4), f32),
+        ],
+        in_specs=[smem] + vmem(6),
+        out_specs=vmem(8),
+        scratch_shapes=[pltpu.VMEM((4, 8, KW), f32)],
+        compiler_params=limit,
+        name="finish",
+    )(me, low, other, *news)
     return (
         new_velocity,
         vel_grad[:, None],
         w_first_grad,
-        b_first_grad,
-        w_mid_grad,
+        b_first_grad[0],
+        jnp.swapaxes(w_mid_grad, 3, 4),
         b_mid_grad,
-        w_last_grad,
-        b_last_grad,
-        rms_stats,
+        jnp.swapaxes(w_last_grad, 2, 3),
+        b_last_grad[0],
+        rms_stats[0],
     )
 
 

time: 157 us -> 108 us (0.69)
  blocking collectives: 21.1 us -> 0 us
  starting transfers between devices: 13.2 us -> 29.1 us
  Pallas kernels: 64.9 us -> 50.8 us
  between operations: 14.2 us -> 0.92 us
  local copies, waits for them, and re-layouts: 14.2 us -> 3.6 us
  waiting for transfers between devices: 25.8 us -> 21.3 us
    all_to_all x1 -> x0, blocking collectives: 21.1 us -> none  [per_device(): lax.all_to_all(jnp.broadcast_to(own_cot[None], (space,) + own_cot.shape),...]
    all_to_all x0 -> x2, starting transfers between devices: none -> 12.2 us  [the longest x1 6.19 us: per_device(): everywhere = lax.all_to_all(prov, 'space', 0, 0, tiled=True)]
    pallas_call x2 -> x4, Pallas kernels: 41.2 us -> 29.5 us  [the longest x1 21.5 us: per_device(): pl.pallas_call(functools.partial(forward_kernel, h), out_shape=[shape((sp...]
    ppermute x8 -> x11, waiting for transfers between devices: 24.4 us -> 19.2 us  [swapped(): return lax.ppermute(x, axis, [(i, i ^ bit) for i in range(n)])]
    ppermute x8 -> x11, starting transfers between devices: 8.28 us -> 12.2 us  [swapped(): return lax.ppermute(x, axis, [(i, i ^ bit) for i in range(n)])]
    broadcast_in_dim x7 -> x0, local copies, waits for them, and re-layouts: 3.23 us -> none  [the longest x2 0.9 us: per_device(): jnp.broadcast_to(own_cot[None], (space,) + own_cot.shape)]
    slice x9 -> x0, local copies, waits for them, and re-layouts: 3.17 us -> none  [the longest x1 1.25 us: per_device(): sums = jnp.concatenate([total[MIDROWS + 24, 0:3], new_sq[0, 0:1]])]
    pallas_call x1, Pallas kernels: 23.7 us -> 21.3 us  [per_device(): pl.pallas_call(functools.partial(backward_kernel, h), out_shape=[shape((2...]
  transfers between devices with their start and end apart: 11 -> 15, of which waited for: 7 -> 7; matrix products, arithmetic and copies ran while one was open for 5% -> 0% of each run, Pallas kernels for 15% -> 24%
where the time goes in v2:
time: 108 us; the launch traced here: 107 us
  Pallas kernels  50.8 us (47%)
  starting transfers between devices  29.1 us (27%)
  waiting for transfers between devices  21.3 us (20%)
  local copies, waits for them, and re-layouts  3.6 us (3%)
  other arithmetic  1.74 us (2%)
    pallas_call x1, Pallas kernels, per_device(): pl.pallas_call(functools.partial(forward_kernel, h), out_shape=[shape((sp...  21.5 us
    pallas_call x1, Pallas kernels, per_device(): pl.pallas_call(functools.partial(backward_kernel, h), out_shape=[shape((2...  21.3 us
    ppermute x11, waiting for transfers between devices, swapped(): return lax.ppermute(x, axis, [(i, i ^ bit) for i in range(n)])  19.2 us
    ppermute x11, starting transfers between devices, swapped(): return lax.ppermute(x, axis, [(i, i ^ bit) for i in range(n)])  12.2 us
    all_to_all x1, starting transfers between devices, per_device(): everywhere = lax.all_to_all(prov, 'space', 0, 0, tiled=True)  6.19 us
    all_to_all x1, starting transfers between devices, per_device(): cot_full = lax.all_to_all(cot_all, 'space', 0, 0, tiled=True)  5.99 us
    ppermute x2, starting transfers between devices, moved(): return lax.ppermute(x, axis, [(i, (i + step) % n) for i in range(n)])  4.72 us
    pallas_call x1, Pallas kernels, per_device(): pl.pallas_call(functools.partial(project_kernel, h), out_shape=shape((2 *...  3.82 us
  transfers between devices with their start and end apart: 15, of which 7 were waited for; matrix products, arithmetic and copies ran while one was open for 0% of the time, Pallas kernels for 24%

profile of v2, /device:TPU:0, one launch (start us, length us, event | category | flops | bytes accessed | tf_op | source)
XLA Modules:
  0.0 107.4 jit_solution(13769068949166539276)
XLA Ops:
  1.2 2.1 %prepare.1 = (bf16[304,256]{1,0:T(8,128)(2,1)}, f32[2,32,256]{2,1,0:T(8,128)}, f32[2,16,256]{2,1,0:T(8,128)}, f32[2,16,256]{2,1,0:T(8,128)}, f32[8,2,32,256]{3,2,1,0:T(8,128)}) custom-call(s32[2]{0:T(128)} %pad_add_fusion.me_ref, f32[2,4,32,256]{3,2,1,0:T(8,128)} %vel_ref.1, f32[2,4,32,256]{3,2,1,0:T(8,128)} %cot_ref.1, bf16[5,3,3,16,64]{4,3,2,1,0:T(8,128)(2,1)} %bitcast.21, ...), custom_call_target="tpu_custom_call" | custom-call | tf_op jit(solution)/shard_map/prepare/pallas_call | solution.py:660
  3.3 2.9 %collective-permute-start = (bf16[304,256]{1,0:T(8,128)(2,1)}, bf16[304,256]{1,0:T(8,128)(2,1)S(1)}, u32[]{:S(2)}, u32[]{:S(2)}) collective-permute-start(bf16[304,256]{1,0:T(8,128)(2,1)} %get-tuple-element.41.w0), channel_id=1, source_target_pairs={{0,16},{8,24},{16,0},{24,8},{1,17},{9,25},{17,1},{25,9},{2,18},{10... | collective-permute-start | bytes 466952 | tf_op jit(solution)/shard_map/ppermute | solution.py:612
  6.3 1.5 %collective-permute-start.1 = (f32[2,16,256]{2,1,0:T(8,128)}, f32[2,16,256]{2,1,0:T(8,128)S(1)}, u32[]{:S(2)}, u32[]{:S(2)}) collective-permute-start(f32[2,16,256]{2,1,0:T(8,128)} %get-tuple-element.42), channel_id=1, source_target_pairs={{0,1},{1,2},{2,3},{3,4},{4,5},{5,6},{6,7},{7,0},{8,9},{9,10},{10,1... | collective-permute-start | bytes 98312 | tf_op jit(solution)/shard_map/ppermute | solution.py:607
  7.8 3.2 %collective-permute-start.2 = (f32[2,16,256]{2,1,0:T(8,128)}, f32[2,16,256]{2,1,0:T(8,128)S(1)}, u32[]{:S(2)}, u32[]{:S(2)}) collective-permute-start(f32[2,16,256]{2,1,0:T(8,128)} %get-tuple-element.43), channel_id=1, source_target_pairs={{0,7},{1,0},{2,1},{3,2},{4,3},{5,4},{6,5},{7,6},{8,15},{9,8},{10,9... | collective-permute-start | bytes 98312 | tf_op jit(solution)/shard_map/ppermute | solution.py:607
  11.0 2.1 %collective-permute-done.1.up_ref = f32[2,16,256]{2,1,0:T(8,128)S(1)} collective-permute-done((f32[2,16,256]{2,1,0:T(8,128)}, f32[2,16,256]{2,1,0:T(8,128)S(1)}, u32[]{:S(2)}, u32[]{:S(2)}) %collective-permute-start.1) | collective-permute-done | bytes 32800 | tf_op jit(solution)/shard_map/ppermute | solution.py:607
  13.1 6.0 %all-to-all-start = ((f32[8,2,32,256]{3,2,1,0:T(8,128)}), f32[8,2,32,256]{3,2,1,0:T(8,128)S(1)}, u32[]{:S(2)}, u32[]{:S(2)}) async-start(f32[8,2,32,256]{3,2,1,0:T(8,128)} %get-tuple-element.45), calls=%async_computation | async-start | bytes 1048576 | tf_op jit(solution)/shard_map/all_to_all | solution.py:683
  19.6 1.1 %collective-permute-done.3.w1 = bf16[304,256]{1,0:T(8,128)(2,1)S(1)} collective-permute-done((bf16[304,256]{1,0:T(8,128)(2,1)}, bf16[304,256]{1,0:T(8,128)(2,1)S(1)}, u32[]{:S(2)}, u32[]{:S(2)}) %collective-permute-start.3) | collective-permute-done | bytes 155680 | tf_op jit(solution)/shard_map/ppermute | solution.py:612
  21.4 21.5 %forward.1 = (f32[8,2,32,256]{3,2,1,0:T(8,128)}, f32[2,64,256]{2,1,0:T(8,128)}, f32[2,512,128]{2,1,0:T(8,128)}, f32[2,36,256]{2,1,0:T(8,128)}, f32[1152,256]{1,0...) custom-call(s32[2]{0:T(128)} %pad_add_fusion.me_ref, ...), custom_call_target="tpu_custom_call" | custom-call | flops 7398752256 | bytes 33554432 | tf_op jit(solution)/shard_map/forward/pallas_call | solution.py:689
  42.9 0.8 copy-done.1
  43.7 21.3 %backward.1 = (f32[2,32,256]{2,1,0:T(8,128)}, bf16[2,288,256]{2,1,0:T(8,128)(2,1)}, bf16[2,288,256]{2,1,0:T(8,128)(2,1)}) custom-call(s32[2]{0:T(128)} %pad_add_fusion.me_ref, f32[8,2,32,256]{3,2,1,0:T(8,128)} %copy-done.1, bf16[2,256,256]{2,1,0:T(8,128)(2,1)} %constant.23.clone.tx_ref, bf16[2,256,256]{2,1,0:T(8,128)(2,1)} %constant.24.clone.ty_ref.back_ref, ...), custom_call_target="tpu_custom_call" | custom-call | flops 14797504512 | bytes 33554432 | tf_op jit(solution)/shard_map/backward/pallas_call | solution.py:726
  65.3 1.6 %collective-permute-done.5 = bf16[2,288,256]{2,1,0:T(8,128)(2,1)S(1)} collective-permute-done((bf16[2,288,256]{2,1,0:T(8,128)(2,1)}, bf16[2,288,256]{2,1,0:T(8,128)(2,1)S(1)}, u32[]{:S(2)}, u32[]{:S(2)}) %collective-permute-start.5) | collective-permute-done | bytes 294944 | tf_op jit(solution)/shard_map/ppermute | solution.py:612
  66.9 1.0 add_convert_fusion
  68.4 6.2 %all-to-all-start.1 = ((f32[8,2,32,256]{3,2,1,0:T(8,128)}), f32[8,2,32,256]{3,2,1,0:T(8,128)S(1)}, u32[]{:S(2)}, u32[]{:S(2)}) async-start(f32[8,2,32,256]{3,2,1,0:T(8,128)} %get-tuple-element.63), calls=%async_computation.1 | async-start | bytes 1048576 | tf_op jit(solution)/shard_map/all_to_all | solution.py:722
  74.6 2.1 %collective-permute-start.7 = (bf16[288,256]{1,0:T(8,128)(2,1)S(1)}, bf16[288,256]{1,0:T(8,128)(2,1)S(1)}, u32[]{:S(2)}, u32[]{:S(2)}) collective-permute-start(bf16[288,256]{1,0:T(8,128)(2,1)S(1)} %fusion), channel_id=1, source_target_pairs={{0,1},{1,0},{2,3},{3,2},{4,5},{5,4},{6,7},{7,6},{8,9},{9,8},{10,11... | collective-permute-start | bytes 442376 | tf_op jit(solution)/shard_map/ppermute | solution.py:612
  76.7 8.0 %collective-permute-done.7 = bf16[288,256]{1,0:T(8,128)(2,1)S(1)} collective-permute-done((bf16[288,256]{1,0:T(8,128)(2,1)S(1)}, bf16[288,256]{1,0:T(8,128)(2,1)S(1)}, u32[]{:S(2)}, u32[]{:S(2)}) %collective-permute-start.7) | collective-permute-done | bytes 147488 | tf_op jit(solution)/shard_map/ppermute | solution.py:612
  84.7 1.9 %collective-permute-start.8 = (bf16[288,256]{1,0:T(8,128)(2,1)S(1)}, bf16[288,256]{1,0:T(8,128)(2,1)S(1)}, u32[]{:S(2)}, u32[]{:S(2)}) collective-permute-start(bf16[288,256]{1,0:T(8,128)(2,1)S(1)} %add_convert_fusion.2), channel_id=1, source_target_pairs={{0,2},{1,3},{2,0},{3,1},{4,6},{5,7},{6,4},{7,5},{8,10},{9,11},{10,... | collective-permute-start | bytes 442376 | tf_op jit(solution)/shard_map/ppermute | solution.py:612
  86.6 4.1 %collective-permute-done.8 = bf16[288,256]{1,0:T(8,128)(2,1)S(1)} collective-permute-done((bf16[288,256]{1,0:T(8,128)(2,1)S(1)}, bf16[288,256]{1,0:T(8,128)(2,1)S(1)}, u32[]{:S(2)}, u32[]{:S(2)}) %collective-permute-start.8) | collective-permute-done | bytes 147488 | tf_op jit(solution)/shard_map/ppermute | solution.py:612
  90.7 2.2 %collective-permute-start.9 = (bf16[288,256]{1,0:T(8,128)(2,1)S(1)}, bf16[288,256]{1,0:T(8,128)(2,1)S(1)}, u32[]{:S(2)}, u32[]{:S(2)}) collective-permute-start(bf16[288,256]{1,0:T(8,128)(2,1)S(1)} %add_convert_fusion.1.low_ref), channel_id=1, source_target_pairs={{0,4},{1,5},{2,6},{3,7},{4,0},{5,1},{6,2},{7,3},{8,12},{9,13},{10,... | collective-permute-start | bytes 442376 | tf_op jit(solution)/shard_map/ppermute | solution.py:612
  92.9 0.8 copy-done.2
  93.7 3.8 %project.1.n0 = f32[72,256]{1,0:T(8,128)} custom-call(s32[2]{0:T(128)} %pad_add_fusion.me_ref, f32[8,2,32,256]{3,2,1,0:T(8,128)} %copy-done.2, bf16[2,256,256]{2,1,0:T(8,128)(2,1)} %constant.23.clone.tx_ref, bf16[2,256,256]{2,1,0:T(8,128)(2,1)} %constant.24.clone.ty_ref.back_ref, bf16[2,256,256]{2,1,0:T(8,128)(2,1)} %constant.24.clone.ty_ref.back_ref, ...), custom_call_target="tpu_custom_call" | custom-call | flops 2147483648 | bytes 4194304 | tf_op jit(solution)/shard_map/project/pallas_call | solution.py:753
  97.5 1.7 %collective-permute-start.11 = (f32[72,256]{1,0:T(8,128)}, f32[72,256]{1,0:T(8,128)S(1)}, u32[]{:S(2)}, u32[]{:S(2)}) collective-permute-start(f32[72,256]{1,0:T(8,128)} %project.1.n0), channel_id=1, source_target_pairs={{0,16},{8,24},{16,0},{24,8},{1,17},{9,25},{17,1},{25,9},{2,18},{10... | collective-permute-start | bytes 221192 | tf_op jit(solution)/shard_map/ppermute | solution.py:612
  99.4 2.7 %collective-permute-done.12.n3 = f32[72,256]{1,0:T(8,128)S(1)} collective-permute-done((f32[72,256]{1,0:T(8,128)}, f32[72,256]{1,0:T(8,128)S(1)}, u32[]{:S(2)}, u32[]{:S(2)}) %collective-permute-start.12) | collective-permute-done | bytes 73760 | tf_op jit(solution)/shard_map/ppermute | solution.py:612
  102.1 1.8 %collective-permute-done.11.n2 = f32[72,256]{1,0:T(8,128)S(1)} collective-permute-done((f32[72,256]{1,0:T(8,128)}, f32[72,256]{1,0:T(8,128)S(1)}, u32[]{:S(2)}, u32[]{:S(2)}) %collective-permute-start.11) | collective-permute-done | bytes 73760 | tf_op jit(solution)/shard_map/ppermute | solution.py:612
  105.2 2.1 %finish.1 = (f32[2,4,32,256]{3,2,1,0:T(8,128)}, f32[3,3,2,16]{3,2,1,0:T(2,128)}, f32[1,16]{1,0:T(1,128)}, f32[5,3,3,16,64]{4,3,2,1,0:T(8,128)}, f32[5,16]{1,0:T(...) custom-call(s32[2]{0:T(128)} %pad_add_fusion.me_ref, bf16[288,256]{1,0:T(8,128)(2,1)} %copy-done, ...), custom_call_target="tpu_custom_call" | custom-call | tf_op jit(solution)/shard_map/finish/pallas_call | solution.py:772
  (41 shorter events, 4.1 us)
Async XLA Ops:
  3.3 9.8 %collective-permute-start = (bf16[304,256]{1,0:T(8,128)(2,1)}, bf16[304,256]{1,0:T(8,128)(2,1)S(1)}, u32[]{:S(2)}, u32[]{:S(2)}) collective-permute-start(bf16[304,256]{1,0:T(8,128)(2,1)} %get-tuple-element.41.w0), channel_id=1, source_target_pairs={{0,16},{8,24},{16,0},{24,8},{1,17},{9,25},{17,1},{25,9},{2,18},{10... | collective-permute-start | bytes 466952 | tf_op jit(solution)/shard_map/ppermute | solution.py:612
  6.3 6.8 %collective-permute-start.1 = (f32[2,16,256]{2,1,0:T(8,128)}, f32[2,16,256]{2,1,0:T(8,128)S(1)}, u32[]{:S(2)}, u32[]{:S(2)}) collective-permute-start(f32[2,16,256]{2,1,0:T(8,128)} %get-tuple-element.42), channel_id=1, source_target_pairs={{0,1},{1,2},{2,3},{3,4},{4,5},{5,6},{6,7},{7,0},{8,9},{9,10},{10,1... | collective-permute-start | bytes 98312 | tf_op jit(solution)/shard_map/ppermute | solution.py:607
  7.8 5.3 %collective-permute-start.2 = (f32[2,16,256]{2,1,0:T(8,128)}, f32[2,16,256]{2,1,0:T(8,128)S(1)}, u32[]{:S(2)}, u32[]{:S(2)}) collective-permute-start(f32[2,16,256]{2,1,0:T(8,128)} %get-tuple-element.43), channel_id=1, source_target_pairs={{0,7},{1,0},{2,1},{3,2},{4,3},{5,4},{6,5},{7,6},{8,15},{9,8},{10,9... | collective-permute-start | bytes 98312 | tf_op jit(solution)/shard_map/ppermute | solution.py:607
  13.1 7.6 %copy-start.10 = (f32[2,16,256]{2,1,0:T(8,128)}, f32[2,16,256]{2,1,0:T(8,128)S(1)}, u32[]{:S(2)}) copy-start(f32[2,16,256]{2,1,0:T(8,128)S(1)} %collective-permute-done.1.up_ref) | copy-start | bytes 98308
  13.1 7.6 %copy-start.11 = (f32[2,16,256]{2,1,0:T(8,128)}, f32[2,16,256]{2,1,0:T(8,128)S(1)}, u32[]{:S(2)}) copy-start(f32[2,16,256]{2,1,0:T(8,128)S(1)} %collective-permute-done.2.down_ref) | copy-start | bytes 98308
  13.1 7.6 %copy-start.7 = (bf16[304,256]{1,0:T(8,128)(2,1)}, bf16[304,256]{1,0:T(8,128)(2,1)S(1)}, u32[]{:S(2)}) copy-start(bf16[304,256]{1,0:T(8,128)(2,1)S(1)} %collective-permute-done.w2) | copy-start | bytes 466948
  13.1 29.8 %all-to-all-start = ((f32[8,2,32,256]{3,2,1,0:T(8,128)}), f32[8,2,32,256]{3,2,1,0:T(8,128)S(1)}, u32[]{:S(2)}, u32[]{:S(2)}) async-start(f32[8,2,32,256]{3,2,1,0:T(8,128)} %get-tuple-element.45), calls=%async_computation | async-start | bytes 1048576 | tf_op jit(solution)/shard_map/all_to_all | solution.py:683
  19.1 1.6 %collective-permute-start.3 = (bf16[304,256]{1,0:T(8,128)(2,1)}, bf16[304,256]{1,0:T(8,128)(2,1)S(1)}, u32[]{:S(2)}, u32[]{:S(2)}) collective-permute-start(bf16[304,256]{1,0:T(8,128)(2,1)} %get-tuple-element.41.w0), channel_id=1, source_target_pairs={{0,8},{8,0},{16,24},{24,16},{1,9},{9,1},{17,25},{25,17},{2,10},{10... | collective-permute-start | bytes 466952 | tf_op jit(solution)/shard_map/ppermute | solution.py:612
  19.1 1.6 %collective-permute-start.4 = (bf16[304,256]{1,0:T(8,128)(2,1)S(1)}, bf16[304,256]{1,0:T(8,128)(2,1)S(1)}, u32[]{:S(2)}, u32[]{:S(2)}) collective-permute-start(bf16[304,256]{1,0:T(8,128)(2,1)S(1)} %collective-permute-done.w2), channel_id=1, source_target_pairs={{0,8},{8,0},{16,24},{24,16},{1,9},{9,1},{17,25},{25,17},{2,10},{10... | collective-permute-start | bytes 466952 | tf_op jit(solution)/shard_map/ppermute | solution.py:612
  20.7 0.7 copy-start.8
  20.7 0.7 copy-start.9
  42.9 0.8 copy-start.1
  65.0 1.9 %collective-permute-start.5 = (bf16[2,288,256]{2,1,0:T(8,128)(2,1)}, bf16[2,288,256]{2,1,0:T(8,128)(2,1)S(1)}, u32[]{:S(2)}, u32[]{:S(2)}) collective-permute-start(bf16[2,288,256]{2,1,0:T(8,128)(2,1)} %get-tuple-element.62), channel_id=1, source_target_pairs={{0,8},{8,0},{16,24},{24,16},{1,9},{9,1},{17,25},{25,17},{2,10},{10... | collective-permute-start | bytes 884744 | tf_op jit(solution)/shard_map/ppermute | solution.py:612
  67.9 6.6 %collective-permute-start.6 = (bf16[288,256]{1,0:T(8,128)(2,1)S(1)}, bf16[288,256]{1,0:T(8,128)(2,1)S(1)}, u32[]{:S(2)}, u32[]{:S(2)}) collective-permute-start(bf16[288,256]{1,0:T(8,128)(2,1)S(1)} %slice_bitcast_fusion), channel_id=1, source_target_pairs={{0,16},{8,24},{16,0},{24,8},{1,17},{9,25},{17,1},{25,9},{2,18},{10... | collective-permute-start | bytes 442376 | tf_op jit(solution)/shard_map/ppermute | solution.py:612
  68.4 24.5 %all-to-all-start.1 = ((f32[8,2,32,256]{3,2,1,0:T(8,128)}), f32[8,2,32,256]{3,2,1,0:T(8,128)S(1)}, u32[]{:S(2)}, u32[]{:S(2)}) async-start(f32[8,2,32,256]{3,2,1,0:T(8,128)} %get-tuple-element.63), calls=%async_computation.1 | async-start | bytes 1048576 | tf_op jit(solution)/shard_map/all_to_all | solution.py:722
  74.6 10.0 %collective-permute-start.7 = (bf16[288,256]{1,0:T(8,128)(2,1)S(1)}, bf16[288,256]{1,0:T(8,128)(2,1)S(1)}, u32[]{:S(2)}, u32[]{:S(2)}) collective-permute-start(bf16[288,256]{1,0:T(8,128)(2,1)S(1)} %fusion), channel_id=1, source_target_pairs={{0,1},{1,0},{2,3},{3,2},{4,5},{5,4},{6,7},{7,6},{8,9},{9,8},{10,11... | collective-permute-start | bytes 442376 | tf_op jit(solution)/shard_map/ppermute | solution.py:612
  84.7 6.0 %collective-permute-start.8 = (bf16[288,256]{1,0:T(8,128)(2,1)S(1)}, bf16[288,256]{1,0:T(8,128)(2,1)S(1)}, u32[]{:S(2)}, u32[]{:S(2)}) collective-permute-start(bf16[288,256]{1,0:T(8,128)(2,1)S(1)} %add_convert_fusion.2), channel_id=1, source_target_pairs={{0,2},{1,3},{2,0},{3,1},{4,6},{5,7},{6,4},{7,5},{8,10},{9,11},{10,... | collective-permute-start | bytes 442376 | tf_op jit(solution)/shard_map/ppermute | solution.py:612
  90.7 13.2 %copy-start = (bf16[288,256]{1,0:T(8,128)(2,1)}, bf16[288,256]{1,0:T(8,128)(2,1)S(1)}, u32[]{:S(2)}) copy-start(bf16[288,256]{1,0:T(8,128)(2,1)S(1)} %add_convert_fusion.1.low_ref) | copy-start | bytes 442372
  90.7 13.2 %collective-permute-start.9 = (bf16[288,256]{1,0:T(8,128)(2,1)S(1)}, bf16[288,256]{1,0:T(8,128)(2,1)S(1)}, u32[]{:S(2)}, u32[]{:S(2)}) collective-permute-start(bf16[288,256]{1,0:T(8,128)(2,1)S(1)} %add_convert_fusion.1.low_ref), channel_id=1, source_target_pairs={{0,4},{1,5},{2,6},{3,7},{4,0},{5,1},{6,2},{7,3},{8,12},{9,13},{10,... | collective-permute-start | bytes 442376 | tf_op jit(solution)/shard_map/ppermute | solution.py:612
  92.9 0.8 copy-start.2
  97.5 4.6 %collective-permute-start.12 = (f32[72,256]{1,0:T(8,128)}, f32[72,256]{1,0:T(8,128)S(1)}, u32[]{:S(2)}, u32[]{:S(2)}) collective-permute-start(f32[72,256]{1,0:T(8,128)} %project.1.n0), channel_id=1, source_target_pairs={{0,24},{8,16},{16,8},{24,0},{1,25},{9,17},{17,9},{25,1},{2,26},{10... | collective-permute-start | bytes 221192 | tf_op jit(solution)/shard_map/ppermute | solution.py:612
  97.5 6.4 %collective-permute-start.11 = (f32[72,256]{1,0:T(8,128)}, f32[72,256]{1,0:T(8,128)S(1)}, u32[]{:S(2)}, u32[]{:S(2)}) collective-permute-start(f32[72,256]{1,0:T(8,128)} %project.1.n0), channel_id=1, source_target_pairs={{0,16},{8,24},{16,0},{24,8},{1,17},{9,25},{17,1},{25,9},{2,18},{10... | collective-permute-start | bytes 221192 | tf_op jit(solution)/shard_map/ppermute | solution.py:612
  99.2 4.7 %collective-permute-start.10 = (f32[72,256]{1,0:T(8,128)}, f32[72,256]{1,0:T(8,128)S(1)}, u32[]{:S(2)}, u32[]{:S(2)}) collective-permute-start(f32[72,256]{1,0:T(8,128)} %project.1.n0), channel_id=1, source_target_pairs={{0,8},{8,0},{16,24},{24,16},{1,9},{9,1},{17,25},{25,17},{2,10},{10... | collective-permute-start | bytes 221192 | tf_op jit(solution)/shard_map/ppermute | solution.py:612
  102.1 1.8 %copy-start.4 = (f32[72,256]{1,0:T(8,128)}, f32[72,256]{1,0:T(8,128)S(1)}, u32[]{:S(2)}) copy-start(f32[72,256]{1,0:T(8,128)S(1)} %collective-permute-done.12.n3) | copy-start | bytes 221188
  (3 other events, 1.9 us)

commit v3 on v2

--- a/solution.py
+++ b/solution.py
@@ -87,10 +87,6 @@
     return dot(a[0], b[0]) + (dot(a[1], b[0]) + dot(a[0], b[1]))
 
 
-def both(ref):
-    return ref[0], ref[1]
-
-
 def spectrum(h, field_ref, tx_ref, ty_ref):
     ny = field_ref.shape[0] * h if h % 8 == 0 else field_ref.shape[0] // 2
     if h % 8 == 0:
@@ -98,8 +94,8 @@
         field = jnp.concatenate(fields, axis=0)
     else:
         field = field_ref[...]
-    along = product(halves(field), both(tx_ref))
-    table = both(ty_ref)
+    along = product(halves(field), halves(tx_ref[...]))
+    table = halves(ty_ref[...])
     if h % 8 == 0:
         return [product(table, halves(along[c * ny : (c + 1) * ny])) for c in range(2)]
     out = product(table, halves(along))
@@ -107,7 +103,7 @@
 
 
 def project_back(trow, u, back_ref):
-    back = both(back_ref)
+    back = halves(back_ref[...])
     return product(halves(product(trow, halves(u))), back)
 
 
@@ -176,10 +172,12 @@
     return count, -(-n // count)
 
 
-def forward_kernel(
+def step_kernel(
     h, me_ref, vel_ref, up_ref, down_ref, w0, w1, w2, w3, offs_ref,
-    prov_ref, vp_ref, vs_ref, face_ref, mix_ref, x_out, g_out, wk_ref, w7_ref, wf_ref, perm_ref, sq_ref,
-    xb, gb, w7k, f8, xsem, gsem,
+    cot_ref, tx_ref, ty_ref, back_ref, trow_ref, mxx_ref, myy_ref, mxy_ref,
+    prov_ref, vel_grad_ref, keep_ref, send_ref,
+    vp_ref, vs_ref, face_ref, mix_ref, xb, gb, wk_ref, w7_ref, wf_ref, w7k,
+    gz7, gz6, gz5, gz4, gz3, gz2, gz1, f8, adv_ref, acc_ref, gp_ref, near8,
 ):
     rows = h + 2 * HALO
     me = me_ref[0]
@@ -194,7 +192,6 @@
             w7k[j, at8, :] = block[0:8]
         wf_ref[at16, :] = piece[MIDROWS + 48 : MIDROWS + 64]
     perm = point_order(offs_ref[...])
-    perm_ref[...] = perm
     perm_low = perm.astype(bf16)
     for i in range(3):
         w7_ref[i] = jnp.dot(perm_low, w7k[i].astype(bf16), preferred_element_type=f32).astype(bf16)
@@ -209,16 +206,6 @@
 
     def vs_rows(y, n):
         return rows_of(vs_ref, (y + HALO) * 8, 8 * n)
-
-    def copies(l):
-        return (
-            pltpu.make_async_copy(xb.at[l, pl.ds(DEEP - 1, h + 2)], x_out.at[l], xsem.at[l]),
-            pltpu.make_async_copy(
-                gb.at[l, pl.ds(DEEP - l - 1, h + 2 * (l + 1))],
-                g_out.at[l, pl.ds(0, h + 2 * (l + 1))],
-                gsem.at[l],
-            ),
-        )
 
     wfirst = wf_ref[:, 0:24]
     bias = jnp.broadcast_to(wf_ref[:, 24:25].astype(f32), (C, KW))
@@ -237,9 +224,6 @@
         return 0
 
     lax.fori_loop(0, count, first_block, 0)
-    for copy in copies(0):
-        copy.start()
-
     for l in range(1, NL + 1):
         weight = wk_ref[3 * (l - 1) : 3 * l].reshape(192, KW)
         bias = jnp.broadcast_to(weight[0:C, 192:193].astype(f32), (C, KW))
@@ -261,8 +245,6 @@
             return 0
 
         lax.fori_loop(0, count, block, 0)
-        for copy in copies(l):
-            copy.start()
 
     weight = w7_ref[...].reshape(96, KW)
     bias = jnp.broadcast_to(weight[0:32, 192:193].astype(f32), (32, KW))
@@ -314,41 +296,14 @@
         own = own + jnp.sum(q * q)
         update = update + jnp.sum((new - q) * (new - q))
     lane = lax.broadcasted_iota(jnp.int32, (8, KW), 1)
-    sq_ref[...] = jnp.where(
+    squares = jnp.where(
         lane == 0, own, jnp.where(lane == 1, total[0], jnp.where(lane == 2, update, 0.0))
     )
-    for l in range(NL + 1):
-        for copy in copies(l):
-            copy.wait()
-
-
-def backward_kernel(
-    h, me_ref, cot_ref, tx_ref, ty_ref, back_ref, trow_ref, mxx_ref, myy_ref, mxy_ref,
-    vp_ref, vs_ref, face_ref, mix_ref, x_in, g_in, wk_ref, w7_ref, wf_ref, perm_ref, sq_ref,
-    vel_grad_ref, keep_ref, send_ref,
-    xb, gb, gz7, gz6, gz5, gz4, gz3, gz2, gz1, f8, adv_ref, acc_ref, gp_ref, near8, xsem, gsem,
-):
-    me_chan = me_ref[0]
-    me_space = me_ref[1]
-
-    def copies(l):
-        return (
-            pltpu.make_async_copy(x_in.at[l], xb.at[l], xsem.at[l]),
-            pltpu.make_async_copy(
-                g_in.at[l, pl.ds(0, h + 2 * (l + 1))],
-                gb.at[l, pl.ds(0, h + 2 * (l + 1))],
-                gsem.at[l],
-            ),
-        )
-
-    for l in range(NL, -1, -1):
-        for copy in copies(l):
-            copy.start()
 
     n = h + 2 * GPH
     u, v = spectrum(h, cot_ref, tx_ref, ty_ref)
     u, v = project_spectral(u, v, mxx_ref[...], myy_ref[...], mxy_ref[...])
-    trow = (trow_ref[0, me_space], trow_ref[1, me_space])
+    trow = halves(trow_ref[me_ref[1]])
     gp_ref[0] = project_back(trow, u, back_ref)
     gp_ref[1] = project_back(trow, v, back_ref)
 
@@ -386,9 +341,6 @@
     def f8_row(y):
         return rows_of(f8, (y + GPH) * 8, 8)
 
-    def vs_rows(y, count):
-        return rows_of(vs_ref, (y + HALO) * 8, 8 * count)
-
     def stencil_row(k, _):
         for r in range(2):
             y = 2 * k + r - 7
@@ -414,10 +366,7 @@
 
     gzs = {7: gz7, 6: gz6, 5: gz5, 4: gz4, 3: gz3, 2: gz2, 1: gz1}
     for l in range(7, 1, -1):
-        for copy in copies(l - 2):
-            copy.wait()
         source, target = gzs[l], gzs[l - 1]
-        xs, gs = xb.at[l - 2], gb.at[l - 2]
         if l == 7:
             parts = [w7_ref[i][:, 0:192].astype(f32) for i in range(3)]
             width = 32
@@ -439,20 +388,22 @@
                 o = jnp.dot(weight, columns[y], preferred_element_type=f32)
                 if y >= 2 - l:
                     ga = p1 + o[0:64]
-                    target[y - 1 + l - 1] = (ga * gs[y - 1 + l - 1].astype(f32)).astype(bf16)
+                    target[y - 1 + l - 1] = (ga * gb[l - 2, y - 1 + DEEP].astype(f32)).astype(bf16)
                 p1 = o[64:128] if p0 is None else p0 + o[64:128]
                 p0 = o[128:192]
             own = [y for y in ys if 0 <= y < h]
             part = wgrad(
                 [columns[y] for y in own],
                 [
-                    jnp.concatenate([xs[y : y + 3].reshape(192, KW), ones], axis=0)
+                    jnp.concatenate(
+                        [xb[l - 2, y + DEEP - 1 : y + DEEP + 2].reshape(192, KW), ones], axis=0
+                    )
                     for y in own
                 ],
             )
             acc = part if acc is None else acc + part
         if l == 7:
-            back = perm_ref[...]
+            back = perm
             acc = jnp.concatenate(
                 [
                     lax.dot_general(
@@ -492,7 +443,7 @@
         vel_grad_ref[c] = total
 
     for k, other in enumerate((0, 2, 1, 3)):
-        slot = jnp.bitwise_xor(me_chan, other)
+        slot = jnp.bitwise_xor(me, other)
         pack_ref = (keep_ref, send_ref)[k // 2]
         k = k % 2
         for l in range(NL):
@@ -503,7 +454,7 @@
             acc_ref[6, pl.ds(pl.multiple_of(j * 32 + slot * 8, 8), 8), :] for j in range(3)
         ]
         pack_ref[k, MIDROWS : MIDROWS + 32, :] = jnp.concatenate(
-            last + [sq_ref[...]], axis=0
+            last + [squares], axis=0
         ).astype(bf16)
         pack_ref[k, MIDROWS + 32 : MIDROWS + 48, :] = acc_ref[
             0, pl.ds(pl.multiple_of(slot * 16, 16), 16), :
@@ -512,7 +463,7 @@
 
 def project_kernel(h, me_ref, prov_ref, tx_ref, ty_ref, back_ref, trow_ref, mxx_ref, myy_ref, mxy_ref, out_ref):
     me_space = me_ref[1]
-    trow = tuple(trow_ref[k, me_space][GPH : GPH + h] for k in range(2))
+    trow = halves(trow_ref[me_space][GPH : GPH + h])
     u, v = spectrum(h, prov_ref, tx_ref, ty_ref)
     u, v = project_spectral(u, v, mxx_ref[...], myy_ref[...], mxy_ref[...])
     out_ref[0:h] = project_back(trow, u, back_ref)
@@ -626,10 +577,8 @@
     ny = h * space
     ty, tx = basis(ny), basis(nx)
 
-    def two(table):
-        high = table.astype(np.float32).astype(jnp.bfloat16)
-        low = (table - high.astype(np.float64)).astype(np.float32).astype(jnp.bfloat16)
-        return jnp.asarray(np.stack([high, low]))
+    def held(table):
+        return jnp.asarray(np.ascontiguousarray(table).astype(np.float32))
 
     back_y = ty.T
     if h % 8:
@@ -639,7 +588,7 @@
         back_y = wide.reshape(2 * ny, 2 * ny)
     ring = (np.arange(space)[:, None] * h + np.arange(h + 2 * GPH)[None, :] - GPH) % ny
     spectral = [jnp.asarray(m.astype(np.float32)) for m in multipliers(ny, nx)]
-    return [two(tx), two(back_y), two(tx.T), two(ty[ring])] + spectral
+    return [held(tx), held(back_y), held(tx.T), held(ty[ring])] + spectral
 
 
 def vmem(count):
@@ -656,106 +605,92 @@
     rows = h + 2 * HALO
     shape = jax.ShapeDtypeStruct
     smem = pl.BlockSpec(memory_space=pltpu.SMEM)
-    limit = pltpu.CompilerParams(vmem_limit_bytes=56 * 2**20)
+    inside = pltpu.VMEM
+
+    def limit(mebibytes):
+        return pltpu.CompilerParams(vmem_limit_bytes=mebibytes * 2**20)
+
+    def outside(x):
+        return pltpu.with_memory_space_constraint(x, pltpu.HBM)
+
     packed, own, top, bottom, cot_all = pl.pallas_call(
         functools.partial(prepare_kernel, h),
         out_shape=[
-            shape((MIDROWS + 64, KW), bf16),
-            shape((2, h, nx), f32),
-            shape((2, min(h, HALO), nx), f32),
-            shape((2, min(h, HALO), nx), f32),
-            shape((space, 2, h, nx), f32),
+            inside((MIDROWS + 64, KW), bf16),
+            inside((2, h, nx), f32),
+            inside((2, min(h, HALO), nx), f32),
+            inside((2, min(h, HALO), nx), f32),
+            inside((space, 2, h, nx), f32),
         ],
         in_specs=[smem] + vmem(8),
         out_specs=vmem(5),
         scratch_shapes=[pltpu.VMEM((128, 128), f32), pltpu.VMEM((8, 128), f32)],
-        compiler_params=limit,
+        compiler_params=limit(16),
         name="prepare",
     )(
-        me, velocity, cotangent, jnp.swapaxes(w_mid, 3, 4), jnp.swapaxes(w_last, 2, 3), w_first,
-        b_mid, b_first[None], b_last[None],
+        me,
+        *[
+            outside(x)
+            for x in (
+                velocity, cotangent, jnp.swapaxes(w_mid, 3, 4), jnp.swapaxes(w_last, 2, 3),
+                w_first, b_mid, b_first[None], b_last[None],
+            )
+        ],
     )
     across = swapped(packed, "chan", 2)
     up, down = halos(own, top, bottom, HALO)
-    across, up, down, cot_all = lax.optimization_barrier((across, up, down, cot_all))
+    across, up, down = lax.optimization_barrier((across, up, down))
     beside = swapped(packed, "chan", 1)
     diagonal = swapped(across, "chan", 1)
     cot_full = lax.all_to_all(cot_all, "space", 0, 0, tiled=True)
     if h % 8:
         cot_full = cot_full.reshape(space * 2 * h, nx)
 
-    any_space = pl.BlockSpec(memory_space=pl.ANY)
     deep = h + 2 * DEEP
-    prov, vp, vs, face, mix, x_all, g_all, wk, w7, wf, perm, squares = pl.pallas_call(
-        functools.partial(forward_kernel, h),
-        out_shape=[
-            shape((space, 2, h, nx), f32),
-            shape((2, rows, nx), f32),
-            shape((nx // 128, rows * 8, 128), f32),
-            shape((2, h + 4, nx), f32),
-            shape(((h + 4) * 32, nx), f32),
-            shape((NL + 1, h + 2, C, nx), bf16),
-            shape((NL + 1, h + 2 * (NL + 1), C, nx), bf16),
-            shape((NL * 3, C, KW), bf16),
-            shape((3, 32, KW), bf16),
-            shape((C, KW), bf16),
-            shape((32, 32), f32),
-            shape((8, KW), f32),
+    constants = [outside(x) for x in tables(h, space, nx)]
+    prov, vel_grad, keep, send = pl.pallas_call(
+        functools.partial(step_kernel, h),
+        out_shape=[inside((space, 2, h, nx), f32), shape((2, h, nx), f32)]
+        + [inside((2, MIDROWS + 48, KW), bf16)] * 2,
+        in_specs=[smem] + vmem(16),
+        out_specs=vmem(4),
+        scratch_shapes=[
+            inside((2, rows, nx), f32),
+            inside((nx // 128, rows * 8, 128), f32),
+            inside((2, h + 4, nx), f32),
+            inside(((h + 4) * 32, nx), f32),
+            inside((NL + 1, deep, C, nx), bf16),
+            inside((NL + 1, deep, C, nx), bf16),
+            inside((NL * 3, C, KW), bf16),
+            inside((3, 32, KW), bf16),
+            inside((C, KW), bf16),
+            inside((3, 32, KW), f32),
+            inside((h + 14, 32, nx), bf16),
+        ]
+        + [inside((h + 2 * l, C, nx), bf16) for l in range(6, 0, -1)]
+        + [
+            inside((nx // 128, (h + 2 * GPH) * 8, 128), f32),
+            inside((2, h + 2 * GPH, nx), f32),
+            inside((7, 192, KW), f32),
+            inside((2, h + 2 * GPH, nx), f32),
+            inside((nx // 128, h * 8, 128), f32),
         ],
-        in_specs=[smem] + vmem(8),
-        out_specs=vmem(5) + [any_space, any_space] + vmem(5),
-        scratch_shapes=[
-            pltpu.VMEM((NL + 1, deep, C, nx), bf16),
-            pltpu.VMEM((NL + 1, deep, C, nx), bf16),
-            pltpu.VMEM((3, 32, KW), f32),
-            pltpu.VMEM((nx // 128, (h + 4) * 8, 128), f32),
-            pltpu.SemaphoreType.DMA((NL + 1,)),
-            pltpu.SemaphoreType.DMA((NL + 1,)),
-        ],
-        compiler_params=limit,
+        compiler_params=limit(52),
         cost_estimate=pl.CostEstimate(
-            flops=2 * 7 * deep * nx * 9 * C * C, bytes_accessed=2**25, transcendentals=6 * deep * nx * C
+            flops=6 * 7 * deep * nx * 9 * C * C, bytes_accessed=2**25, transcendentals=6 * deep * nx * C
         ),
-        name="forward",
-    )(me, own, up, down, packed, beside, across, diagonal, offsets)
-
+        name="step",
+    )(me, own, up, down, packed, beside, across, diagonal, outside(offsets), cot_full, *constants)
     everywhere = lax.all_to_all(prov, "space", 0, 0, tiled=True)
     if h % 8:
         everywhere = everywhere.reshape(space * 2 * h, nx)
-    constants = tables(h, space, nx)
-    vel_grad, keep, send = pl.pallas_call(
-        functools.partial(backward_kernel, h),
-        out_shape=[shape((2, h, nx), f32)] + [shape((2, MIDROWS + 48, KW), bf16)] * 2,
-        in_specs=[smem] + vmem(12) + [any_space, any_space] + vmem(5),
-        out_specs=vmem(3),
-        scratch_shapes=[
-            pltpu.VMEM((NL + 1, h + 2, C, nx), bf16),
-            pltpu.VMEM((NL + 1, h + 2 * (NL + 1), C, nx), bf16),
-            pltpu.VMEM((h + 14, 32, nx), bf16),
-        ]
-        + [pltpu.VMEM((h + 2 * l, C, nx), bf16) for l in range(6, 0, -1)]
-        + [
-            pltpu.VMEM((nx // 128, (h + 2 * GPH) * 8, 128), f32),
-            pltpu.VMEM((2, h + 2 * GPH, nx), f32),
-            pltpu.VMEM((7, 192, KW), f32),
-            pltpu.VMEM((2, h + 2 * GPH, nx), f32),
-            pltpu.VMEM((nx // 128, h * 8, 128), f32),
-            pltpu.SemaphoreType.DMA((NL + 1,)),
-            pltpu.SemaphoreType.DMA((NL + 1,)),
-        ],
-        compiler_params=limit,
-        cost_estimate=pl.CostEstimate(
-            flops=4 * 7 * deep * nx * 9 * C * C, bytes_accessed=2**25, transcendentals=0
-        ),
-        name="backward",
-    )(me, cot_full, *constants, vp, vs, face, mix, x_all, g_all, wk, w7, wf, perm, squares)
 
     new_own = pl.pallas_call(
         functools.partial(project_kernel, h),
-        out_shape=shape((2 * h + 8, nx), f32),
+        out_shape=inside((2 * h + 8, nx), f32),
         in_specs=[smem] + vmem(8),
         out_specs=vmem(1)[0],
-        compiler_params=limit,
+        compiler_params=limit(16),
         cost_estimate=pl.CostEstimate(flops=2**31, bytes_accessed=2**22, transcendentals=0),
         name="project",
     )(me, everywhere, *constants)
@@ -784,7 +719,7 @@
         in_specs=[smem] + vmem(6),
         out_specs=vmem(8),
         scratch_shapes=[pltpu.VMEM((4, 8, KW), f32)],
-        compiler_params=limit,
+        compiler_params=limit(16),
         name="finish",
     )(me, low, other, *news)
     return (

time: 108 us -> 97.2 us (0.900)
  Pallas kernels: 50.8 us -> 41.9 us
  waiting for transfers between devices: 21.3 us -> 26.9 us
  starting transfers between devices: 29.1 us -> 26.3 us
  local copies, waits for them, and re-layouts: 3.6 us -> 0.8 us
  other arithmetic: 1.74 us -> 0.26 us
    pallas_call x4 -> x3, Pallas kernels: 48.7 us -> 40.3 us  [the longest x1 35.3 us: per_device(): pl.pallas_call(functools.partial(step_kernel, h), out_shape=[inside((spac...]
    ppermute x2, waiting for transfers between devices: 2.1 us -> 8.06 us  [moved(): return lax.ppermute(x, axis, [(i, (i + step) % n) for i in range(n)])]
    unnamed x24 -> x2, local copies, waits for them, and re-layouts: 3.59 us -> 0.79 us
    all_to_all x1, starting transfers between devices: 6.19 us -> 3.66 us  [per_device(): everywhere = lax.all_to_all(prov, 'space', 0, 0, tiled=True)]
    ppermute x11, starting transfers between devices: 12.2 us -> 10.6 us  [swapped(): return lax.ppermute(x, axis, [(i, i ^ bit) for i in range(n)])]
    all_to_all x1, starting transfers between devices: 5.99 us -> 7.28 us  [per_device(): cot_full = lax.all_to_all(cot_all, 'space', 0, 0, tiled=True)]
  transfers between devices with their start and end apart: 15 -> 15, of which waited for: 7 -> 9; matrix products, arithmetic and copies ran while one was open for 0% -> 0% of each run, Pallas kernels for 24% -> 3%
where the time goes in v3:
time: 97.2 us; the launch traced here: 96.8 us
  Pallas kernels  41.9 us (43%)
  waiting for transfers between devices  26.9 us (28%)
  starting transfers between devices  26.3 us (27%)
    pallas_call x1, Pallas kernels, per_device(): pl.pallas_call(functools.partial(step_kernel, h), out_shape=[inside((spac...  35.3 us
    ppermute x11, waiting for transfers between devices, swapped(): return lax.ppermute(x, axis, [(i, i ^ bit) for i in range(n)])  18.8 us
    ppermute x11, starting transfers between devices, swapped(): return lax.ppermute(x, axis, [(i, i ^ bit) for i in range(n)])  10.6 us
    ppermute x2, waiting for transfers between devices, moved(): return lax.ppermute(x, axis, [(i, (i + step) % n) for i in range(n)])  8.06 us
    all_to_all x1, starting transfers between devices, per_device(): cot_full = lax.all_to_all(cot_all, 'space', 0, 0, tiled=True)  7.28 us
    ppermute x2, starting transfers between devices, moved(): return lax.ppermute(x, axis, [(i, (i + step) % n) for i in range(n)])  4.72 us
    all_to_all x1, starting transfers between devices, per_device(): everywhere = lax.all_to_all(prov, 'space', 0, 0, tiled=True)  3.66 us
    pallas_call x1, Pallas kernels, per_device(): pl.pallas_call(functools.partial(project_kernel, h), out_shape=inside((2...  3.02 us
  transfers between devices with their start and end apart: 15, of which 9 were waited for; matrix products, arithmetic and copies ran while one was open for 0% of the time, Pallas kernels for 3%

profile of v3, /device:TPU:0, one launch (start us, length us, event | category | flops | bytes accessed | tf_op | source)
XLA Modules:
  0.0 96.8 jit_solution(11140021784368786344)
XLA Ops:
  0.7 2.1 %prepare.1 = (bf16[304,256]{1,0:T(8,128)(2,1)S(1)}, f32[2,32,256]{2,1,0:T(8,128)S(1)}, f32[2,16,256]{2,1,0:T(8,128)S(1)}, f32[2,16,256]{2,1,0:T(8,128)S(1)}, f32[8,2,32,256]{3,2,1,0:T(8,128)}) custom-call(s32[2]{0:T(128)S(1)} %pad_add_fusion.me_ref, f32[2,4,32,256]{3,2,1,0:T(8,128)} %vel_ref.1, f32[2,4,32,256]{3,2,1,0:T(8,128)} %cot_ref.1, ...), custom_call_target="tpu_custom_call" | custom-call | tf_op jit(solution)/shard_map/prepare/pallas_call | solution.py:616
  2.8 7.3 %all-to-all-start = ((f32[8,2,32,256]{3,2,1,0:T(8,128)}), f32[8,2,32,256]{3,2,1,0:T(8,128)S(1)}, u32[]{:S(2)}, u32[]{:S(2)}) async-start(f32[8,2,32,256]{3,2,1,0:T(8,128)} %get-tuple-element.36), calls=%async_computation | async-start | bytes 1048576 | tf_op jit(solution)/shard_map/all_to_all | solution.py:645
  10.1 1.5 %collective-permute-start = (bf16[304,256]{1,0:T(8,128)(2,1)S(1)}, bf16[304,256]{1,0:T(8,128)(2,1)S(1)}, u32[]{:S(2)}, u32[]{:S(2)}) collective-permute-start(bf16[304,256]{1,0:T(8,128)(2,1)S(1)} %get-tuple-element.30.w0), channel_id=1, source_target_pairs={{0,16},{8,24},{16,0},{24,8},{1,17},{9,25},{17,1},{25,9},{2,18},{10... | collective-permute-start | bytes 466952 | tf_op jit(solution)/shard_map/ppermute | solution.py:563
  11.6 2.0 %collective-permute-start.1 = (f32[2,16,256]{2,1,0:T(8,128)S(1)}, f32[2,16,256]{2,1,0:T(8,128)S(1)}, u32[]{:S(2)}, u32[]{:S(2)}) collective-permute-start(f32[2,16,256]{2,1,0:T(8,128)S(1)} %get-tuple-element.31), channel_id=1, source_target_pairs={{0,1},{1,2},{2,3},{3,4},{4,5},{5,6},{6,7},{7,0},{8,9},{9,10},{10,1... | collective-permute-start | bytes 98312 | tf_op jit(solution)/shard_map/ppermute | solution.py:558
  13.6 2.7 %collective-permute-start.2 = (f32[2,16,256]{2,1,0:T(8,128)S(1)}, f32[2,16,256]{2,1,0:T(8,128)S(1)}, u32[]{:S(2)}, u32[]{:S(2)}) collective-permute-start(f32[2,16,256]{2,1,0:T(8,128)S(1)} %get-tuple-element.32), channel_id=1, source_target_pairs={{0,7},{1,0},{2,1},{3,2},{4,3},{5,4},{6,5},{7,6},{8,15},{9,8},{10,9... | collective-permute-start | bytes 98312 | tf_op jit(solution)/shard_map/ppermute | solution.py:558
  16.3 8.1 %collective-permute-done.1.up_ref = f32[2,16,256]{2,1,0:T(8,128)S(1)} collective-permute-done((f32[2,16,256]{2,1,0:T(8,128)S(1)}, f32[2,16,256]{2,1,0:T(8,128)S(1)}, u32[]{:S(2)}, u32[]{:S(2)}) %collective-permute-start.1) | collective-permute-done | bytes 32800 | tf_op jit(solution)/shard_map/ppermute | solution.py:558
  24.4 1.4 %collective-permute-done.4.w3 = bf16[304,256]{1,0:T(8,128)(2,1)S(1)} collective-permute-done((bf16[304,256]{1,0:T(8,128)(2,1)S(1)}, bf16[304,256]{1,0:T(8,128)(2,1)S(1)}, u32[]{:S(2)}, u32[]{:S(2)}) %collective-permute-start.4) | collective-permute-done | bytes 155680 | tf_op jit(solution)/shard_map/ppermute | solution.py:563
  25.7 0.8 copy-done
  26.5 35.3 %step.1 = (f32[8,2,32,256]{3,2,1,0:T(8,128)}, f32[2,32,256]{2,1,0:T(8,128)}, bf16[2,288,256]{2,1,0:T(8,128)(2,1)S(1)}, bf16[2,288,256]{2,1,0:T(8,128)(2,1)S(1)}) custom-call(s32[2]{0:T(128)S(1)} %pad_add_fusion.me_ref, f32[2,32,256]{2,1,0:T(8,128)S(1)} %get-tuple-element.29.vel_ref, f32[2,16,256]{2,1,0:T(8,128)S(1)} %collective-permute-done.1.up_ref, ...), custom_call_target="tpu_custom_call" | custom-call | flops 22196256768 | bytes 33554432 | tf_op jit(solution)/shard_map/step/pallas_call | solution.py:651
  61.9 1.4 %collective-permute-done.5 = bf16[2,288,256]{2,1,0:T(8,128)(2,1)S(1)} collective-permute-done((bf16[2,288,256]{2,1,0:T(8,128)(2,1)S(1)}, bf16[2,288,256]{2,1,0:T(8,128)(2,1)S(1)}, u32[]{:S(2)}, u32[]{:S(2)}) %collective-permute-start.5) | collective-permute-done | bytes 294944 | tf_op jit(solution)/shard_map/ppermute | solution.py:563
  63.5 1.6 %collective-permute-start.6 = (bf16[288,256]{1,0:T(8,128)(2,1)S(1)}, bf16[288,256]{1,0:T(8,128)(2,1)S(1)}, u32[]{:S(2)}, u32[]{:S(2)}) collective-permute-start(bf16[288,256]{1,0:T(8,128)(2,1)S(1)} %slice_bitcast_fusion), channel_id=1, source_target_pairs={{0,16},{8,24},{16,0},{24,8},{1,17},{9,25},{17,1},{25,9},{2,18},{10... | collective-permute-start | bytes 442376 | tf_op jit(solution)/shard_map/ppermute | solution.py:563
  65.0 3.7 %all-to-all-start.1 = ((f32[8,2,32,256]{3,2,1,0:T(8,128)}), f32[8,2,32,256]{3,2,1,0:T(8,128)S(1)}, u32[]{:S(2)}, u32[]{:S(2)}) async-start(f32[8,2,32,256]{3,2,1,0:T(8,128)} %get-tuple-element.39), calls=%async_computation.1 | async-start | bytes 1048576 | tf_op jit(solution)/shard_map/all_to_all | solution.py:684
  68.7 0.8 collective-permute-done.6
  69.5 1.3 %collective-permute-start.7 = (bf16[288,256]{1,0:T(8,128)(2,1)S(1)}, bf16[288,256]{1,0:T(8,128)(2,1)S(1)}, u32[]{:S(2)}, u32[]{:S(2)}) collective-permute-start(bf16[288,256]{1,0:T(8,128)(2,1)S(1)} %fusion), channel_id=1, source_target_pairs={{0,1},{1,0},{2,3},{3,2},{4,5},{5,4},{6,7},{7,6},{8,9},{9,8},{10,11... | collective-permute-start | bytes 442376 | tf_op jit(solution)/shard_map/ppermute | solution.py:563
  70.8 7.9 %collective-permute-done.7 = bf16[288,256]{1,0:T(8,128)(2,1)S(1)} collective-permute-done((bf16[288,256]{1,0:T(8,128)(2,1)S(1)}, bf16[288,256]{1,0:T(8,128)(2,1)S(1)}, u32[]{:S(2)}, u32[]{:S(2)}) %collective-permute-start.7) | collective-permute-done | bytes 147488 | tf_op jit(solution)/shard_map/ppermute | solution.py:563
  78.7 2.0 %collective-permute-start.8 = (bf16[288,256]{1,0:T(8,128)(2,1)S(1)}, bf16[288,256]{1,0:T(8,128)(2,1)S(1)}, u32[]{:S(2)}, u32[]{:S(2)}) collective-permute-start(bf16[288,256]{1,0:T(8,128)(2,1)S(1)} %add_convert_fusion.2), channel_id=1, source_target_pairs={{0,2},{1,3},{2,0},{3,1},{4,6},{5,7},{6,4},{7,5},{8,10},{9,11},{10,... | collective-permute-start | bytes 442376 | tf_op jit(solution)/shard_map/ppermute | solution.py:563
  80.7 4.1 %collective-permute-done.8 = bf16[288,256]{1,0:T(8,128)(2,1)S(1)} collective-permute-done((bf16[288,256]{1,0:T(8,128)(2,1)S(1)}, bf16[288,256]{1,0:T(8,128)(2,1)S(1)}, u32[]{:S(2)}, u32[]{:S(2)}) %collective-permute-start.8) | collective-permute-done | bytes 147488 | tf_op jit(solution)/shard_map/ppermute | solution.py:563
  84.9 2.2 %collective-permute-start.9 = (bf16[288,256]{1,0:T(8,128)(2,1)S(1)}, bf16[288,256]{1,0:T(8,128)(2,1)S(1)}, u32[]{:S(2)}, u32[]{:S(2)}) collective-permute-start(bf16[288,256]{1,0:T(8,128)(2,1)S(1)} %add_convert_fusion.1.low_ref), channel_id=1, source_target_pairs={{0,4},{1,5},{2,6},{3,7},{4,0},{5,1},{6,2},{7,3},{8,12},{9,13},{10,... | collective-permute-start | bytes 442376 | tf_op jit(solution)/shard_map/ppermute | solution.py:563
  87.1 3.0 %project.1.n0 = f32[72,256]{1,0:T(8,128)S(1)} custom-call(s32[2]{0:T(128)S(1)} %pad_add_fusion.me_ref, f32[8,2,32,256]{3,2,1,0:T(8,128)S(1)} %all-to-all-done.1.prov_ref, f32[256,256]{1,0:T(8,128)} %constant.23.clone.tx_ref, f32[256,256]{1,0:T(8,128)} %constant.24.clone.ty_ref.back_ref, f32[256,256]{1,0:T(8,128)} %constant.24.clone.ty_ref.back_ref, ...), custom_call_target="tpu_custom_call" | custom-call | flops 2147483648 | bytes 4194304 | tf_op jit(solution)/shard_map/project/pallas_call | solution.py:688
  90.1 0.6 collective-permute-start.11
  90.7 1.3 %collective-permute-start.10 = (f32[72,256]{1,0:T(8,128)S(1)}, f32[72,256]{1,0:T(8,128)S(1)}, u32[]{:S(2)}, u32[]{:S(2)}) collective-permute-start(f32[72,256]{1,0:T(8,128)S(1)} %project.1.n0), channel_id=1, source_target_pairs={{0,8},{8,0},{16,24},{24,16},{1,9},{9,1},{17,25},{25,17},{2,10},{10... | collective-permute-start | bytes 221192 | tf_op jit(solution)/shard_map/ppermute | solution.py:563
  92.6 1.5 %collective-permute-done.12.n3 = f32[72,256]{1,0:T(8,128)S(1)} collective-permute-done((f32[72,256]{1,0:T(8,128)S(1)}, f32[72,256]{1,0:T(8,128)S(1)}, u32[]{:S(2)}, u32[]{:S(2)}) %collective-permute-start.12) | collective-permute-done | bytes 73760 | tf_op jit(solution)/shard_map/ppermute | solution.py:563
  94.1 1.2 %collective-permute-done.11.n2 = f32[72,256]{1,0:T(8,128)S(1)} collective-permute-done((f32[72,256]{1,0:T(8,128)S(1)}, f32[72,256]{1,0:T(8,128)S(1)}, u32[]{:S(2)}, u32[]{:S(2)}) %collective-permute-start.11) | collective-permute-done | bytes 73760 | tf_op jit(solution)/shard_map/ppermute | solution.py:563
  95.3 1.5 %finish.1 = (f32[2,4,32,256]{3,2,1,0:T(8,128)}, f32[3,3,2,16]{3,2,1,0:T(2,128)}, f32[1,16]{1,0:T(1,128)}, f32[5,3,3,16,64]{4,3,2,1,0:T(8,128)}, f32[5,16]{1,0:T(...) custom-call(s32[2]{0:T(128)S(1)} %pad_add_fusion.me_ref, ...), custom_call_target="tpu_custom_call" | custom-call | tf_op jit(solution)/shard_map/finish/pallas_call | solution.py:707
  (18 shorter events, 1.0 us)
Async XLA Ops:
  2.8 22.9 %all-to-all-start = ((f32[8,2,32,256]{3,2,1,0:T(8,128)}), f32[8,2,32,256]{3,2,1,0:T(8,128)S(1)}, u32[]{:S(2)}, u32[]{:S(2)}) async-start(f32[8,2,32,256]{3,2,1,0:T(8,128)} %get-tuple-element.36), calls=%async_computation | async-start | bytes 1048576 | tf_op jit(solution)/shard_map/all_to_all | solution.py:645
  10.1 14.3 %collective-permute-start = (bf16[304,256]{1,0:T(8,128)(2,1)S(1)}, bf16[304,256]{1,0:T(8,128)(2,1)S(1)}, u32[]{:S(2)}, u32[]{:S(2)}) collective-permute-start(bf16[304,256]{1,0:T(8,128)(2,1)S(1)} %get-tuple-element.30.w0), channel_id=1, source_target_pairs={{0,16},{8,24},{16,0},{24,8},{1,17},{9,25},{17,1},{25,9},{2,18},{10... | collective-permute-start | bytes 466952 | tf_op jit(solution)/shard_map/ppermute | solution.py:563
  11.6 12.8 %collective-permute-start.1 = (f32[2,16,256]{2,1,0:T(8,128)S(1)}, f32[2,16,256]{2,1,0:T(8,128)S(1)}, u32[]{:S(2)}, u32[]{:S(2)}) collective-permute-start(f32[2,16,256]{2,1,0:T(8,128)S(1)} %get-tuple-element.31), channel_id=1, source_target_pairs={{0,1},{1,2},{2,3},{3,4},{4,5},{5,6},{6,7},{7,0},{8,9},{9,10},{10,1... | collective-permute-start | bytes 98312 | tf_op jit(solution)/shard_map/ppermute | solution.py:558
  13.6 10.8 %collective-permute-start.2 = (f32[2,16,256]{2,1,0:T(8,128)S(1)}, f32[2,16,256]{2,1,0:T(8,128)S(1)}, u32[]{:S(2)}, u32[]{:S(2)}) collective-permute-start(f32[2,16,256]{2,1,0:T(8,128)S(1)} %get-tuple-element.32), channel_id=1, source_target_pairs={{0,7},{1,0},{2,1},{3,2},{4,3},{5,4},{6,5},{7,6},{8,15},{9,8},{10,9... | collective-permute-start | bytes 98312 | tf_op jit(solution)/shard_map/ppermute | solution.py:558
  16.3 8.1 %collective-permute-start.3 = (bf16[304,256]{1,0:T(8,128)(2,1)S(1)}, bf16[304,256]{1,0:T(8,128)(2,1)S(1)}, u32[]{:S(2)}, u32[]{:S(2)}) collective-permute-start(bf16[304,256]{1,0:T(8,128)(2,1)S(1)} %get-tuple-element.30.w0), channel_id=1, source_target_pairs={{0,8},{8,0},{16,24},{24,16},{1,9},{9,1},{17,25},{25,17},{2,10},{10... | collective-permute-start | bytes 466952 | tf_op jit(solution)/shard_map/ppermute | solution.py:563
  24.4 1.4 %collective-permute-start.4 = (bf16[304,256]{1,0:T(8,128)(2,1)S(1)}, bf16[304,256]{1,0:T(8,128)(2,1)S(1)}, u32[]{:S(2)}, u32[]{:S(2)}) collective-permute-start(bf16[304,256]{1,0:T(8,128)(2,1)S(1)} %collective-permute-done.w2), channel_id=1, source_target_pairs={{0,8},{8,0},{16,24},{24,16},{1,9},{9,1},{17,25},{25,17},{2,10},{10... | collective-permute-start | bytes 466952 | tf_op jit(solution)/shard_map/ppermute | solution.py:563
  25.7 0.8 copy-start
  61.8 1.6 %collective-permute-start.5 = (bf16[2,288,256]{2,1,0:T(8,128)(2,1)S(1)}, bf16[2,288,256]{2,1,0:T(8,128)(2,1)S(1)}, u32[]{:S(2)}, u32[]{:S(2)}) collective-permute-start(bf16[2,288,256]{2,1,0:T(8,128)(2,1)S(1)} %get-tuple-element.38), channel_id=1, source_target_pairs={{0,8},{8,0},{16,24},{24,16},{1,9},{9,1},{17,25},{25,17},{2,10},{10... | collective-permute-start | bytes 884744 | tf_op jit(solution)/shard_map/ppermute | solution.py:563
  63.5 6.0 %collective-permute-start.6 = (bf16[288,256]{1,0:T(8,128)(2,1)S(1)}, bf16[288,256]{1,0:T(8,128)(2,1)S(1)}, u32[]{:S(2)}, u32[]{:S(2)}) collective-permute-start(bf16[288,256]{1,0:T(8,128)(2,1)S(1)} %slice_bitcast_fusion), channel_id=1, source_target_pairs={{0,16},{8,24},{16,0},{24,8},{1,17},{9,25},{17,1},{25,9},{2,18},{10... | collective-permute-start | bytes 442376 | tf_op jit(solution)/shard_map/ppermute | solution.py:563
  65.0 22.0 %all-to-all-start.1 = ((f32[8,2,32,256]{3,2,1,0:T(8,128)}), f32[8,2,32,256]{3,2,1,0:T(8,128)S(1)}, u32[]{:S(2)}, u32[]{:S(2)}) async-start(f32[8,2,32,256]{3,2,1,0:T(8,128)} %get-tuple-element.39), calls=%async_computation.1 | async-start | bytes 1048576 | tf_op jit(solution)/shard_map/all_to_all | solution.py:684
  69.5 9.2 %collective-permute-start.7 = (bf16[288,256]{1,0:T(8,128)(2,1)S(1)}, bf16[288,256]{1,0:T(8,128)(2,1)S(1)}, u32[]{:S(2)}, u32[]{:S(2)}) collective-permute-start(bf16[288,256]{1,0:T(8,128)(2,1)S(1)} %fusion), channel_id=1, source_target_pairs={{0,1},{1,0},{2,3},{3,2},{4,5},{5,4},{6,7},{7,6},{8,9},{9,8},{10,11... | collective-permute-start | bytes 442376 | tf_op jit(solution)/shard_map/ppermute | solution.py:563
  78.7 6.1 %collective-permute-start.8 = (bf16[288,256]{1,0:T(8,128)(2,1)S(1)}, bf16[288,256]{1,0:T(8,128)(2,1)S(1)}, u32[]{:S(2)}, u32[]{:S(2)}) collective-permute-start(bf16[288,256]{1,0:T(8,128)(2,1)S(1)} %add_convert_fusion.2), channel_id=1, source_target_pairs={{0,2},{1,3},{2,0},{3,1},{4,6},{5,7},{6,4},{7,5},{8,10},{9,11},{10,... | collective-permute-start | bytes 442376 | tf_op jit(solution)/shard_map/ppermute | solution.py:563
  84.9 7.7 %collective-permute-start.9 = (bf16[288,256]{1,0:T(8,128)(2,1)S(1)}, bf16[288,256]{1,0:T(8,128)(2,1)S(1)}, u32[]{:S(2)}, u32[]{:S(2)}) collective-permute-start(bf16[288,256]{1,0:T(8,128)(2,1)S(1)} %add_convert_fusion.1.low_ref), channel_id=1, source_target_pairs={{0,4},{1,5},{2,6},{3,7},{4,0},{5,1},{6,2},{7,3},{8,12},{9,13},{10,... | collective-permute-start | bytes 442376 | tf_op jit(solution)/shard_map/ppermute | solution.py:563
  90.1 4.0 %collective-permute-start.12 = (f32[72,256]{1,0:T(8,128)S(1)}, f32[72,256]{1,0:T(8,128)S(1)}, u32[]{:S(2)}, u32[]{:S(2)}) collective-permute-start(f32[72,256]{1,0:T(8,128)S(1)} %project.1.n0), channel_id=1, source_target_pairs={{0,24},{8,16},{16,8},{24,0},{1,25},{9,17},{17,9},{25,1},{2,26},{10... | collective-permute-start | bytes 221192 | tf_op jit(solution)/shard_map/ppermute | solution.py:563
  90.1 5.2 %collective-permute-start.11 = (f32[72,256]{1,0:T(8,128)S(1)}, f32[72,256]{1,0:T(8,128)S(1)}, u32[]{:S(2)}, u32[]{:S(2)}) collective-permute-start(f32[72,256]{1,0:T(8,128)S(1)} %project.1.n0), channel_id=1, source_target_pairs={{0,16},{8,24},{16,0},{24,8},{1,17},{9,25},{17,1},{25,9},{2,18},{10... | collective-permute-start | bytes 221192 | tf_op jit(solution)/shard_map/ppermute | solution.py:563
  90.7 4.6 %collective-permute-start.10 = (f32[72,256]{1,0:T(8,128)S(1)}, f32[72,256]{1,0:T(8,128)S(1)}, u32[]{:S(2)}, u32[]{:S(2)}) collective-permute-start(f32[72,256]{1,0:T(8,128)S(1)} %project.1.n0), channel_id=1, source_target_pairs={{0,8},{8,0},{16,24},{24,16},{1,9},{9,1},{17,25},{25,17},{2,10},{10... | collective-permute-start | bytes 221192 | tf_op jit(solution)/shard_map/ppermute | solution.py:563

commit v4 on v3

--- a/solution.py
+++ b/solution.py
@@ -20,6 +20,10 @@
 NL = 5
 KW = 256
 MIDROWS = NL * 3 * 16
+TAILS = MIDROWS
+LAST = TAILS + 128
+FIRST = LAST + 48
+SUMROWS = FIRST + 16
 A0 = 0.7978845608028654
 A1 = 0.044715 * A0
 
@@ -91,9 +95,9 @@
     ny = field_ref.shape[0] * h if h % 8 == 0 else field_ref.shape[0] // 2
     if h % 8 == 0:
         fields = [field_ref[:, c].reshape(ny, KW) for c in range(2)]
-        field = jnp.concatenate(fields, axis=0)
+        field = jnp.concatenate(fields, axis=0).astype(f32)
     else:
-        field = field_ref[...]
+        field = field_ref[...].astype(f32)
     along = product(halves(field), halves(tx_ref[...]))
     table = halves(ty_ref[...])
     if h % 8 == 0:
@@ -107,12 +111,15 @@
     return product(halves(product(trow, halves(u))), back)
 
 
-def gelu_both(z):
+def gelu(z):
+    t = jnp.tanh(z * (A0 + A1 * (z * z)))
+    return z * (0.5 * t + 0.5)
+
+
+def gelu_slope(z):
     z2 = z * z
     t = jnp.tanh(z * (A0 + A1 * z2))
-    h = 0.5 * t + 0.5
-    a = z * h
-    return a, h + a * (1.0 - h) * (2.0 * A0 + 6.0 * A1 * z2)
+    return (0.5 * t + 0.5) + (z * (0.5 * A0 + 1.5 * A1 * z2)) * (1.0 - t * t)
 
 
 def lroll(x, s):
@@ -173,14 +180,26 @@
 
 
 def step_kernel(
-    h, me_ref, vel_ref, up_ref, down_ref, w0, w1, w2, w3, offs_ref,
-    cot_ref, tx_ref, ty_ref, back_ref, trow_ref, mxx_ref, myy_ref, mxy_ref,
+    h, vel_ref, up_ref, down_ref, w0, w1, w2, w3, offs_ref,
+    cot_ref, *rest,
+):
+    held = rest[:7]
+    (
     prov_ref, vel_grad_ref, keep_ref, send_ref,
-    vp_ref, vs_ref, face_ref, mix_ref, xb, gb, wk_ref, w7_ref, wf_ref, w7k,
-    gz7, gz6, gz5, gz4, gz3, gz2, gz1, f8, adv_ref, acc_ref, gp_ref, near8,
-):
+    tx_ref, ty_ref, back_ref, trow_ref, mxx_ref, myy_ref, mxy_ref,
+    vp_ref, vs_ref, face_ref, mix_ref, xb, zb, wk_ref, w7_ref, wf_ref, w7k,
+    gz7, gz6, gz5, gz4, gz3, gz2, gz1, f8, adv_ref, acc_ref, gp_ref, near8, sems,
+    ) = rest[7:]
+    loads = [
+        pltpu.make_async_copy(table.at[lax.axis_index("space")] if k == 3 else table, place, sems.at[k])
+        for k, (table, place) in enumerate(
+            zip(held, (tx_ref, ty_ref, back_ref, trow_ref, mxx_ref, myy_ref, mxy_ref))
+        )
+    ]
+    for load in loads:
+        load.start()
     rows = h + 2 * HALO
-    me = me_ref[0]
+    me = lax.axis_index("chan")
     for k, piece in enumerate((w0, w1, w2, w3)):
         slot = jnp.bitwise_xor(me, k)
         at16 = pl.ds(pl.multiple_of(slot * 16, 16), 16)
@@ -207,74 +226,73 @@
     def vs_rows(y, n):
         return rows_of(vs_ref, (y + HALO) * 8, 8 * n)
 
-    wfirst = wf_ref[:, 0:24]
-    bias = jnp.broadcast_to(wf_ref[:, 24:25].astype(f32), (C, KW))
+    ones = jnp.ones((16, KW), bf16)
+
+    wfirst = wf_ref[:, 0:32]
     n = h + 2 * (DEEP - 1)
     count, size = blocks(n)
 
     def first_block(k, _):
-        top = jnp.minimum(k * size, n - size) - (DEEP - 1)
+        top = k * size - (DEEP - 1)
         for r in range(size):
             y = top + r
-            x = vs_rows(y - 1, 3).astype(bf16)
-            z = jnp.dot(wfirst, x, preferred_element_type=f32)
-            a, d = gelu_both(z + bias)
-            xb[0, y + DEEP] = a.astype(bf16)
-            gb[0, y + DEEP] = d.astype(bf16)
+            x = jnp.concatenate([vs_rows(y - 1, 3), jnp.ones((8, KW), f32)], axis=0)
+            z = jnp.dot(wfirst, x.astype(bf16), preferred_element_type=f32)
+            zb[0, y + DEEP] = z
+            xb[0, y + DEEP] = gelu(z).astype(bf16)
         return 0
 
     lax.fori_loop(0, count, first_block, 0)
+
+    def rows_through(source, weight, width, first, n, most, done):
+        count, size = blocks(n, most)
+
+        def taps(row):
+            x = jnp.concatenate([shifts(source(row)), ones], axis=0)
+            o = jnp.dot(weight, x, preferred_element_type=f32)
+            return [o[i * width : (i + 1) * width] for i in range(3)]
+
+        def block(k, carry):
+            p0, p1 = carry
+            for r in range(size):
+                row = first + k * size + r
+                o = taps(row + 1)
+                done(row, p1 + o[2])
+                p0, p1 = o[0], p0 + o[1]
+            return p0, p1
+
+        before, here = taps(first - 1), taps(first)
+        lax.fori_loop(0, count, block, (here[0], before[0] + here[1]))
+
     for l in range(1, NL + 1):
-        weight = wk_ref[3 * (l - 1) : 3 * l].reshape(192, KW)
-        bias = jnp.broadcast_to(weight[0:C, 192:193].astype(f32), (C, KW))
-        weight = weight[:, 0:192]
-        n = h + 2 * (DEEP - 1 - l)
-        count, size = blocks(n)
-
-        def block(k, _, l=l, weight=weight, bias=bias, n=n, size=size):
-            top = jnp.minimum(k * size, n - size) - (DEEP - 1 - l) + DEEP
-            p0 = p1 = None
-            for r in range(-1, size + 1):
-                o = jnp.dot(weight, shifts(xb[l - 1, top + r]), preferred_element_type=f32)
-                if r >= 1:
-                    a, d = gelu_both(p1 + o[128:192] + bias)
-                    xb[l, top + r - 1] = a.astype(bf16)
-                    gb[l, top + r - 1] = d.astype(bf16)
-                p1 = o[64:128] if p0 is None else p0 + o[64:128]
-                p0 = o[0:64]
-            return 0
-
-        lax.fori_loop(0, count, block, 0)
-
-    weight = w7_ref[...].reshape(96, KW)
-    bias = jnp.broadcast_to(weight[0:32, 192:193].astype(f32), (32, KW))
-    weight = weight[:, 0:192]
+
+        def done(row, z, l=l):
+            zb[l, row] = z
+            xb[l, row] = gelu(z).astype(bf16)
+
+        rows_through(
+            lambda row, l=l: xb[l - 1, row],
+            wk_ref[3 * (l - 1) : 3 * l].reshape(192, KW)[:, 0:208],
+            C, 1 + l, h + 2 * (DEEP - 1 - l), 27, done,
+        )
+
     row = lax.broadcasted_iota(jnp.int32, (32, KW), 0)
     point = (row // 8) * 4 + row % 4
     second = jnp.where((row // 4) % 2 == 0, 6, 9)
     base = jnp.where((point == 5) | (point == second), 0.5, 0.0).astype(f32)
-    n = h + 4
-    count, size = blocks(n, 12)
-
-    def last_block(k, _):
-        top = jnp.minimum(k * size, n - size) - 2
-        p0 = p1 = None
-        for r in range(-1, size + 1):
-            o = jnp.dot(weight, shifts(xb[NL, top + r + DEEP]), preferred_element_type=f32)
-            if r >= 1:
-                y = top + r - 1
-                s = p1 + o[64:96] + bias
-                mean = group4(s[0:8] + s[8:16] + s[16:24] + s[24:32]) * (1.0 / 16.0)
-                mix = s - jnp.concatenate([mean] * 4, axis=0) + base
-                mix_ref[pl.ds(pl.multiple_of((y + 2) * 32, 32), 32), :] = mix
-                m = mix * vs_rows(y - 1, 4)
-                m = group4(m[0:8] + m[8:16] + m[16:24] + m[24:32])
-                put_rows(f8, (y + 2) * 8, m)
-            p1 = o[32:64] if p0 is None else p0 + o[32:64]
-            p0 = o[0:32]
-        return 0
-
-    lax.fori_loop(0, count, last_block, 0)
+
+    def mixed(row, s):
+        y = row - DEEP
+        mean = group4(s[0:8] + s[8:16] + s[16:24] + s[24:32]) * (1.0 / 16.0)
+        mix = s - jnp.concatenate([mean] * 4, axis=0) + base
+        mix_ref[pl.ds(pl.multiple_of((y + 2) * 32, 32), 32), :] = mix
+        m = mix * vs_rows(y - 1, 4)
+        m = group4(m[0:8] + m[8:16] + m[16:24] + m[24:32])
+        put_rows(f8, (y + 2) * 8, m)
+
+    rows_through(
+        lambda row: xb[NL, row], w7_ref[...].reshape(96, KW)[:, 0:208], 32, DEEP - 2, h + 4, 18, mixed
+    )
     for c in range(2):
         face_ref[c] = collect(f8, c * 4, h + 4)
     ue = face_ref[0, 2 : 2 + h]
@@ -292,7 +310,7 @@
         adv = fx - lroll(fx, 1) + vn * (q + north) * 0.5 - vn_south * (south + q) * 0.5
         new = q + time_step * (viscosity * lap - adv)
         for k in range(prov_ref.shape[0]):
-            prov_ref[k, c] = new
+            prov_ref[k, c] = new.astype(prov_ref.dtype)
         own = own + jnp.sum(q * q)
         update = update + jnp.sum((new - q) * (new - q))
     lane = lax.broadcasted_iota(jnp.int32, (8, KW), 1)
@@ -300,10 +318,13 @@
         lane == 0, own, jnp.where(lane == 1, total[0], jnp.where(lane == 2, update, 0.0))
     )
 
+    for load in loads:
+        load.wait()
+
     n = h + 2 * GPH
     u, v = spectrum(h, cot_ref, tx_ref, ty_ref)
     u, v = project_spectral(u, v, mxx_ref[...], myy_ref[...], mxy_ref[...])
-    trow = halves(trow_ref[me_ref[1]])
+    trow = halves(trow_ref[...])
     gp_ref[0] = project_back(trow, u, back_ref)
     gp_ref[1] = project_back(trow, v, back_ref)
 
@@ -354,8 +375,6 @@
 
     lax.fori_loop(0, (h + 14) // 2, stencil_row, 0, unroll=4 if h >= 16 else 1)
 
-    ones = jnp.ones((16, KW), bf16)
-
     def wgrad(columns, inputs):
         return lax.dot_general(
             jnp.concatenate(columns, axis=1),
@@ -388,7 +407,8 @@
                 o = jnp.dot(weight, columns[y], preferred_element_type=f32)
                 if y >= 2 - l:
                     ga = p1 + o[0:64]
-                    target[y - 1 + l - 1] = (ga * gb[l - 2, y - 1 + DEEP].astype(f32)).astype(bf16)
+                    slope = gelu_slope(zb[l - 2, y - 1 + DEEP])
+                    target[y - 1 + l - 1] = (ga * slope).astype(bf16)
                 p1 = o[64:128] if p0 is None else p0 + o[64:128]
                 p0 = o[128:192]
             own = [y for y in ys if 0 <= y < h]
@@ -442,28 +462,41 @@
             total = total + lroll(collect(near8, c * 4 + d, h), d - 1)
         vel_grad_ref[c] = total
 
+    lane = lax.broadcasted_iota(jnp.int32, (16, 64), 1)
     for k, other in enumerate((0, 2, 1, 3)):
         slot = jnp.bitwise_xor(me, other)
         pack_ref = (keep_ref, send_ref)[k // 2]
         k = k % 2
+        tails = []
+        bias = jnp.zeros((16, 64), f32)
         for l in range(NL):
             for j in range(3):
                 piece = acc_ref[l + 1, pl.ds(pl.multiple_of(j * 64 + slot * 16, 16), 16), :]
-                pack_ref[k, (3 * l + j) * 16 : (3 * l + j) * 16 + 16, :] = piece.astype(bf16)
+                at = (3 * l + j) * 16
+                pack_ref[k, at : at + 16, :] = piece[:, 0:128].astype(bf16)
+                tails.append(piece[:, 128:192])
+                if j == 0:
+                    bias = jnp.where(lane == l, jnp.broadcast_to(piece[:, 192:193], (16, 64)), bias)
+        tails.append(bias)
+        for n in range(8):
+            at = TAILS + 16 * n
+            pack_ref[k, at : at + 16, :] = jnp.concatenate(tails[2 * n : 2 * n + 2], axis=1).astype(bf16)
         last = [
             acc_ref[6, pl.ds(pl.multiple_of(j * 32 + slot * 8, 8), 8), :] for j in range(3)
         ]
-        pack_ref[k, MIDROWS : MIDROWS + 32, :] = jnp.concatenate(
-            last + [squares], axis=0
-        ).astype(bf16)
-        pack_ref[k, MIDROWS + 32 : MIDROWS + 48, :] = acc_ref[
-            0, pl.ds(pl.multiple_of(slot * 16, 16), 16), :
+        tails = [p[:, 128:192] for p in last]
+        tails.append(jnp.broadcast_to(last[0][:, 192:193], (8, 64)))
+        groups = [p[:, 0:128] for p in last]
+        groups += [jnp.concatenate(tails[0:2], axis=1), jnp.concatenate(tails[2:4], axis=1)]
+        groups.append(squares[:, 0:128])
+        pack_ref[k, LAST:FIRST, :] = jnp.concatenate(groups, axis=0).astype(bf16)
+        pack_ref[k, FIRST:SUMROWS, :] = acc_ref[
+            0, pl.ds(pl.multiple_of(slot * 16, 16), 16), 0:128
         ].astype(bf16)
 
 
-def project_kernel(h, me_ref, prov_ref, tx_ref, ty_ref, back_ref, trow_ref, mxx_ref, myy_ref, mxy_ref, out_ref):
-    me_space = me_ref[1]
-    trow = halves(trow_ref[me_space][GPH : GPH + h])
+def project_kernel(h, prov_ref, tx_ref, ty_ref, back_ref, trow_ref, mxx_ref, myy_ref, mxy_ref, out_ref):
+    trow = halves(trow_ref[GPH : GPH + h])
     u, v = spectrum(h, prov_ref, tx_ref, ty_ref)
     u, v = project_spectral(u, v, mxx_ref[...], myy_ref[...], mxy_ref[...])
     out_ref[0:h] = project_back(trow, u, back_ref)
@@ -471,32 +504,31 @@
     out_ref[2 * h :] = jnp.full((8, KW), jnp.sum(u * u) + jnp.sum(v * v), f32)
 
 
-def prepare_kernel(h, me_ref, vel_ref, cot_ref, wm_ref, wl_ref, wf_ref, bm_ref, bf_ref, bl_ref, pack_ref, own_ref, top_ref, bottom_ref, cot_all_ref, tall, wide):
-    me = me_ref[0]
+def prepare_kernel(h, vel_ref, wm_ref, wl_ref, wf_ref, bm_ref, bf_ref, bl_ref, pack_ref, own_ref, top_ref, bottom_ref, tall, wide):
+    me = lax.axis_index("chan")
     own = vel_ref[:, me]
     own_ref[...] = own
     if h >= HALO:
         top_ref[...] = own[:, :HALO]
         bottom_ref[...] = own[:, h - HALO :]
-    cot = cot_ref[:, me]
-    for k in range(cot_all_ref.shape[0]):
-        cot_all_ref[k] = cot
     wide[...] = jnp.zeros_like(wide)
     wide[0:NL, 0:16] = bm_ref[...].astype(f32)
     wide[NL : NL + 1, 0:16] = bf_ref[...].astype(f32)
     wide[NL + 1 : NL + 2, 0:8] = bl_ref[...].astype(f32)
     columns = wide[...].T
 
-    def column(k, count, width):
-        return jnp.broadcast_to(columns[0:count, k : k + 1], (count, width))
+    def column(k, count, i):
+        lane = lax.broadcasted_iota(jnp.int32, (count, 64), 1)
+        here = jnp.broadcast_to(columns[0:count, k : k + 1], (count, 64))
+        return jnp.where((lane == 0) & (i == 1), here, 0.0)
 
     for l in range(NL):
         for i in range(3):
-            parts = [wm_ref[l, i, j] for j in range(3)] + [column(l, 16, 64).astype(bf16)]
+            parts = [wm_ref[l, i, j] for j in range(3)] + [column(l, 16, i).astype(bf16)]
             at = (3 * l + i) * 16
             pack_ref[at : at + 16, :] = jnp.concatenate(parts, axis=1)
     for i in range(3):
-        parts = [wl_ref[i, j].astype(f32) for j in range(3)] + [column(NL + 1, 8, 64)]
+        parts = [wl_ref[i, j].astype(f32) for j in range(3)] + [column(NL + 1, 8, i)]
         block = jnp.concatenate(parts, axis=1)
         at = MIDROWS + i * 16
         pack_ref[at : at + 16, :] = jnp.concatenate([block, jnp.zeros_like(block)], axis=0).astype(bf16)
@@ -512,8 +544,8 @@
     pack_ref[MIDROWS + 48 :, :] = jnp.concatenate([first, jnp.zeros_like(first)], axis=1).astype(bf16)
 
 
-def finish_kernel(h, cells, me_ref, low_ref, other_ref, n0, n1, n2, n3, new_ref, wf_ref, bf_ref, wm_ref, bm_ref, wl_ref, bl_ref, rms_ref, parts):
-    me = me_ref[0]
+def finish_kernel(h, cells, low_ref, other_ref, n0, n1, n2, n3, new_ref, wf_ref, bf_ref, wm_ref, bm_ref, wl_ref, bl_ref, rms_ref, parts):
+    me = lax.axis_index("chan")
     for k, piece in enumerate((n0, n1, n2, n3)):
         slot = jnp.bitwise_xor(me, k)
         new_ref[0, slot] = piece[0:h]
@@ -528,19 +560,22 @@
 
     for l in range(NL):
         for j in range(3):
-            block = total((3 * l + j) * 16, 16)
-            for i in range(3):
-                wm_ref[l, i, j] = block[:, i * 64 : i * 64 + 64]
-            if j == 0:
-                bm_ref[l : l + 1, :] = turned(block[:, 128:256])[64:65, 0:16]
-    tail = total(MIDROWS, 32)
+            n = 3 * l + j
+            block = total(n * 16, 16)
+            tail = total(TAILS + (n // 2) * 16, 16)
+            wm_ref[l, 0, j] = block[:, 0:64]
+            wm_ref[l, 1, j] = block[:, 64:128]
+            wm_ref[l, 2, j] = tail[:, 64 * (n % 2) : 64 * (n % 2) + 64]
+    bm_ref[...] = turned(total(TAILS + 112, 16))[64 : 64 + NL, 0:16]
+    tail = total(LAST, 48)
     for j in range(3):
-        block = tail[j * 8 : j * 8 + 8]
-        for i in range(3):
-            wl_ref[i, j] = block[:, i * 64 : i * 64 + 64]
-        if j == 0:
-            bl_ref[...] = turned(block[:, 128:256])[64:65, 0:8]
-    first = turned(total(MIDROWS + 32, 16)[:, 0:128])
+        wl_ref[0, j] = tail[j * 8 : j * 8 + 8, 0:64]
+        wl_ref[1, j] = tail[j * 8 : j * 8 + 8, 64:128]
+    wl_ref[2, 0] = tail[24:32, 0:64]
+    wl_ref[2, 1] = tail[24:32, 64:128]
+    wl_ref[2, 2] = tail[32:40, 0:64]
+    bl_ref[...] = turned(tail[32:40])[64:65, 0:8]
+    first = turned(total(FIRST, 16))
     for i in range(3):
         for j in range(3):
             for c in range(2):
@@ -549,7 +584,7 @@
     bf_ref[...] = first[24:25, 0:16]
     news = (parts[0] + parts[1]) + (parts[2] + parts[3])
     lane = lax.broadcasted_iota(jnp.int32, (8, 128), 1)
-    sums = jnp.where(lane == 3, news[:, 0:128], tail[24:32, 0:128])
+    sums = jnp.where(lane == 3, news[:, 0:128], tail[40:48])
     rms_ref[...] = jnp.sqrt(sums * (1.0 / cells))[0:1, 0:4]
 
 
@@ -600,11 +635,8 @@
     space = lax.axis_size("space")
     ny = h * space
     me_chan = lax.axis_index("chan")
-    me_space = lax.axis_index("space")
-    me = jnp.stack([me_chan, me_space]).astype(jnp.int32)
     rows = h + 2 * HALO
     shape = jax.ShapeDtypeStruct
-    smem = pl.BlockSpec(memory_space=pltpu.SMEM)
     inside = pltpu.VMEM
 
     def limit(mebibytes):
@@ -613,26 +645,26 @@
     def outside(x):
         return pltpu.with_memory_space_constraint(x, pltpu.HBM)
 
-    packed, own, top, bottom, cot_all = pl.pallas_call(
+    own_cot = lax.dynamic_index_in_dim(cotangent, me_chan, 1, keepdims=False).astype(bf16)
+    cot_all = jnp.broadcast_to(own_cot[None], (space,) + own_cot.shape)
+    packed, own, top, bottom = pl.pallas_call(
         functools.partial(prepare_kernel, h),
         out_shape=[
             inside((MIDROWS + 64, KW), bf16),
             inside((2, h, nx), f32),
             inside((2, min(h, HALO), nx), f32),
             inside((2, min(h, HALO), nx), f32),
-            inside((space, 2, h, nx), f32),
         ],
-        in_specs=[smem] + vmem(8),
-        out_specs=vmem(5),
+        in_specs=vmem(7),
+        out_specs=vmem(4),
         scratch_shapes=[pltpu.VMEM((128, 128), f32), pltpu.VMEM((8, 128), f32)],
         compiler_params=limit(16),
         name="prepare",
     )(
-        me,
         *[
             outside(x)
             for x in (
-                velocity, cotangent, jnp.swapaxes(w_mid, 3, 4), jnp.swapaxes(w_last, 2, 3),
+                velocity, jnp.swapaxes(w_mid, 3, 4), jnp.swapaxes(w_last, 2, 3),
                 w_first, b_mid, b_first[None], b_last[None],
             )
         ],
@@ -648,19 +680,21 @@
 
     deep = h + 2 * DEEP
     constants = [outside(x) for x in tables(h, space, nx)]
-    prov, vel_grad, keep, send = pl.pallas_call(
+    places = [inside(x.shape[1:] if k == 3 else x.shape, f32) for k, x in enumerate(constants)]
+    prov, vel_grad, keep, send, *constants = pl.pallas_call(
         functools.partial(step_kernel, h),
-        out_shape=[inside((space, 2, h, nx), f32), shape((2, h, nx), f32)]
-        + [inside((2, MIDROWS + 48, KW), bf16)] * 2,
-        in_specs=[smem] + vmem(16),
-        out_specs=vmem(4),
+        out_shape=[inside((space, 2, h, nx), bf16), shape((2, h, nx), f32)]
+        + [inside((2, SUMROWS, 128), bf16)] * 2
+        + places,
+        in_specs=vmem(9) + [pl.BlockSpec(memory_space=pl.ANY)] * 7,
+        out_specs=vmem(11),
         scratch_shapes=[
             inside((2, rows, nx), f32),
             inside((nx // 128, rows * 8, 128), f32),
             inside((2, h + 4, nx), f32),
             inside(((h + 4) * 32, nx), f32),
             inside((NL + 1, deep, C, nx), bf16),
-            inside((NL + 1, deep, C, nx), bf16),
+            inside((NL + 1, deep, C, nx), f32),
             inside((NL * 3, C, KW), bf16),
             inside((3, 32, KW), bf16),
             inside((C, KW), bf16),
@@ -674,13 +708,14 @@
             inside((7, 192, KW), f32),
             inside((2, h + 2 * GPH, nx), f32),
             inside((nx // 128, h * 8, 128), f32),
-        ],
-        compiler_params=limit(52),
+        ]
+        + [pltpu.SemaphoreType.DMA((7,))],
+        compiler_params=limit(50),
         cost_estimate=pl.CostEstimate(
             flops=6 * 7 * deep * nx * 9 * C * C, bytes_accessed=2**25, transcendentals=6 * deep * nx * C
         ),
         name="step",
-    )(me, own, up, down, packed, beside, across, diagonal, outside(offsets), cot_full, *constants)
+    )(own, up, down, packed, beside, across, diagonal, outside(offsets), cot_full, *constants)
     everywhere = lax.all_to_all(prov, "space", 0, 0, tiled=True)
     if h % 8:
         everywhere = everywhere.reshape(space * 2 * h, nx)
@@ -688,12 +723,12 @@
     new_own = pl.pallas_call(
         functools.partial(project_kernel, h),
         out_shape=inside((2 * h + 8, nx), f32),
-        in_specs=[smem] + vmem(8),
+        in_specs=vmem(8),
         out_specs=vmem(1)[0],
         compiler_params=limit(16),
         cost_estimate=pl.CostEstimate(flops=2**31, bytes_accessed=2**22, transcendentals=0),
         name="project",
-    )(me, everywhere, *constants)
+    )(everywhere, *constants)
 
     pair = (keep.astype(f32) + swapped(send, "chan", 1).astype(f32)).astype(bf16)
     low = (pair[0].astype(f32) + swapped(pair[1], "chan", 2).astype(f32)).astype(bf16)
@@ -716,12 +751,12 @@
             shape((1, 8), f32),
             shape((1, 4), f32),
         ],
-        in_specs=[smem] + vmem(6),
+        in_specs=vmem(6),
         out_specs=vmem(8),
         scratch_shapes=[pltpu.VMEM((4, 8, KW), f32)],
         compiler_params=limit(16),
         name="finish",
-    )(me, low, other, *news)
+    )(low, other, *news)
     return (
         new_velocity,
         vel_grad[:, None],

time: 97.2 us -> 84.4 us (0.87)
  waiting for transfers between devices: 26.9 us -> 18 us
  Pallas kernels: 41.9 us -> 35.4 us
  starting transfers between devices: 26.3 us -> 28.1 us
    ppermute x2, waiting for transfers between devices: 8.06 us -> 2.37 us  [moved(): return lax.ppermute(x, axis, [(i, (i + step) % n) for i in range(n)])]
    pallas_call x1, Pallas kernels: 35.3 us -> 31.6 us  [per_device(): pl.pallas_call(functools.partial(step_kernel, h), out_shape=[inside((spac...]
    ppermute x11, waiting for transfers between devices: 18.8 us -> 15.6 us  [swapped(): return lax.ppermute(x, axis, [(i, i ^ bit) for i in range(n)])]
    pallas_call x1, Pallas kernels: 3.02 us -> 1.55 us  [per_device(): pl.pallas_call(functools.partial(project_kernel, h), out_shape=inside((2...]
    all_to_all x1, starting transfers between devices: 3.66 us -> 4.87 us  [per_device(): everywhere = lax.all_to_all(prov, 'space', 0, 0, tiled=True)]
  transfers between devices with their start and end apart: 15 -> 15, of which waited for: 9 -> 7; matrix products, arithmetic and copies ran while one was open for 0% -> 0% of each run, Pallas kernels for 3% -> 3%
where the time goes in v4:
time: 84.4 us; the launch traced here: 84.1 us
  Pallas kernels  35.4 us (42%)
  starting transfers between devices  28.1 us (33%)
  waiting for transfers between devices  18 us (21%)
  local copies, waits for them, and re-layouts  1.69 us (2%)
    pallas_call x1, Pallas kernels, per_device(): pl.pallas_call(functools.partial(step_kernel, h), out_shape=[inside((spac...  31.6 us
    ppermute x11, waiting for transfers between devices, swapped(): return lax.ppermute(x, axis, [(i, i ^ bit) for i in range(n)])  15.6 us
    ppermute x11, starting transfers between devices, swapped(): return lax.ppermute(x, axis, [(i, i ^ bit) for i in range(n)])  11.2 us
    all_to_all x1, starting transfers between devices, per_device(): cot_full = lax.all_to_all(cot_all, 'space', 0, 0, tiled=True)  7.28 us
    all_to_all x1, starting transfers between devices, per_device(): everywhere = lax.all_to_all(prov, 'space', 0, 0, tiled=True)  4.87 us
    ppermute x2, starting transfers between devices, moved(): return lax.ppermute(x, axis, [(i, (i + step) % n) for i in range(n)])  4.72 us
    ppermute x2, waiting for transfers between devices, moved(): return lax.ppermute(x, axis, [(i, (i + step) % n) for i in range(n)])  2.37 us
  transfers between devices with their start and end apart: 15, of which 7 were waited for; matrix products, arithmetic and copies ran while one was open for 0% of the time, Pallas kernels for 3%

profile of v4, /device:TPU:0, one launch (start us, length us, event | category | flops | bytes accessed | tf_op | source)
XLA Modules:
  0.0 84.1 jit_solution(6030914163005151164)
XLA Ops:
  0.7 0.9 %copy-done = f32[2,4,32,256]{3,2,1,0:T(8,128)S(1)} copy-done((f32[2,4,32,256]{3,2,1,0:T(8,128)S(1)}, f32[2,4,32,256]{3,2,1,0:T(8,128)}, u32[]{:S(2)}) %copy-start) | copy-done | bytes 262168
  1.6 0.7 broadcast_in_dim.17
  2.3 7.3 %all-to-all-start = ((bf16[8,2,32,256]{3,2,1,0:T(8,128)(2,1)}), bf16[8,2,32,256]{3,2,1,0:T(8,128)(2,1)S(1)}, u32[]{:S(2)}, u32[]{:S(2)}) async-start(bf16[8,2,32,256]{3,2,1,0:T(8,128)(2,1)} %broadcast_in_dim.17), calls=%async_computation | async-start | bytes 524288 | tf_op jit(solution)/shard_map/all_to_all | solution.py:677
  9.6 1.3 %prepare.1 = (bf16[304,256]{1,0:T(8,128)(2,1)S(1)}, f32[2,32,256]{2,1,0:T(8,128)S(1)}, f32[2,16,256]{2,1,0:T(8,128)S(1)}, f32[2,16,256]{2,1,0:T(8,128)S(1)}) custom-call(f32[2,4,32,256]{3,2,1,0:T(8,128)} %vel_ref.1, bf16[5,3,3,16,64]{4,3,2,1,0:T(8,128)(2,1)} %bitcast.21, bf16[3,3,8,64]{3,2,1,0:T(8,128)(2,1)} %bitcast.22, bf16[3,3,2,16]{3,2,1,0:T(2,128)(2,1)} %wf_ref.1, ...), custom_call_target="tpu_custom_call" | custom-call | tf_op jit(solution)/shard_map/prepare/pallas_call | solution.py:650
  10.9 1.6 %collective-permute-start = (bf16[304,256]{1,0:T(8,128)(2,1)S(1)}, bf16[304,256]{1,0:T(8,128)(2,1)S(1)}, u32[]{:S(2)}, u32[]{:S(2)}) collective-permute-start(bf16[304,256]{1,0:T(8,128)(2,1)S(1)} %get-tuple-element.36.w0), channel_id=1, source_target_pairs={{0,16},{8,24},{16,0},{24,8},{1,17},{9,25},{17,1},{25,9},{2,18},{10... | collective-permute-start | bytes 466952 | tf_op jit(solution)/shard_map/ppermute | solution.py:598
  12.5 2.0 %collective-permute-start.1 = (f32[2,16,256]{2,1,0:T(8,128)S(1)}, f32[2,16,256]{2,1,0:T(8,128)S(1)}, u32[]{:S(2)}, u32[]{:S(2)}) collective-permute-start(f32[2,16,256]{2,1,0:T(8,128)S(1)} %get-tuple-element.37), channel_id=1, source_target_pairs={{0,1},{1,2},{2,3},{3,4},{4,5},{5,6},{6,7},{7,0},{8,9},{9,10},{10,1... | collective-permute-start | bytes 98312 | tf_op jit(solution)/shard_map/ppermute | solution.py:593
  14.5 2.7 %collective-permute-start.2 = (f32[2,16,256]{2,1,0:T(8,128)S(1)}, f32[2,16,256]{2,1,0:T(8,128)S(1)}, u32[]{:S(2)}, u32[]{:S(2)}) collective-permute-start(f32[2,16,256]{2,1,0:T(8,128)S(1)} %get-tuple-element.38), channel_id=1, source_target_pairs={{0,7},{1,0},{2,1},{3,2},{4,3},{5,4},{6,5},{7,6},{8,15},{9,8},{10,9... | collective-permute-start | bytes 98312 | tf_op jit(solution)/shard_map/ppermute | solution.py:593
  17.2 2.4 %collective-permute-done.1.up_ref = f32[2,16,256]{2,1,0:T(8,128)S(1)} collective-permute-done((f32[2,16,256]{2,1,0:T(8,128)S(1)}, f32[2,16,256]{2,1,0:T(8,128)S(1)}, u32[]{:S(2)}, u32[]{:S(2)}) %collective-permute-start.1) | collective-permute-done | bytes 32800 | tf_op jit(solution)/shard_map/ppermute | solution.py:593
  19.6 1.4 %collective-permute-done.4.w3 = bf16[304,256]{1,0:T(8,128)(2,1)S(1)} collective-permute-done((bf16[304,256]{1,0:T(8,128)(2,1)S(1)}, bf16[304,256]{1,0:T(8,128)(2,1)S(1)}, u32[]{:S(2)}, u32[]{:S(2)}) %collective-permute-start.4) | collective-permute-done | bytes 155680 | tf_op jit(solution)/shard_map/ppermute | solution.py:598
  21.0 31.6 %step.1 = (bf16[8,2,32,256]{3,2,1,0:T(8,128)(2,1)}, f32[2,32,256]{2,1,0:T(8,128)}, bf16[2,432,128]{2,1,0:T(8,128)(2,1)S(1)}, bf16[2,432,128]{2,1,0:T(8,128)(2,1)...) custom-call(f32[2,32,256]{2,1,0:T(8,128)S(1)} %get-tuple-element.35., ...), custom_call_target="tpu_custom_call" | custom-call | flops 22196256768 | bytes 33554432 | tf_op jit(solution)/shard_map/step/pallas_call | solution.py:684
  52.8 1.3 %collective-permute-done.5 = bf16[2,432,128]{2,1,0:T(8,128)(2,1)S(1)} collective-permute-done((bf16[2,432,128]{2,1,0:T(8,128)(2,1)S(1)}, bf16[2,432,128]{2,1,0:T(8,128)(2,1)S(1)}, u32[]{:S(2)}, u32[]{:S(2)}) %collective-permute-start.5) | collective-permute-done | bytes 221216 | tf_op jit(solution)/shard_map/ppermute | solution.py:598
  54.2 1.6 %collective-permute-start.6 = (bf16[432,128]{1,0:T(8,128)(2,1)S(1)}, bf16[432,128]{1,0:T(8,128)(2,1)S(1)}, u32[]{:S(2)}, u32[]{:S(2)}) collective-permute-start(bf16[432,128]{1,0:T(8,128)(2,1)S(1)} %slice_bitcast_fusion), channel_id=1, source_target_pairs={{0,16},{8,24},{16,0},{24,8},{1,17},{9,25},{17,1},{25,9},{2,18},{10... | collective-permute-start | bytes 331784 | tf_op jit(solution)/shard_map/ppermute | solution.py:598
  55.8 3.6 %collective-permute-done.6 = bf16[432,128]{1,0:T(8,128)(2,1)S(1)} collective-permute-done((bf16[432,128]{1,0:T(8,128)(2,1)S(1)}, bf16[432,128]{1,0:T(8,128)(2,1)S(1)}, u32[]{:S(2)}, u32[]{:S(2)}) %collective-permute-start.6) | collective-permute-done | bytes 110624 | tf_op jit(solution)/shard_map/ppermute | solution.py:598
  59.4 1.3 %collective-permute-start.7 = (bf16[432,128]{1,0:T(8,128)(2,1)S(1)}, bf16[432,128]{1,0:T(8,128)(2,1)S(1)}, u32[]{:S(2)}, u32[]{:S(2)}) collective-permute-start(bf16[432,128]{1,0:T(8,128)(2,1)S(1)} %fusion), channel_id=1, source_target_pairs={{0,1},{1,0},{2,3},{3,2},{4,5},{5,4},{6,7},{7,6},{8,9},{9,8},{10,11... | collective-permute-start | bytes 331784 | tf_op jit(solution)/shard_map/ppermute | solution.py:598
  60.7 4.9 %all-to-all-start.1 = ((bf16[8,2,32,256]{3,2,1,0:T(8,128)(2,1)}), bf16[8,2,32,256]{3,2,1,0:T(8,128)(2,1)S(1)}, u32[]{:S(2)}, u32[]{:S(2)}) async-start(bf16[8,2,32,256]{3,2,1,0:T(8,128)(2,1)} %get-tuple-element.44), calls=%async_computation.1 | async-start | bytes 524288 | tf_op jit(solution)/shard_map/all_to_all | solution.py:719
  65.6 2.1 %collective-permute-start.8 = (bf16[432,128]{1,0:T(8,128)(2,1)S(1)}, bf16[432,128]{1,0:T(8,128)(2,1)S(1)}, u32[]{:S(2)}, u32[]{:S(2)}) collective-permute-start(bf16[432,128]{1,0:T(8,128)(2,1)S(1)} %add_convert_fusion.2), channel_id=1, source_target_pairs={{0,2},{1,3},{2,0},{3,1},{4,6},{5,7},{6,4},{7,5},{8,10},{9,11},{10,... | collective-permute-start | bytes 331784 | tf_op jit(solution)/shard_map/ppermute | solution.py:598
  67.7 6.0 %collective-permute-done.8 = bf16[432,128]{1,0:T(8,128)(2,1)S(1)} collective-permute-done((bf16[432,128]{1,0:T(8,128)(2,1)S(1)}, bf16[432,128]{1,0:T(8,128)(2,1)S(1)}, u32[]{:S(2)}, u32[]{:S(2)}) %collective-permute-start.8) | collective-permute-done | bytes 110624 | tf_op jit(solution)/shard_map/ppermute | solution.py:598
  73.7 2.7 %collective-permute-start.9 = (bf16[432,128]{1,0:T(8,128)(2,1)S(1)}, bf16[432,128]{1,0:T(8,128)(2,1)S(1)}, u32[]{:S(2)}, u32[]{:S(2)}) collective-permute-start(bf16[432,128]{1,0:T(8,128)(2,1)S(1)} %add_convert_fusion.1.low_ref), channel_id=1, source_target_pairs={{0,4},{1,5},{2,6},{3,7},{4,0},{5,1},{6,2},{7,3},{8,12},{9,13},{10,... | collective-permute-start | bytes 331784 | tf_op jit(solution)/shard_map/ppermute | solution.py:598
  76.4 1.6 %project.1.n0 = f32[72,256]{1,0:T(8,128)S(1)} custom-call(bf16[8,2,32,256]{3,2,1,0:T(8,128)(2,1)S(1)} %all-to-all-done.1.prov_ref, f32[256,256]{1,0:T(8,128)S(1)} %get-tuple-element.45.tx_ref, f32[256,256]{1,0:T(8,128)S(1)} %get-tuple-element.46.ty_ref, f32[256,256]{1,0:T(8,128)S(1)} %get-tuple-element.47.back_ref, ...), custom_call_target="tpu_custom_call" | custom-call | flops 2147483648 | bytes 4194304 | tf_op jit(solution)/shard_map/project/pallas_call | solution.py:723
  78.0 0.6 collective-permute-start.11
  78.6 1.3 %collective-permute-start.10 = (f32[72,256]{1,0:T(8,128)S(1)}, f32[72,256]{1,0:T(8,128)S(1)}, u32[]{:S(2)}, u32[]{:S(2)}) collective-permute-start(f32[72,256]{1,0:T(8,128)S(1)} %project.1.n0), channel_id=1, source_target_pairs={{0,8},{8,0},{16,24},{24,16},{1,9},{9,1},{17,25},{25,17},{2,10},{10... | collective-permute-start | bytes 221192 | tf_op jit(solution)/shard_map/ppermute | solution.py:598
  79.9 2.1 %collective-permute-done.12.n3 = f32[72,256]{1,0:T(8,128)S(1)} collective-permute-done((f32[72,256]{1,0:T(8,128)S(1)}, f32[72,256]{1,0:T(8,128)S(1)}, u32[]{:S(2)}, u32[]{:S(2)}) %collective-permute-start.12) | collective-permute-done | bytes 73760 | tf_op jit(solution)/shard_map/ppermute | solution.py:598
  82.0 1.1 %collective-permute-done.11.n2 = f32[72,256]{1,0:T(8,128)S(1)} collective-permute-done((f32[72,256]{1,0:T(8,128)S(1)}, f32[72,256]{1,0:T(8,128)S(1)}, u32[]{:S(2)}, u32[]{:S(2)}) %collective-permute-start.11) | collective-permute-done | bytes 73760 | tf_op jit(solution)/shard_map/ppermute | solution.py:598
  83.1 0.9 %finish.1 = (f32[2,4,32,256]{3,2,1,0:T(8,128)}, f32[3,3,2,16]{3,2,1,0:T(2,128)}, f32[1,16]{1,0:T(1,128)}, f32[5,3,3,16,64]{4,3,2,1,0:T(8,128)}, f32[5,16]{1,0:T(...) custom-call(bf16[432,128]{1,0:T(8,128)(2,1)S(1)} %add_convert_fusion.1.low_ref, ...), custom_call_target="tpu_custom_call" | custom-call | tf_op jit(solution)/shard_map/finish/pallas_call | solution.py:742
  (19 shorter events, 0.4 us)
Async XLA Ops:
  0.6 1.0 %copy-start = (f32[2,4,32,256]{3,2,1,0:T(8,128)S(1)}, f32[2,4,32,256]{3,2,1,0:T(8,128)}, u32[]{:S(2)}) copy-start(f32[2,4,32,256]{3,2,1,0:T(8,128)} %param.24) | copy-start | bytes 786436
  2.3 18.6 %all-to-all-start = ((bf16[8,2,32,256]{3,2,1,0:T(8,128)(2,1)}), bf16[8,2,32,256]{3,2,1,0:T(8,128)(2,1)S(1)}, u32[]{:S(2)}, u32[]{:S(2)}) async-start(bf16[8,2,32,256]{3,2,1,0:T(8,128)(2,1)} %broadcast_in_dim.17), calls=%async_computation | async-start | bytes 524288 | tf_op jit(solution)/shard_map/all_to_all | solution.py:677
  10.9 8.7 %collective-permute-start = (bf16[304,256]{1,0:T(8,128)(2,1)S(1)}, bf16[304,256]{1,0:T(8,128)(2,1)S(1)}, u32[]{:S(2)}, u32[]{:S(2)}) collective-permute-start(bf16[304,256]{1,0:T(8,128)(2,1)S(1)} %get-tuple-element.36.w0), channel_id=1, source_target_pairs={{0,16},{8,24},{16,0},{24,8},{1,17},{9,25},{17,1},{25,9},{2,18},{10... | collective-permute-start | bytes 466952 | tf_op jit(solution)/shard_map/ppermute | solution.py:598
  12.5 7.1 %collective-permute-start.1 = (f32[2,16,256]{2,1,0:T(8,128)S(1)}, f32[2,16,256]{2,1,0:T(8,128)S(1)}, u32[]{:S(2)}, u32[]{:S(2)}) collective-permute-start(f32[2,16,256]{2,1,0:T(8,128)S(1)} %get-tuple-element.37), channel_id=1, source_target_pairs={{0,1},{1,2},{2,3},{3,4},{4,5},{5,6},{6,7},{7,0},{8,9},{9,10},{10,1... | collective-permute-start | bytes 98312 | tf_op jit(solution)/shard_map/ppermute | solution.py:593
  14.5 5.1 %collective-permute-start.2 = (f32[2,16,256]{2,1,0:T(8,128)S(1)}, f32[2,16,256]{2,1,0:T(8,128)S(1)}, u32[]{:S(2)}, u32[]{:S(2)}) collective-permute-start(f32[2,16,256]{2,1,0:T(8,128)S(1)} %get-tuple-element.38), channel_id=1, source_target_pairs={{0,7},{1,0},{2,1},{3,2},{4,3},{5,4},{6,5},{7,6},{8,15},{9,8},{10,9... | collective-permute-start | bytes 98312 | tf_op jit(solution)/shard_map/ppermute | solution.py:593
  17.2 2.4 %collective-permute-start.3 = (bf16[304,256]{1,0:T(8,128)(2,1)S(1)}, bf16[304,256]{1,0:T(8,128)(2,1)S(1)}, u32[]{:S(2)}, u32[]{:S(2)}) collective-permute-start(bf16[304,256]{1,0:T(8,128)(2,1)S(1)} %get-tuple-element.36.w0), channel_id=1, source_target_pairs={{0,8},{8,0},{16,24},{24,16},{1,9},{9,1},{17,25},{25,17},{2,10},{10... | collective-permute-start | bytes 466952 | tf_op jit(solution)/shard_map/ppermute | solution.py:598
  19.6 1.4 %collective-permute-start.4 = (bf16[304,256]{1,0:T(8,128)(2,1)S(1)}, bf16[304,256]{1,0:T(8,128)(2,1)S(1)}, u32[]{:S(2)}, u32[]{:S(2)}) collective-permute-start(bf16[304,256]{1,0:T(8,128)(2,1)S(1)} %collective-permute-done.w2), channel_id=1, source_target_pairs={{0,8},{8,0},{16,24},{24,16},{1,9},{9,1},{17,25},{25,17},{2,10},{10... | collective-permute-start | bytes 466952 | tf_op jit(solution)/shard_map/ppermute | solution.py:598
  52.6 1.5 %collective-permute-start.5 = (bf16[2,432,128]{2,1,0:T(8,128)(2,1)S(1)}, bf16[2,432,128]{2,1,0:T(8,128)(2,1)S(1)}, u32[]{:S(2)}, u32[]{:S(2)}) collective-permute-start(bf16[2,432,128]{2,1,0:T(8,128)(2,1)S(1)} %get-tuple-element.43), channel_id=1, source_target_pairs={{0,8},{8,0},{16,24},{24,16},{1,9},{9,1},{17,25},{25,17},{2,10},{10... | collective-permute-start | bytes 663560 | tf_op jit(solution)/shard_map/ppermute | solution.py:598
  54.2 5.2 %collective-permute-start.6 = (bf16[432,128]{1,0:T(8,128)(2,1)S(1)}, bf16[432,128]{1,0:T(8,128)(2,1)S(1)}, u32[]{:S(2)}, u32[]{:S(2)}) collective-permute-start(bf16[432,128]{1,0:T(8,128)(2,1)S(1)} %slice_bitcast_fusion), channel_id=1, source_target_pairs={{0,16},{8,24},{16,0},{24,8},{1,17},{9,25},{17,1},{25,9},{2,18},{10... | collective-permute-start | bytes 331784 | tf_op jit(solution)/shard_map/ppermute | solution.py:598
  59.4 6.1 %collective-permute-start.7 = (bf16[432,128]{1,0:T(8,128)(2,1)S(1)}, bf16[432,128]{1,0:T(8,128)(2,1)S(1)}, u32[]{:S(2)}, u32[]{:S(2)}) collective-permute-start(bf16[432,128]{1,0:T(8,128)(2,1)S(1)} %fusion), channel_id=1, source_target_pairs={{0,1},{1,0},{2,3},{3,2},{4,5},{5,4},{6,7},{7,6},{8,9},{9,8},{10,11... | collective-permute-start | bytes 331784 | tf_op jit(solution)/shard_map/ppermute | solution.py:598
  60.7 15.7 %all-to-all-start.1 = ((bf16[8,2,32,256]{3,2,1,0:T(8,128)(2,1)}), bf16[8,2,32,256]{3,2,1,0:T(8,128)(2,1)S(1)}, u32[]{:S(2)}, u32[]{:S(2)}) async-start(bf16[8,2,32,256]{3,2,1,0:T(8,128)(2,1)} %get-tuple-element.44), calls=%async_computation.1 | async-start | bytes 524288 | tf_op jit(solution)/shard_map/all_to_all | solution.py:719
  65.6 8.1 %collective-permute-start.8 = (bf16[432,128]{1,0:T(8,128)(2,1)S(1)}, bf16[432,128]{1,0:T(8,128)(2,1)S(1)}, u32[]{:S(2)}, u32[]{:S(2)}) collective-permute-start(bf16[432,128]{1,0:T(8,128)(2,1)S(1)} %add_convert_fusion.2), channel_id=1, source_target_pairs={{0,2},{1,3},{2,0},{3,1},{4,6},{5,7},{6,4},{7,5},{8,10},{9,11},{10,... | collective-permute-start | bytes 331784 | tf_op jit(solution)/shard_map/ppermute | solution.py:598
  73.7 9.4 %collective-permute-start.9 = (bf16[432,128]{1,0:T(8,128)(2,1)S(1)}, bf16[432,128]{1,0:T(8,128)(2,1)S(1)}, u32[]{:S(2)}, u32[]{:S(2)}) collective-permute-start(bf16[432,128]{1,0:T(8,128)(2,1)S(1)} %add_convert_fusion.1.low_ref), channel_id=1, source_target_pairs={{0,4},{1,5},{2,6},{3,7},{4,0},{5,1},{6,2},{7,3},{8,12},{9,13},{10,... | collective-permute-start | bytes 331784 | tf_op jit(solution)/shard_map/ppermute | solution.py:598
  78.0 4.0 %collective-permute-start.12 = (f32[72,256]{1,0:T(8,128)S(1)}, f32[72,256]{1,0:T(8,128)S(1)}, u32[]{:S(2)}, u32[]{:S(2)}) collective-permute-start(f32[72,256]{1,0:T(8,128)S(1)} %project.1.n0), channel_id=1, source_target_pairs={{0,24},{8,16},{16,8},{24,0},{1,25},{9,17},{17,9},{25,1},{2,26},{10... | collective-permute-start | bytes 221192 | tf_op jit(solution)/shard_map/ppermute | solution.py:598
  78.0 5.2 %collective-permute-start.11 = (f32[72,256]{1,0:T(8,128)S(1)}, f32[72,256]{1,0:T(8,128)S(1)}, u32[]{:S(2)}, u32[]{:S(2)}) collective-permute-start(f32[72,256]{1,0:T(8,128)S(1)} %project.1.n0), channel_id=1, source_target_pairs={{0,16},{8,24},{16,0},{24,8},{1,17},{9,25},{17,1},{25,9},{2,18},{10... | collective-permute-start | bytes 221192 | tf_op jit(solution)/shard_map/ppermute | solution.py:598
  78.6 4.6 %collective-permute-start.10 = (f32[72,256]{1,0:T(8,128)S(1)}, f32[72,256]{1,0:T(8,128)S(1)}, u32[]{:S(2)}, u32[]{:S(2)}) collective-permute-start(f32[72,256]{1,0:T(8,128)S(1)} %project.1.n0), channel_id=1, source_target_pairs={{0,8},{8,0},{16,24},{24,16},{1,9},{9,1},{17,25},{25,17},{2,10},{10... | collective-permute-start | bytes 221192 | tf_op jit(solution)/shard_map/ppermute | solution.py:598

commit v5 on v4

--- a/solution.py
+++ b/solution.py
@@ -230,7 +230,7 @@
 
     wfirst = wf_ref[:, 0:32]
     n = h + 2 * (DEEP - 1)
-    count, size = blocks(n)
+    count, size = blocks(n, 60)
 
     def first_block(k, _):
         top = k * size - (DEEP - 1)
@@ -273,7 +273,7 @@
         rows_through(
             lambda row, l=l: xb[l - 1, row],
             wk_ref[3 * (l - 1) : 3 * l].reshape(192, KW)[:, 0:208],
-            C, 1 + l, h + 2 * (DEEP - 1 - l), 27, done,
+            C, 1 + l, h + 2 * (DEEP - 1 - l), 60, done,
         )
 
     row = lax.broadcasted_iota(jnp.int32, (32, KW), 0)
@@ -736,8 +736,10 @@
     while 2 * bit < space:
         low = (low.astype(f32) + swapped(low, "space", bit).astype(f32)).astype(bf16)
         bit *= 2
+    low, _ = lax.optimization_barrier((low, new_own))
+    new_across = swapped(new_own, "chan", 2)
     other = swapped(low, "space", bit)
-    news = [new_own] + [swapped(new_own, "chan", k) for k in (1, 2, 3)]
+    news = [new_own, swapped(new_own, "chan", 1), new_across, swapped(new_across, "chan", 1)]
 
     new_velocity, w_first_grad, b_first_grad, w_mid_grad, b_mid_grad, w_last_grad, b_last_grad, rms_stats = pl.pallas_call(
         functools.partial(finish_kernel, h, 2 * traj * ny * nx),

time: 84.4 us -> 78.8 us (0.934)
  waiting for transfers between devices: 18 us -> 14.4 us
  Pallas kernels: 35.4 us -> 33.5 us
    ppermute x11, waiting for transfers between devices: 15.6 us -> 11.7 us  [swapped(): return lax.ppermute(x, axis, [(i, i ^ bit) for i in range(n)])]
    pallas_call x1, Pallas kernels: 31.6 us -> 29.7 us  [per_device(): pl.pallas_call(functools.partial(step_kernel, h), out_shape=[inside((spac...]
  transfers between devices with their start and end apart: 15 -> 15, of which waited for: 7 -> 9; matrix products, arithmetic and copies ran while one was open for 0% -> 0% of each run, Pallas kernels for 3% -> 4%
where the time goes in v5:
time: 78.8 us; the launch traced here: 78.4 us
  Pallas kernels  33.5 us (43%)
  starting transfers between devices  27.9 us (35%)
  waiting for transfers between devices  14.4 us (18%)
  local copies, waits for them, and re-layouts  1.69 us (2%)
    pallas_call x1, Pallas kernels, per_device(): pl.pallas_call(functools.partial(step_kernel, h), out_shape=[inside((spac...  29.7 us
    ppermute x11, waiting for transfers between devices, swapped(): return lax.ppermute(x, axis, [(i, i ^ bit) for i in range(n)])  11.7 us
    ppermute x11, starting transfers between devices, swapped(): return lax.ppermute(x, axis, [(i, i ^ bit) for i in range(n)])  11.4 us
    all_to_all x1, starting transfers between devices, per_device(): cot_full = lax.all_to_all(cot_all, 'space', 0, 0, tiled=True)  7.28 us
    ppermute x2, starting transfers between devices, moved(): return lax.ppermute(x, axis, [(i, (i + step) % n) for i in range(n)])  4.72 us
    all_to_all x1, starting transfers between devices, per_device(): everywhere = lax.all_to_all(prov, 'space', 0, 0, tiled=True)  4.56 us
    ppermute x2, waiting for transfers between devices, moved(): return lax.ppermute(x, axis, [(i, (i + step) % n) for i in range(n)])  2.37 us
  transfers between devices with their start and end apart: 15, of which 9 were waited for; matrix products, arithmetic and copies ran while one was open for 0% of the time, Pallas kernels for 4%

profile of v5, /device:TPU:0, one launch (start us, length us, event | category | flops | bytes accessed | tf_op | source)
XLA Modules:
  0.0 78.4 jit_solution(10456922980072267826)
XLA Ops:
  0.7 0.9 %copy-done = f32[2,4,32,256]{3,2,1,0:T(8,128)S(1)} copy-done((f32[2,4,32,256]{3,2,1,0:T(8,128)S(1)}, f32[2,4,32,256]{3,2,1,0:T(8,128)}, u32[]{:S(2)}) %copy-start) | copy-done | bytes 262168
  1.6 0.7 broadcast_in_dim.17
  2.3 7.3 %all-to-all-start = ((bf16[8,2,32,256]{3,2,1,0:T(8,128)(2,1)}), bf16[8,2,32,256]{3,2,1,0:T(8,128)(2,1)S(1)}, u32[]{:S(2)}, u32[]{:S(2)}) async-start(bf16[8,2,32,256]{3,2,1,0:T(8,128)(2,1)} %broadcast_in_dim.17), calls=%async_computation | async-start | bytes 524288 | tf_op jit(solution)/shard_map/all_to_all | solution.py:677
  9.6 1.3 %prepare.1 = (bf16[304,256]{1,0:T(8,128)(2,1)S(1)}, f32[2,32,256]{2,1,0:T(8,128)S(1)}, f32[2,16,256]{2,1,0:T(8,128)S(1)}, f32[2,16,256]{2,1,0:T(8,128)S(1)}) custom-call(f32[2,4,32,256]{3,2,1,0:T(8,128)} %vel_ref.1, bf16[5,3,3,16,64]{4,3,2,1,0:T(8,128)(2,1)} %bitcast.21, bf16[3,3,8,64]{3,2,1,0:T(8,128)(2,1)} %bitcast.22, bf16[3,3,2,16]{3,2,1,0:T(2,128)(2,1)} %wf_ref.1, ...), custom_call_target="tpu_custom_call" | custom-call | tf_op jit(solution)/shard_map/prepare/pallas_call | solution.py:650
  10.9 1.6 %collective-permute-start = (bf16[304,256]{1,0:T(8,128)(2,1)S(1)}, bf16[304,256]{1,0:T(8,128)(2,1)S(1)}, u32[]{:S(2)}, u32[]{:S(2)}) collective-permute-start(bf16[304,256]{1,0:T(8,128)(2,1)S(1)} %get-tuple-element.37.w0), channel_id=1, source_target_pairs={{0,16},{8,24},{16,0},{24,8},{1,17},{9,25},{17,1},{25,9},{2,18},{10... | collective-permute-start | bytes 466952 | tf_op jit(solution)/shard_map/ppermute | solution.py:598
  12.5 2.0 %collective-permute-start.1 = (f32[2,16,256]{2,1,0:T(8,128)S(1)}, f32[2,16,256]{2,1,0:T(8,128)S(1)}, u32[]{:S(2)}, u32[]{:S(2)}) collective-permute-start(f32[2,16,256]{2,1,0:T(8,128)S(1)} %get-tuple-element.38), channel_id=1, source_target_pairs={{0,1},{1,2},{2,3},{3,4},{4,5},{5,6},{6,7},{7,0},{8,9},{9,10},{10,1... | collective-permute-start | bytes 98312 | tf_op jit(solution)/shard_map/ppermute | solution.py:593
  14.5 2.7 %collective-permute-start.2 = (f32[2,16,256]{2,1,0:T(8,128)S(1)}, f32[2,16,256]{2,1,0:T(8,128)S(1)}, u32[]{:S(2)}, u32[]{:S(2)}) collective-permute-start(f32[2,16,256]{2,1,0:T(8,128)S(1)} %get-tuple-element.39), channel_id=1, source_target_pairs={{0,7},{1,0},{2,1},{3,2},{4,3},{5,4},{6,5},{7,6},{8,15},{9,8},{10,9... | collective-permute-start | bytes 98312 | tf_op jit(solution)/shard_map/ppermute | solution.py:593
  17.2 2.4 %collective-permute-done.1.up_ref = f32[2,16,256]{2,1,0:T(8,128)S(1)} collective-permute-done((f32[2,16,256]{2,1,0:T(8,128)S(1)}, f32[2,16,256]{2,1,0:T(8,128)S(1)}, u32[]{:S(2)}, u32[]{:S(2)}) %collective-permute-start.1) | collective-permute-done | bytes 32800 | tf_op jit(solution)/shard_map/ppermute | solution.py:593
  19.6 1.4 %collective-permute-done.4.w3 = bf16[304,256]{1,0:T(8,128)(2,1)S(1)} collective-permute-done((bf16[304,256]{1,0:T(8,128)(2,1)S(1)}, bf16[304,256]{1,0:T(8,128)(2,1)S(1)}, u32[]{:S(2)}, u32[]{:S(2)}) %collective-permute-start.4) | collective-permute-done | bytes 155680 | tf_op jit(solution)/shard_map/ppermute | solution.py:598
  21.0 29.7 %step.1 = (bf16[8,2,32,256]{3,2,1,0:T(8,128)(2,1)}, f32[2,32,256]{2,1,0:T(8,128)}, bf16[2,432,128]{2,1,0:T(8,128)(2,1)S(1)}, bf16[2,432,128]{2,1,0:T(8,128)(2,1)...) custom-call(f32[2,32,256]{2,1,0:T(8,128)S(1)} %get-tuple-element.36., ...), custom_call_target="tpu_custom_call" | custom-call | flops 22196256768 | bytes 33554432 | tf_op jit(solution)/shard_map/step/pallas_call | solution.py:684
  50.9 1.3 %collective-permute-done.5 = bf16[2,432,128]{2,1,0:T(8,128)(2,1)S(1)} collective-permute-done((bf16[2,432,128]{2,1,0:T(8,128)(2,1)S(1)}, bf16[2,432,128]{2,1,0:T(8,128)(2,1)S(1)}, u32[]{:S(2)}, u32[]{:S(2)}) %collective-permute-start.5) | collective-permute-done | bytes 221216 | tf_op jit(solution)/shard_map/ppermute | solution.py:598
  52.4 1.6 %collective-permute-start.6 = (bf16[432,128]{1,0:T(8,128)(2,1)S(1)}, bf16[432,128]{1,0:T(8,128)(2,1)S(1)}, u32[]{:S(2)}, u32[]{:S(2)}) collective-permute-start(bf16[432,128]{1,0:T(8,128)(2,1)S(1)} %slice_bitcast_fusion), channel_id=1, source_target_pairs={{0,16},{8,24},{16,0},{24,8},{1,17},{9,25},{17,1},{25,9},{2,18},{10... | collective-permute-start | bytes 331784 | tf_op jit(solution)/shard_map/ppermute | solution.py:598
  53.9 4.6 %all-to-all-start.1 = ((bf16[8,2,32,256]{3,2,1,0:T(8,128)(2,1)}), bf16[8,2,32,256]{3,2,1,0:T(8,128)(2,1)S(1)}, u32[]{:S(2)}, u32[]{:S(2)}) async-start(bf16[8,2,32,256]{3,2,1,0:T(8,128)(2,1)} %get-tuple-element.45), calls=%async_computation.1 | async-start | bytes 524288 | tf_op jit(solution)/shard_map/all_to_all | solution.py:719
  58.5 2.1 %collective-permute-start.7 = (bf16[432,128]{1,0:T(8,128)(2,1)S(1)}, bf16[432,128]{1,0:T(8,128)(2,1)S(1)}, u32[]{:S(2)}, u32[]{:S(2)}) collective-permute-start(bf16[432,128]{1,0:T(8,128)(2,1)S(1)} %fusion), channel_id=1, source_target_pairs={{0,1},{1,0},{2,3},{3,2},{4,5},{5,4},{6,7},{7,6},{8,9},{9,8},{10,11... | collective-permute-start | bytes 331784 | tf_op jit(solution)/shard_map/ppermute | solution.py:598
  60.6 5.0 %collective-permute-done.7 = bf16[432,128]{1,0:T(8,128)(2,1)S(1)} collective-permute-done((bf16[432,128]{1,0:T(8,128)(2,1)S(1)}, bf16[432,128]{1,0:T(8,128)(2,1)S(1)}, u32[]{:S(2)}, u32[]{:S(2)}) %collective-permute-start.7) | collective-permute-done | bytes 110624 | tf_op jit(solution)/shard_map/ppermute | solution.py:598
  65.6 1.7 %collective-permute-start.8 = (bf16[432,128]{1,0:T(8,128)(2,1)S(1)}, bf16[432,128]{1,0:T(8,128)(2,1)S(1)}, u32[]{:S(2)}, u32[]{:S(2)}) collective-permute-start(bf16[432,128]{1,0:T(8,128)(2,1)S(1)} %add_convert_fusion.2), channel_id=1, source_target_pairs={{0,2},{1,3},{2,0},{3,1},{4,6},{5,7},{6,4},{7,5},{8,10},{9,11},{10,... | collective-permute-start | bytes 331784 | tf_op jit(solution)/shard_map/ppermute | solution.py:598
  67.3 0.3 all-to-all-done.1.prov_ref
  67.5 1.6 %project.1.n0 = f32[72,256]{1,0:T(8,128)S(1)} custom-call(bf16[8,2,32,256]{3,2,1,0:T(8,128)(2,1)S(1)} %all-to-all-done.1.prov_ref, f32[256,256]{1,0:T(8,128)S(1)} %get-tuple-element.46.tx_ref, f32[256,256]{1,0:T(8,128)S(1)} %get-tuple-element.47.ty_ref, f32[256,256]{1,0:T(8,128)S(1)} %get-tuple-element.48.back_ref, ...), custom_call_target="tpu_custom_call" | custom-call | flops 2147483648 | bytes 4194304 | tf_op jit(solution)/shard_map/project/pallas_call | solution.py:723
  69.1 1.5 %collective-permute-start.11 = (f32[72,256]{1,0:T(8,128)S(1)}, f32[72,256]{1,0:T(8,128)S(1)}, u32[]{:S(2)}, u32[]{:S(2)}) collective-permute-start(f32[72,256]{1,0:T(8,128)S(1)} %project.1.n0), channel_id=1, source_target_pairs={{0,16},{8,24},{16,0},{24,8},{1,17},{9,25},{17,1},{25,9},{2,18},{10... | collective-permute-start | bytes 221192 | tf_op jit(solution)/shard_map/ppermute | solution.py:598
  70.6 2.6 %collective-permute-start.9 = (bf16[432,128]{1,0:T(8,128)(2,1)S(1)}, bf16[432,128]{1,0:T(8,128)(2,1)S(1)}, u32[]{:S(2)}, u32[]{:S(2)}) collective-permute-start(bf16[432,128]{1,0:T(8,128)(2,1)S(1)} %add_convert_fusion.1.low_ref), channel_id=1, source_target_pairs={{0,4},{1,5},{2,6},{3,7},{4,0},{5,1},{6,2},{7,3},{8,12},{9,13},{10,... | collective-permute-start | bytes 331784 | tf_op jit(solution)/shard_map/ppermute | solution.py:598
  73.7 0.8 collective-permute-done.10.n1
  74.5 0.3 collective-permute-done.12.n3
  74.7 2.8 %collective-permute-done.9.other_ref = bf16[432,128]{1,0:T(8,128)(2,1)S(1)} collective-permute-done((bf16[432,128]{1,0:T(8,128)(2,1)S(1)}, bf16[432,128]{1,0:T(8,128)(2,1)S(1)}, u32[]{:S(2)}, u32[]{:S(2)}) %collective-permute-start.9) | collective-permute-done | bytes 110624 | tf_op jit(solution)/shard_map/ppermute | solution.py:598
  77.5 0.9 %finish.1 = (f32[2,4,32,256]{3,2,1,0:T(8,128)}, f32[3,3,2,16]{3,2,1,0:T(2,128)}, f32[1,16]{1,0:T(1,128)}, f32[5,3,3,16,64]{4,3,2,1,0:T(8,128)}, f32[5,16]{1,0:T(...) custom-call(bf16[432,128]{1,0:T(8,128)(2,1)S(1)} %add_convert_fusion.1.low_ref, ...), custom_call_target="tpu_custom_call" | custom-call | tf_op jit(solution)/shard_map/finish/pallas_call | solution.py:744
  (19 shorter events, 0.9 us)
Async XLA Ops:
  0.6 1.0 %copy-start = (f32[2,4,32,256]{3,2,1,0:T(8,128)S(1)}, f32[2,4,32,256]{3,2,1,0:T(8,128)}, u32[]{:S(2)}) copy-start(f32[2,4,32,256]{3,2,1,0:T(8,128)} %param.24) | copy-start | bytes 786436
  2.3 18.6 %all-to-all-start = ((bf16[8,2,32,256]{3,2,1,0:T(8,128)(2,1)}), bf16[8,2,32,256]{3,2,1,0:T(8,128)(2,1)S(1)}, u32[]{:S(2)}, u32[]{:S(2)}) async-start(bf16[8,2,32,256]{3,2,1,0:T(8,128)(2,1)} %broadcast_in_dim.17), calls=%async_computation | async-start | bytes 524288 | tf_op jit(solution)/shard_map/all_to_all | solution.py:677
  10.9 8.7 %collective-permute-start = (bf16[304,256]{1,0:T(8,128)(2,1)S(1)}, bf16[304,256]{1,0:T(8,128)(2,1)S(1)}, u32[]{:S(2)}, u32[]{:S(2)}) collective-permute-start(bf16[304,256]{1,0:T(8,128)(2,1)S(1)} %get-tuple-element.37.w0), channel_id=1, source_target_pairs={{0,16},{8,24},{16,0},{24,8},{1,17},{9,25},{17,1},{25,9},{2,18},{10... | collective-permute-start | bytes 466952 | tf_op jit(solution)/shard_map/ppermute | solution.py:598
  12.5 7.1 %collective-permute-start.1 = (f32[2,16,256]{2,1,0:T(8,128)S(1)}, f32[2,16,256]{2,1,0:T(8,128)S(1)}, u32[]{:S(2)}, u32[]{:S(2)}) collective-permute-start(f32[2,16,256]{2,1,0:T(8,128)S(1)} %get-tuple-element.38), channel_id=1, source_target_pairs={{0,1},{1,2},{2,3},{3,4},{4,5},{5,6},{6,7},{7,0},{8,9},{9,10},{10,1... | collective-permute-start | bytes 98312 | tf_op jit(solution)/shard_map/ppermute | solution.py:593
  14.5 5.1 %collective-permute-start.2 = (f32[2,16,256]{2,1,0:T(8,128)S(1)}, f32[2,16,256]{2,1,0:T(8,128)S(1)}, u32[]{:S(2)}, u32[]{:S(2)}) collective-permute-start(f32[2,16,256]{2,1,0:T(8,128)S(1)} %get-tuple-element.39), channel_id=1, source_target_pairs={{0,7},{1,0},{2,1},{3,2},{4,3},{5,4},{6,5},{7,6},{8,15},{9,8},{10,9... | collective-permute-start | bytes 98312 | tf_op jit(solution)/shard_map/ppermute | solution.py:593
  17.2 2.4 %collective-permute-start.3 = (bf16[304,256]{1,0:T(8,128)(2,1)S(1)}, bf16[304,256]{1,0:T(8,128)(2,1)S(1)}, u32[]{:S(2)}, u32[]{:S(2)}) collective-permute-start(bf16[304,256]{1,0:T(8,128)(2,1)S(1)} %get-tuple-element.37.w0), channel_id=1, source_target_pairs={{0,8},{8,0},{16,24},{24,16},{1,9},{9,1},{17,25},{25,17},{2,10},{10... | collective-permute-start | bytes 466952 | tf_op jit(solution)/shard_map/ppermute | solution.py:598
  19.6 1.4 %collective-permute-start.4 = (bf16[304,256]{1,0:T(8,128)(2,1)S(1)}, bf16[304,256]{1,0:T(8,128)(2,1)S(1)}, u32[]{:S(2)}, u32[]{:S(2)}) collective-permute-start(bf16[304,256]{1,0:T(8,128)(2,1)S(1)} %collective-permute-done.w2), channel_id=1, source_target_pairs={{0,8},{8,0},{16,24},{24,16},{1,9},{9,1},{17,25},{25,17},{2,10},{10... | collective-permute-start | bytes 466952 | tf_op jit(solution)/shard_map/ppermute | solution.py:598
  50.7 1.5 %collective-permute-start.5 = (bf16[2,432,128]{2,1,0:T(8,128)(2,1)S(1)}, bf16[2,432,128]{2,1,0:T(8,128)(2,1)S(1)}, u32[]{:S(2)}, u32[]{:S(2)}) collective-permute-start(bf16[2,432,128]{2,1,0:T(8,128)(2,1)S(1)} %get-tuple-element.44), channel_id=1, source_target_pairs={{0,8},{8,0},{16,24},{24,16},{1,9},{9,1},{17,25},{25,17},{2,10},{10... | collective-permute-start | bytes 663560 | tf_op jit(solution)/shard_map/ppermute | solution.py:598
  52.4 6.1 %collective-permute-start.6 = (bf16[432,128]{1,0:T(8,128)(2,1)S(1)}, bf16[432,128]{1,0:T(8,128)(2,1)S(1)}, u32[]{:S(2)}, u32[]{:S(2)}) collective-permute-start(bf16[432,128]{1,0:T(8,128)(2,1)S(1)} %slice_bitcast_fusion), channel_id=1, source_target_pairs={{0,16},{8,24},{16,0},{24,8},{1,17},{9,25},{17,1},{25,9},{2,18},{10... | collective-permute-start | bytes 331784 | tf_op jit(solution)/shard_map/ppermute | solution.py:598
  53.9 13.6 %all-to-all-start.1 = ((bf16[8,2,32,256]{3,2,1,0:T(8,128)(2,1)}), bf16[8,2,32,256]{3,2,1,0:T(8,128)(2,1)S(1)}, u32[]{:S(2)}, u32[]{:S(2)}) async-start(bf16[8,2,32,256]{3,2,1,0:T(8,128)(2,1)} %get-tuple-element.45), calls=%async_computation.1 | async-start | bytes 524288 | tf_op jit(solution)/shard_map/all_to_all | solution.py:719
  58.5 7.0 %collective-permute-start.7 = (bf16[432,128]{1,0:T(8,128)(2,1)S(1)}, bf16[432,128]{1,0:T(8,128)(2,1)S(1)}, u32[]{:S(2)}, u32[]{:S(2)}) collective-permute-start(bf16[432,128]{1,0:T(8,128)(2,1)S(1)} %fusion), channel_id=1, source_target_pairs={{0,1},{1,0},{2,3},{3,2},{4,5},{5,4},{6,7},{7,6},{8,9},{9,8},{10,11... | collective-permute-start | bytes 331784 | tf_op jit(solution)/shard_map/ppermute | solution.py:598
  65.6 5.0 %collective-permute-start.8 = (bf16[432,128]{1,0:T(8,128)(2,1)S(1)}, bf16[432,128]{1,0:T(8,128)(2,1)S(1)}, u32[]{:S(2)}, u32[]{:S(2)}) collective-permute-start(bf16[432,128]{1,0:T(8,128)(2,1)S(1)} %add_convert_fusion.2), channel_id=1, source_target_pairs={{0,2},{1,3},{2,0},{3,1},{4,6},{5,7},{6,4},{7,5},{8,10},{9,11},{10,... | collective-permute-start | bytes 331784 | tf_op jit(solution)/shard_map/ppermute | solution.py:598
  69.1 4.4 %collective-permute-start.11 = (f32[72,256]{1,0:T(8,128)S(1)}, f32[72,256]{1,0:T(8,128)S(1)}, u32[]{:S(2)}, u32[]{:S(2)}) collective-permute-start(f32[72,256]{1,0:T(8,128)S(1)} %project.1.n0), channel_id=1, source_target_pairs={{0,16},{8,24},{16,0},{24,8},{1,17},{9,25},{17,1},{25,9},{2,18},{10... | collective-permute-start | bytes 221192 | tf_op jit(solution)/shard_map/ppermute | solution.py:598
  70.6 6.9 %collective-permute-start.9 = (bf16[432,128]{1,0:T(8,128)(2,1)S(1)}, bf16[432,128]{1,0:T(8,128)(2,1)S(1)}, u32[]{:S(2)}, u32[]{:S(2)}) collective-permute-start(bf16[432,128]{1,0:T(8,128)(2,1)S(1)} %add_convert_fusion.1.low_ref), channel_id=1, source_target_pairs={{0,4},{1,5},{2,6},{3,7},{4,0},{5,1},{6,2},{7,3},{8,12},{9,13},{10,... | collective-permute-start | bytes 331784 | tf_op jit(solution)/shard_map/ppermute | solution.py:598
  73.2 1.3 %collective-permute-start.10 = (f32[72,256]{1,0:T(8,128)S(1)}, f32[72,256]{1,0:T(8,128)S(1)}, u32[]{:S(2)}, u32[]{:S(2)}) collective-permute-start(f32[72,256]{1,0:T(8,128)S(1)} %project.1.n0), channel_id=1, source_target_pairs={{0,8},{8,0},{16,24},{24,16},{1,9},{9,1},{17,25},{25,17},{2,10},{10... | collective-permute-start | bytes 221192 | tf_op jit(solution)/shard_map/ppermute | solution.py:598
  73.5 1.3 %collective-permute-start.12 = (f32[72,256]{1,0:T(8,128)S(1)}, f32[72,256]{1,0:T(8,128)S(1)}, u32[]{:S(2)}, u32[]{:S(2)}) collective-permute-start(f32[72,256]{1,0:T(8,128)S(1)} %collective-permute-done.11.n2), channel_id=1, source_target_pairs={{0,8},{8,0},{16,24},{24,16},{1,9},{9,1},{17,25},{25,17},{2,10},{10... | collective-permute-start | bytes 221192 | tf_op jit(solution)/shard_map/ppermute | solution.py:598

commit v6 on v5

--- a/solution.py
+++ b/solution.py
@@ -95,10 +95,12 @@
     ny = field_ref.shape[0] * h if h % 8 == 0 else field_ref.shape[0] // 2
     if h % 8 == 0:
         fields = [field_ref[:, c].reshape(ny, KW) for c in range(2)]
-        field = jnp.concatenate(fields, axis=0).astype(f32)
+        field = jnp.concatenate(fields, axis=0)
     else:
-        field = field_ref[...].astype(f32)
-    along = product(halves(field), halves(tx_ref[...]))
+        field = field_ref[...]
+    along = sum(
+        jnp.dot(field, part, preferred_element_type=f32) for part in halves(tx_ref[...])[::-1]
+    )
     table = halves(ty_ref[...])
     if h % 8 == 0:
         return [product(table, halves(along[c * ny : (c + 1) * ny])) for c in range(2)]
@@ -180,7 +182,7 @@
 
 
 def step_kernel(
-    h, vel_ref, up_ref, down_ref, w0, w1, w2, w3, offs_ref,
+    h, vel_ref, up_ref, down_ref, w0, w1, w2, w3, perm_ref,
     cot_ref, *rest,
 ):
     held = rest[:7]
@@ -210,7 +212,7 @@
             block = piece[MIDROWS + j * 16 : MIDROWS + j * 16 + 16].astype(f32)
             w7k[j, at8, :] = block[0:8]
         wf_ref[at16, :] = piece[MIDROWS + 48 : MIDROWS + 64]
-    perm = point_order(offs_ref[...])
+    perm = perm_ref[...]
     perm_low = perm.astype(bf16)
     for i in range(3):
         w7_ref[i] = jnp.dot(perm_low, w7k[i].astype(bf16), preferred_element_type=f32).astype(bf16)
@@ -504,13 +506,14 @@
     out_ref[2 * h :] = jnp.full((8, KW), jnp.sum(u * u) + jnp.sum(v * v), f32)
 
 
-def prepare_kernel(h, vel_ref, wm_ref, wl_ref, wf_ref, bm_ref, bf_ref, bl_ref, pack_ref, own_ref, top_ref, bottom_ref, tall, wide):
+def prepare_kernel(h, vel_ref, wm_ref, wl_ref, wf_ref, bm_ref, bf_ref, bl_ref, offs_ref, pack_ref, own_ref, top_ref, bottom_ref, perm_ref, tall, wide):
     me = lax.axis_index("chan")
     own = vel_ref[:, me]
     own_ref[...] = own
     if h >= HALO:
         top_ref[...] = own[:, :HALO]
         bottom_ref[...] = own[:, h - HALO :]
+    perm_ref[...] = point_order(offs_ref[...])
     wide[...] = jnp.zeros_like(wide)
     wide[0:NL, 0:16] = bm_ref[...].astype(f32)
     wide[NL : NL + 1, 0:16] = bf_ref[...].astype(f32)
@@ -647,16 +650,17 @@
 
     own_cot = lax.dynamic_index_in_dim(cotangent, me_chan, 1, keepdims=False).astype(bf16)
     cot_all = jnp.broadcast_to(own_cot[None], (space,) + own_cot.shape)
-    packed, own, top, bottom = pl.pallas_call(
+    packed, own, top, bottom, perm = pl.pallas_call(
         functools.partial(prepare_kernel, h),
         out_shape=[
             inside((MIDROWS + 64, KW), bf16),
             inside((2, h, nx), f32),
             inside((2, min(h, HALO), nx), f32),
             inside((2, min(h, HALO), nx), f32),
+            inside((32, 32), f32),
         ],
-        in_specs=vmem(7),
-        out_specs=vmem(4),
+        in_specs=vmem(8),
+        out_specs=vmem(5),
         scratch_shapes=[pltpu.VMEM((128, 128), f32), pltpu.VMEM((8, 128), f32)],
         compiler_params=limit(16),
         name="prepare",
@@ -665,7 +669,7 @@
             outside(x)
             for x in (
                 velocity, jnp.swapaxes(w_mid, 3, 4), jnp.swapaxes(w_last, 2, 3),
-                w_first, b_mid, b_first[None], b_last[None],
+                w_first, b_mid, b_first[None], b_last[None], offsets,
             )
         ],
     )
@@ -683,7 +687,7 @@
     places = [inside(x.shape[1:] if k == 3 else x.shape, f32) for k, x in enumerate(constants)]
     prov, vel_grad, keep, send, *constants = pl.pallas_call(
         functools.partial(step_kernel, h),
-        out_shape=[inside((space, 2, h, nx), bf16), shape((2, h, nx), f32)]
+        out_shape=[inside((space, 2, h, nx), bf16), inside((2, h, nx), f32)]
         + [inside((2, SUMROWS, 128), bf16)] * 2
         + places,
         in_specs=vmem(9) + [pl.BlockSpec(memory_space=pl.ANY)] * 7,
@@ -715,7 +719,7 @@
             flops=6 * 7 * deep * nx * 9 * C * C, bytes_accessed=2**25, transcendentals=6 * deep * nx * C
         ),
         name="step",
-    )(own, up, down, packed, beside, across, diagonal, outside(offsets), cot_full, *constants)
+    )(own, up, down, packed, beside, across, diagonal, perm, cot_full, *constants)
     everywhere = lax.all_to_all(prov, "space", 0, 0, tiled=True)
     if h % 8:
         everywhere = everywhere.reshape(space * 2 * h, nx)

time: 78.8 us -> 77.6 us (0.985)
  Pallas kernels: 33.5 us -> 32.3 us
  waiting for transfers between devices: 14.4 us -> 13.4 us
    pallas_call x1, Pallas kernels: 29.7 us -> 28.6 us  [per_device(): pl.pallas_call(functools.partial(step_kernel, h), out_shape=[inside((spac...]
    ppermute x11, waiting for transfers between devices: 11.7 us -> 10.8 us  [swapped(): return lax.ppermute(x, axis, [(i, i ^ bit) for i in range(n)])]
  transfers between devices with their start and end apart: 15 -> 15, of which waited for: 9 -> 9; matrix products, arithmetic and copies ran while one was open for 0% -> 1% of each run, Pallas kernels for 4% -> 4%
where the time goes in v6:
time: 77.6 us; the launch traced here: 77.2 us
  Pallas kernels  32.3 us (42%)
  starting transfers between devices  28.3 us (36%)
  waiting for transfers between devices  13.4 us (17%)
  local copies, waits for them, and re-layouts  2.32 us (3%)
    pallas_call x1, Pallas kernels, per_device(): pl.pallas_call(functools.partial(step_kernel, h), out_shape=[inside((spac...  28.6 us
    ppermute x11, starting transfers between devices, swapped(): return lax.ppermute(x, axis, [(i, i ^ bit) for i in range(n)])  11.7 us
    ppermute x11, waiting for transfers between devices, swapped(): return lax.ppermute(x, axis, [(i, i ^ bit) for i in range(n)])  10.8 us
    all_to_all x1, starting transfers between devices, per_device(): cot_full = lax.all_to_all(cot_all, 'space', 0, 0, tiled=True)  7.28 us
    ppermute x2, starting transfers between devices, moved(): return lax.ppermute(x, axis, [(i, (i + step) % n) for i in range(n)])  4.72 us
    all_to_all x1, starting transfers between devices, per_device(): everywhere = lax.all_to_all(prov, 'space', 0, 0, tiled=True)  4.56 us
    ppermute x2, waiting for transfers between devices, moved(): return lax.ppermute(x, axis, [(i, (i + step) % n) for i in range(n)])  2.36 us
    unnamed x3, local copies, waits for them, and re-layouts  1.57 us
  transfers between devices with their start and end apart: 15, of which 9 were waited for; matrix products, arithmetic and copies ran while one was open for 1% of the time, Pallas kernels for 4%

profile of v6, /device:TPU:0, one launch (start us, length us, event | category | flops | bytes accessed | tf_op | source)
XLA Modules:
  0.0 77.2 jit_solution(9565001200863481092)
XLA Ops:
  0.7 0.9 %copy-done = f32[2,4,32,256]{3,2,1,0:T(8,128)S(1)} copy-done((f32[2,4,32,256]{3,2,1,0:T(8,128)S(1)}, f32[2,4,32,256]{3,2,1,0:T(8,128)}, u32[]{:S(2)}) %copy-start) | copy-done | bytes 262168
  1.6 0.7 broadcast_in_dim.17
  2.3 7.3 %all-to-all-start = ((bf16[8,2,32,256]{3,2,1,0:T(8,128)(2,1)}), bf16[8,2,32,256]{3,2,1,0:T(8,128)(2,1)S(1)}, u32[]{:S(2)}, u32[]{:S(2)}) async-start(bf16[8,2,32,256]{3,2,1,0:T(8,128)(2,1)} %broadcast_in_dim.17), calls=%async_computation | async-start | bytes 524288 | tf_op jit(solution)/shard_map/all_to_all | solution.py:681
  9.6 1.3 %prepare.1 = (bf16[304,256]{1,0:T(8,128)(2,1)S(1)}, f32[2,32,256]{2,1,0:T(8,128)S(1)}, f32[2,16,256]{2,1,0:T(8,128)S(1)}, f32[2,16,256]{2,1,0:T(8,128)S(1)}, f32[32,32]{1,0:T(8,128)S(1)}) custom-call(f32[2,4,32,256]{3,2,1,0:T(8,128)} %vel_ref.1, bf16[5,3,3,16,64]{4,3,2,1,0:T(8,128)(2,1)} %bitcast.22, bf16[3,3,8,64]{3,2,1,0:T(8,128)(2,1)} %bitcast.23, ...), custom_call_target="tpu_custom_call" | custom-call | tf_op jit(solution)/shard_map/prepare/pallas_call | solution.py:653
  11.0 1.5 %collective-permute-start = (bf16[304,256]{1,0:T(8,128)(2,1)S(1)}, bf16[304,256]{1,0:T(8,128)(2,1)S(1)}, u32[]{:S(2)}, u32[]{:S(2)}) collective-permute-start(bf16[304,256]{1,0:T(8,128)(2,1)S(1)} %get-tuple-element.38.w0), channel_id=1, source_target_pairs={{0,16},{8,24},{16,0},{24,8},{1,17},{9,25},{17,1},{25,9},{2,18},{10... | collective-permute-start | bytes 466952 | tf_op jit(solution)/shard_map/ppermute | solution.py:601
  12.5 2.0 %collective-permute-start.1 = (f32[2,16,256]{2,1,0:T(8,128)S(1)}, f32[2,16,256]{2,1,0:T(8,128)S(1)}, u32[]{:S(2)}, u32[]{:S(2)}) collective-permute-start(f32[2,16,256]{2,1,0:T(8,128)S(1)} %get-tuple-element.39), channel_id=1, source_target_pairs={{0,1},{1,2},{2,3},{3,4},{4,5},{5,6},{6,7},{7,0},{8,9},{9,10},{10,1... | collective-permute-start | bytes 98312 | tf_op jit(solution)/shard_map/ppermute | solution.py:596
  14.5 2.7 %collective-permute-start.2 = (f32[2,16,256]{2,1,0:T(8,128)S(1)}, f32[2,16,256]{2,1,0:T(8,128)S(1)}, u32[]{:S(2)}, u32[]{:S(2)}) collective-permute-start(f32[2,16,256]{2,1,0:T(8,128)S(1)} %get-tuple-element.40), channel_id=1, source_target_pairs={{0,7},{1,0},{2,1},{3,2},{4,3},{5,4},{6,5},{7,6},{8,15},{9,8},{10,9... | collective-permute-start | bytes 98312 | tf_op jit(solution)/shard_map/ppermute | solution.py:596
  17.2 2.4 %collective-permute-done.1.up_ref = f32[2,16,256]{2,1,0:T(8,128)S(1)} collective-permute-done((f32[2,16,256]{2,1,0:T(8,128)S(1)}, f32[2,16,256]{2,1,0:T(8,128)S(1)}, u32[]{:S(2)}, u32[]{:S(2)}) %collective-permute-start.1) | collective-permute-done | bytes 32800 | tf_op jit(solution)/shard_map/ppermute | solution.py:596
  19.6 1.4 %collective-permute-done.4.w3 = bf16[304,256]{1,0:T(8,128)(2,1)S(1)} collective-permute-done((bf16[304,256]{1,0:T(8,128)(2,1)S(1)}, bf16[304,256]{1,0:T(8,128)(2,1)S(1)}, u32[]{:S(2)}, u32[]{:S(2)}) %collective-permute-start.4) | collective-permute-done | bytes 155680 | tf_op jit(solution)/shard_map/ppermute | solution.py:601
  21.0 28.6 %step.1 = (bf16[8,2,32,256]{3,2,1,0:T(8,128)(2,1)}, f32[2,32,256]{2,1,0:T(8,128)S(1)}, bf16[2,432,128]{2,1,0:T(8,128)(2,1)S(1)}, bf16[2,432,128]{2,1,0:T(8,128)(...) custom-call(f32[2,32,256]{2,1,0:T(8,128)S(1)} %get-tuple-element.37., ...), custom_call_target="tpu_custom_call" | custom-call | flops 22196256768 | bytes 33554432 | tf_op jit(solution)/shard_map/step/pallas_call | solution.py:688
  49.8 1.3 %collective-permute-done.5 = bf16[2,432,128]{2,1,0:T(8,128)(2,1)S(1)} collective-permute-done((bf16[2,432,128]{2,1,0:T(8,128)(2,1)S(1)}, bf16[2,432,128]{2,1,0:T(8,128)(2,1)S(1)}, u32[]{:S(2)}, u32[]{:S(2)}) %collective-permute-start.5) | collective-permute-done | bytes 221216 | tf_op jit(solution)/shard_map/ppermute | solution.py:601
  51.2 1.6 %collective-permute-start.6 = (bf16[432,128]{1,0:T(8,128)(2,1)S(1)}, bf16[432,128]{1,0:T(8,128)(2,1)S(1)}, u32[]{:S(2)}, u32[]{:S(2)}) collective-permute-start(bf16[432,128]{1,0:T(8,128)(2,1)S(1)} %slice_bitcast_fusion), channel_id=1, source_target_pairs={{0,16},{8,24},{16,0},{24,8},{1,17},{9,25},{17,1},{25,9},{2,18},{10... | collective-permute-start | bytes 331784 | tf_op jit(solution)/shard_map/ppermute | solution.py:601
  52.8 4.6 %all-to-all-start.1 = ((bf16[8,2,32,256]{3,2,1,0:T(8,128)(2,1)}), bf16[8,2,32,256]{3,2,1,0:T(8,128)(2,1)S(1)}, u32[]{:S(2)}, u32[]{:S(2)}) async-start(bf16[8,2,32,256]{3,2,1,0:T(8,128)(2,1)} %get-tuple-element.47), calls=%async_computation.1 | async-start | bytes 524288 | tf_op jit(solution)/shard_map/all_to_all | solution.py:723
  57.4 2.1 %collective-permute-start.7 = (bf16[432,128]{1,0:T(8,128)(2,1)S(1)}, bf16[432,128]{1,0:T(8,128)(2,1)S(1)}, u32[]{:S(2)}, u32[]{:S(2)}) collective-permute-start(bf16[432,128]{1,0:T(8,128)(2,1)S(1)} %fusion), channel_id=1, source_target_pairs={{0,1},{1,0},{2,3},{3,2},{4,5},{5,4},{6,7},{7,6},{8,9},{9,8},{10,11... | collective-permute-start | bytes 331784 | tf_op jit(solution)/shard_map/ppermute | solution.py:601
  59.5 5.0 %collective-permute-done.7 = bf16[432,128]{1,0:T(8,128)(2,1)S(1)} collective-permute-done((bf16[432,128]{1,0:T(8,128)(2,1)S(1)}, bf16[432,128]{1,0:T(8,128)(2,1)S(1)}, u32[]{:S(2)}, u32[]{:S(2)}) %collective-permute-start.7) | collective-permute-done | bytes 110624 | tf_op jit(solution)/shard_map/ppermute | solution.py:601
  64.5 1.7 %collective-permute-start.8 = (bf16[432,128]{1,0:T(8,128)(2,1)S(1)}, bf16[432,128]{1,0:T(8,128)(2,1)S(1)}, u32[]{:S(2)}, u32[]{:S(2)}) collective-permute-start(bf16[432,128]{1,0:T(8,128)(2,1)S(1)} %add_convert_fusion.2), channel_id=1, source_target_pairs={{0,2},{1,3},{2,0},{3,1},{4,6},{5,7},{6,4},{7,5},{8,10},{9,11},{10,... | collective-permute-start | bytes 331784 | tf_op jit(solution)/shard_map/ppermute | solution.py:601
  66.2 0.3 all-to-all-done.1.prov_ref
  66.4 1.4 %project.1.n0 = f32[72,256]{1,0:T(8,128)S(1)} custom-call(bf16[8,2,32,256]{3,2,1,0:T(8,128)(2,1)S(1)} %all-to-all-done.1.prov_ref, f32[256,256]{1,0:T(8,128)S(1)} %get-tuple-element.48.tx_ref, f32[256,256]{1,0:T(8,128)S(1)} %get-tuple-element.49.ty_ref, f32[256,256]{1,0:T(8,128)S(1)} %get-tuple-element.50.back_ref, ...), custom_call_target="tpu_custom_call" | custom-call | flops 2147483648 | bytes 4194304 | tf_op jit(solution)/shard_map/project/pallas_call | solution.py:727
  67.8 1.5 %collective-permute-start.11 = (f32[72,256]{1,0:T(8,128)S(1)}, f32[72,256]{1,0:T(8,128)S(1)}, u32[]{:S(2)}, u32[]{:S(2)}) collective-permute-start(f32[72,256]{1,0:T(8,128)S(1)} %project.1.n0), channel_id=1, source_target_pairs={{0,16},{8,24},{16,0},{24,8},{1,17},{9,25},{17,1},{25,9},{2,18},{10... | collective-permute-start | bytes 221192 | tf_op jit(solution)/shard_map/ppermute | solution.py:601
  69.4 2.7 %collective-permute-start.9 = (bf16[432,128]{1,0:T(8,128)(2,1)S(1)}, bf16[432,128]{1,0:T(8,128)(2,1)S(1)}, u32[]{:S(2)}, u32[]{:S(2)}) collective-permute-start(bf16[432,128]{1,0:T(8,128)(2,1)S(1)} %add_convert_fusion.1.low_ref), channel_id=1, source_target_pairs={{0,4},{1,5},{2,6},{3,7},{4,0},{5,1},{6,2},{7,3},{8,12},{9,13},{10,... | collective-permute-start | bytes 331784 | tf_op jit(solution)/shard_map/ppermute | solution.py:601
  72.2 0.4 collective-permute-start.12
  72.6 0.6 copy.26
  73.5 2.7 %collective-permute-done.9.other_ref = bf16[432,128]{1,0:T(8,128)(2,1)S(1)} collective-permute-done((bf16[432,128]{1,0:T(8,128)(2,1)S(1)}, bf16[432,128]{1,0:T(8,128)(2,1)S(1)}, u32[]{:S(2)}, u32[]{:S(2)}) %collective-permute-start.9) | collective-permute-done | bytes 110624 | tf_op jit(solution)/shard_map/ppermute | solution.py:601
  76.3 0.9 %finish.1 = (f32[2,4,32,256]{3,2,1,0:T(8,128)}, f32[3,3,2,16]{3,2,1,0:T(2,128)}, f32[1,16]{1,0:T(1,128)}, f32[5,3,3,16,64]{4,3,2,1,0:T(8,128)}, f32[5,16]{1,0:T(...) custom-call(bf16[432,128]{1,0:T(8,128)(2,1)S(1)} %add_convert_fusion.1.low_ref, ...), custom_call_target="tpu_custom_call" | custom-call | tf_op jit(solution)/shard_map/finish/pallas_call | solution.py:748
  (20 shorter events, 0.8 us)
Async XLA Ops:
  0.6 1.0 %copy-start = (f32[2,4,32,256]{3,2,1,0:T(8,128)S(1)}, f32[2,4,32,256]{3,2,1,0:T(8,128)}, u32[]{:S(2)}) copy-start(f32[2,4,32,256]{3,2,1,0:T(8,128)} %param.24) | copy-start | bytes 786436
  2.3 18.6 %all-to-all-start = ((bf16[8,2,32,256]{3,2,1,0:T(8,128)(2,1)}), bf16[8,2,32,256]{3,2,1,0:T(8,128)(2,1)S(1)}, u32[]{:S(2)}, u32[]{:S(2)}) async-start(bf16[8,2,32,256]{3,2,1,0:T(8,128)(2,1)} %broadcast_in_dim.17), calls=%async_computation | async-start | bytes 524288 | tf_op jit(solution)/shard_map/all_to_all | solution.py:681
  11.0 8.6 %collective-permute-start = (bf16[304,256]{1,0:T(8,128)(2,1)S(1)}, bf16[304,256]{1,0:T(8,128)(2,1)S(1)}, u32[]{:S(2)}, u32[]{:S(2)}) collective-permute-start(bf16[304,256]{1,0:T(8,128)(2,1)S(1)} %get-tuple-element.38.w0), channel_id=1, source_target_pairs={{0,16},{8,24},{16,0},{24,8},{1,17},{9,25},{17,1},{25,9},{2,18},{10... | collective-permute-start | bytes 466952 | tf_op jit(solution)/shard_map/ppermute | solution.py:601
  12.5 7.1 %collective-permute-start.1 = (f32[2,16,256]{2,1,0:T(8,128)S(1)}, f32[2,16,256]{2,1,0:T(8,128)S(1)}, u32[]{:S(2)}, u32[]{:S(2)}) collective-permute-start(f32[2,16,256]{2,1,0:T(8,128)S(1)} %get-tuple-element.39), channel_id=1, source_target_pairs={{0,1},{1,2},{2,3},{3,4},{4,5},{5,6},{6,7},{7,0},{8,9},{9,10},{10,1... | collective-permute-start | bytes 98312 | tf_op jit(solution)/shard_map/ppermute | solution.py:596
  14.5 5.1 %collective-permute-start.2 = (f32[2,16,256]{2,1,0:T(8,128)S(1)}, f32[2,16,256]{2,1,0:T(8,128)S(1)}, u32[]{:S(2)}, u32[]{:S(2)}) collective-permute-start(f32[2,16,256]{2,1,0:T(8,128)S(1)} %get-tuple-element.40), channel_id=1, source_target_pairs={{0,7},{1,0},{2,1},{3,2},{4,3},{5,4},{6,5},{7,6},{8,15},{9,8},{10,9... | collective-permute-start | bytes 98312 | tf_op jit(solution)/shard_map/ppermute | solution.py:596
  17.2 2.4 %collective-permute-start.3 = (bf16[304,256]{1,0:T(8,128)(2,1)S(1)}, bf16[304,256]{1,0:T(8,128)(2,1)S(1)}, u32[]{:S(2)}, u32[]{:S(2)}) collective-permute-start(bf16[304,256]{1,0:T(8,128)(2,1)S(1)} %get-tuple-element.38.w0), channel_id=1, source_target_pairs={{0,8},{8,0},{16,24},{24,16},{1,9},{9,1},{17,25},{25,17},{2,10},{10... | collective-permute-start | bytes 466952 | tf_op jit(solution)/shard_map/ppermute | solution.py:601
  19.6 1.4 %collective-permute-start.4 = (bf16[304,256]{1,0:T(8,128)(2,1)S(1)}, bf16[304,256]{1,0:T(8,128)(2,1)S(1)}, u32[]{:S(2)}, u32[]{:S(2)}) collective-permute-start(bf16[304,256]{1,0:T(8,128)(2,1)S(1)} %collective-permute-done.w2), channel_id=1, source_target_pairs={{0,8},{8,0},{16,24},{24,16},{1,9},{9,1},{17,25},{25,17},{2,10},{10... | collective-permute-start | bytes 466952 | tf_op jit(solution)/shard_map/ppermute | solution.py:601
  49.6 1.5 %collective-permute-start.5 = (bf16[2,432,128]{2,1,0:T(8,128)(2,1)S(1)}, bf16[2,432,128]{2,1,0:T(8,128)(2,1)S(1)}, u32[]{:S(2)}, u32[]{:S(2)}) collective-permute-start(bf16[2,432,128]{2,1,0:T(8,128)(2,1)S(1)} %get-tuple-element.46), channel_id=1, source_target_pairs={{0,8},{8,0},{16,24},{24,16},{1,9},{9,1},{17,25},{25,17},{2,10},{10... | collective-permute-start | bytes 663560 | tf_op jit(solution)/shard_map/ppermute | solution.py:601
  51.2 6.1 %collective-permute-start.6 = (bf16[432,128]{1,0:T(8,128)(2,1)S(1)}, bf16[432,128]{1,0:T(8,128)(2,1)S(1)}, u32[]{:S(2)}, u32[]{:S(2)}) collective-permute-start(bf16[432,128]{1,0:T(8,128)(2,1)S(1)} %slice_bitcast_fusion), channel_id=1, source_target_pairs={{0,16},{8,24},{16,0},{24,8},{1,17},{9,25},{17,1},{25,9},{2,18},{10... | collective-permute-start | bytes 331784 | tf_op jit(solution)/shard_map/ppermute | solution.py:601
  52.8 13.6 %all-to-all-start.1 = ((bf16[8,2,32,256]{3,2,1,0:T(8,128)(2,1)}), bf16[8,2,32,256]{3,2,1,0:T(8,128)(2,1)S(1)}, u32[]{:S(2)}, u32[]{:S(2)}) async-start(bf16[8,2,32,256]{3,2,1,0:T(8,128)(2,1)} %get-tuple-element.47), calls=%async_computation.1 | async-start | bytes 524288 | tf_op jit(solution)/shard_map/all_to_all | solution.py:723
  57.4 7.0 %collective-permute-start.7 = (bf16[432,128]{1,0:T(8,128)(2,1)S(1)}, bf16[432,128]{1,0:T(8,128)(2,1)S(1)}, u32[]{:S(2)}, u32[]{:S(2)}) collective-permute-start(bf16[432,128]{1,0:T(8,128)(2,1)S(1)} %fusion), channel_id=1, source_target_pairs={{0,1},{1,0},{2,3},{3,2},{4,5},{5,4},{6,7},{7,6},{8,9},{9,8},{10,11... | collective-permute-start | bytes 331784 | tf_op jit(solution)/shard_map/ppermute | solution.py:601
  64.5 4.8 %collective-permute-start.8 = (bf16[432,128]{1,0:T(8,128)(2,1)S(1)}, bf16[432,128]{1,0:T(8,128)(2,1)S(1)}, u32[]{:S(2)}, u32[]{:S(2)}) collective-permute-start(bf16[432,128]{1,0:T(8,128)(2,1)S(1)} %add_convert_fusion.2), channel_id=1, source_target_pairs={{0,2},{1,3},{2,0},{3,1},{4,6},{5,7},{6,4},{7,5},{8,10},{9,11},{10,... | collective-permute-start | bytes 331784 | tf_op jit(solution)/shard_map/ppermute | solution.py:601
  67.8 4.4 %collective-permute-start.11 = (f32[72,256]{1,0:T(8,128)S(1)}, f32[72,256]{1,0:T(8,128)S(1)}, u32[]{:S(2)}, u32[]{:S(2)}) collective-permute-start(f32[72,256]{1,0:T(8,128)S(1)} %project.1.n0), channel_id=1, source_target_pairs={{0,16},{8,24},{16,0},{24,8},{1,17},{9,25},{17,1},{25,9},{2,18},{10... | collective-permute-start | bytes 221192 | tf_op jit(solution)/shard_map/ppermute | solution.py:601
  69.4 6.9 %collective-permute-start.9 = (bf16[432,128]{1,0:T(8,128)(2,1)S(1)}, bf16[432,128]{1,0:T(8,128)(2,1)S(1)}, u32[]{:S(2)}, u32[]{:S(2)}) collective-permute-start(bf16[432,128]{1,0:T(8,128)(2,1)S(1)} %add_convert_fusion.1.low_ref), channel_id=1, source_target_pairs={{0,4},{1,5},{2,6},{3,7},{4,0},{5,1},{6,2},{7,3},{8,12},{9,13},{10,... | collective-permute-start | bytes 331784 | tf_op jit(solution)/shard_map/ppermute | solution.py:601
  72.1 1.3 %collective-permute-start.10 = (f32[72,256]{1,0:T(8,128)S(1)}, f32[72,256]{1,0:T(8,128)S(1)}, u32[]{:S(2)}, u32[]{:S(2)}) collective-permute-start(f32[72,256]{1,0:T(8,128)S(1)} %project.1.n0), channel_id=1, source_target_pairs={{0,8},{8,0},{16,24},{24,16},{1,9},{9,1},{17,25},{25,17},{2,10},{10... | collective-permute-start | bytes 221192 | tf_op jit(solution)/shard_map/ppermute | solution.py:601
  72.2 1.3 %collective-permute-start.12 = (f32[72,256]{1,0:T(8,128)S(1)}, f32[72,256]{1,0:T(8,128)S(1)}, u32[]{:S(2)}, u32[]{:S(2)}) collective-permute-start(f32[72,256]{1,0:T(8,128)S(1)} %collective-permute-done.11.n2), channel_id=1, source_target_pairs={{0,8},{8,0},{16,24},{24,16},{1,9},{9,1},{17,25},{25,17},{2,10},{10... | collective-permute-start | bytes 221192 | tf_op jit(solution)/shard_map/ppermute | solution.py:601

commit v7 on v6

--- a/solution.py
+++ b/solution.py
@@ -675,9 +675,8 @@
     )
     across = swapped(packed, "chan", 2)
     up, down = halos(own, top, bottom, HALO)
-    across, up, down = lax.optimization_barrier((across, up, down))
     beside = swapped(packed, "chan", 1)
-    diagonal = swapped(across, "chan", 1)
+    diagonal = swapped(packed, "chan", 3)
     cot_full = lax.all_to_all(cot_all, "space", 0, 0, tiled=True)
     if h % 8:
         cot_full = cot_full.reshape(space * 2 * h, nx)

time: 77.6 us -> 76.6 us (0.987)
  waiting for transfers between devices: 13.4 us -> 11.5 us
  starting transfers between devices: 28.3 us -> 29.3 us
    ppermute x11, waiting for transfers between devices: 10.8 us -> 9.23 us  [swapped(): return lax.ppermute(x, axis, [(i, i ^ bit) for i in range(n)])]
    all_to_all x1, starting transfers between devices: 4.56 us -> 5.52 us  [per_device(): everywhere = lax.all_to_all(prov, 'space', 0, 0, tiled=True)]
  transfers between devices with their start and end apart: 15 -> 15, of which waited for: 9 -> 8; matrix products, arithmetic and copies ran while one was open for 1% -> 1% of each run, Pallas kernels for 4% -> 4%
where the time goes in v7:
time: 76.6 us; the launch traced here: 76.2 us
  Pallas kernels  32.3 us (42%)
  starting transfers between devices  29.3 us (38%)
  waiting for transfers between devices  11.5 us (15%)
  local copies, waits for them, and re-layouts  2.32 us (3%)
    pallas_call x1, Pallas kernels, per_device(): pl.pallas_call(functools.partial(step_kernel, h), out_shape=[inside((spac...  28.6 us
    ppermute x11, starting transfers between devices, swapped(): return lax.ppermute(x, axis, [(i, i ^ bit) for i in range(n)])  11.7 us
    ppermute x11, waiting for transfers between devices, swapped(): return lax.ppermute(x, axis, [(i, i ^ bit) for i in range(n)])  9.23 us
    all_to_all x1, starting transfers between devices, per_device(): cot_full = lax.all_to_all(cot_all, 'space', 0, 0, tiled=True)  7.28 us
    all_to_all x1, starting transfers between devices, per_device(): everywhere = lax.all_to_all(prov, 'space', 0, 0, tiled=True)  5.52 us
    ppermute x2, starting transfers between devices, moved(): return lax.ppermute(x, axis, [(i, (i + step) % n) for i in range(n)])  4.72 us
    ppermute x2, waiting for transfers between devices, moved(): return lax.ppermute(x, axis, [(i, (i + step) % n) for i in range(n)])  2 us
    unnamed x3, local copies, waits for them, and re-layouts  1.57 us
  transfers between devices with their start and end apart: 15, of which 8 were waited for; matrix products, arithmetic and copies ran while one was open for 1% of the time, Pallas kernels for 4%

profile of v7, /device:TPU:0, one launch (start us, length us, event | category | flops | bytes accessed | tf_op | source)
XLA Modules:
  0.0 76.2 jit_solution(16957282424697042675)
XLA Ops:
  0.7 0.9 %copy-done = f32[2,4,32,256]{3,2,1,0:T(8,128)S(1)} copy-done((f32[2,4,32,256]{3,2,1,0:T(8,128)S(1)}, f32[2,4,32,256]{3,2,1,0:T(8,128)}, u32[]{:S(2)}) %copy-start) | copy-done | bytes 262168
  1.6 0.7 broadcast_in_dim.17
  2.3 7.3 %all-to-all-start = ((bf16[8,2,32,256]{3,2,1,0:T(8,128)(2,1)}), bf16[8,2,32,256]{3,2,1,0:T(8,128)(2,1)S(1)}, u32[]{:S(2)}, u32[]{:S(2)}) async-start(bf16[8,2,32,256]{3,2,1,0:T(8,128)(2,1)} %broadcast_in_dim.17), calls=%async_computation | async-start | bytes 524288 | tf_op jit(solution)/shard_map/all_to_all | solution.py:680
  9.6 1.3 %prepare.1 = (bf16[304,256]{1,0:T(8,128)(2,1)S(1)}, f32[2,32,256]{2,1,0:T(8,128)S(1)}, f32[2,16,256]{2,1,0:T(8,128)S(1)}, f32[2,16,256]{2,1,0:T(8,128)S(1)}, f32[32,32]{1,0:T(8,128)S(1)}) custom-call(f32[2,4,32,256]{3,2,1,0:T(8,128)} %vel_ref.1, bf16[5,3,3,16,64]{4,3,2,1,0:T(8,128)(2,1)} %bitcast.22, bf16[3,3,8,64]{3,2,1,0:T(8,128)(2,1)} %bitcast.23, ...), custom_call_target="tpu_custom_call" | custom-call | tf_op jit(solution)/shard_map/prepare/pallas_call | solution.py:653
  11.0 0.7 collective-permute-start.4
  11.7 0.9 %collective-permute-start.3 = (bf16[304,256]{1,0:T(8,128)(2,1)S(1)}, bf16[304,256]{1,0:T(8,128)(2,1)S(1)}, u32[]{:S(2)}, u32[]{:S(2)}) collective-permute-start(bf16[304,256]{1,0:T(8,128)(2,1)S(1)} %get-tuple-element.37.w0), channel_id=1, source_target_pairs={{0,16},{8,24},{16,0},{24,8},{1,17},{9,25},{17,1},{25,9},{2,18},{10... | collective-permute-start | bytes 466952 | tf_op jit(solution)/shard_map/ppermute | solution.py:601
  12.9 2.0 %collective-permute-start = (f32[2,16,256]{2,1,0:T(8,128)S(1)}, f32[2,16,256]{2,1,0:T(8,128)S(1)}, u32[]{:S(2)}, u32[]{:S(2)}) collective-permute-start(f32[2,16,256]{2,1,0:T(8,128)S(1)} %get-tuple-element.35), channel_id=1, source_target_pairs={{0,1},{1,2},{2,3},{3,4},{4,5},{5,6},{6,7},{7,0},{8,9},{9,10},{10,1... | collective-permute-start | bytes 98312 | tf_op jit(solution)/shard_map/ppermute | solution.py:596
  14.9 2.7 %collective-permute-start.1 = (f32[2,16,256]{2,1,0:T(8,128)S(1)}, f32[2,16,256]{2,1,0:T(8,128)S(1)}, u32[]{:S(2)}, u32[]{:S(2)}) collective-permute-start(f32[2,16,256]{2,1,0:T(8,128)S(1)} %get-tuple-element.36), channel_id=1, source_target_pairs={{0,7},{1,0},{2,1},{3,2},{4,3},{5,4},{6,5},{7,6},{8,15},{9,8},{10,9... | collective-permute-start | bytes 98312 | tf_op jit(solution)/shard_map/ppermute | solution.py:596
  17.6 2.0 %collective-permute-done.up_ref = f32[2,16,256]{2,1,0:T(8,128)S(1)} collective-permute-done((f32[2,16,256]{2,1,0:T(8,128)S(1)}, f32[2,16,256]{2,1,0:T(8,128)S(1)}, u32[]{:S(2)}, u32[]{:S(2)}) %collective-permute-start) | collective-permute-done | bytes 32800 | tf_op jit(solution)/shard_map/ppermute | solution.py:596
  19.6 1.1 %collective-permute-done.3.w2 = bf16[304,256]{1,0:T(8,128)(2,1)S(1)} collective-permute-done((bf16[304,256]{1,0:T(8,128)(2,1)S(1)}, bf16[304,256]{1,0:T(8,128)(2,1)S(1)}, u32[]{:S(2)}, u32[]{:S(2)}) %collective-permute-start.3) | collective-permute-done | bytes 155680 | tf_op jit(solution)/shard_map/ppermute | solution.py:601
  20.7 28.6 %step.1 = (bf16[8,2,32,256]{3,2,1,0:T(8,128)(2,1)}, f32[2,32,256]{2,1,0:T(8,128)S(1)}, bf16[2,432,128]{2,1,0:T(8,128)(2,1)S(1)}, bf16[2,432,128]{2,1,0:T(8,128)(...) custom-call(f32[2,32,256]{2,1,0:T(8,128)S(1)} %get-tuple-element.34., ...), custom_call_target="tpu_custom_call" | custom-call | flops 22196256768 | bytes 33554432 | tf_op jit(solution)/shard_map/step/pallas_call | solution.py:687
  49.4 1.4 %collective-permute-done.5 = bf16[2,432,128]{2,1,0:T(8,128)(2,1)S(1)} collective-permute-done((bf16[2,432,128]{2,1,0:T(8,128)(2,1)S(1)}, bf16[2,432,128]{2,1,0:T(8,128)(2,1)S(1)}, u32[]{:S(2)}, u32[]{:S(2)}) %collective-permute-start.5) | collective-permute-done | bytes 221216 | tf_op jit(solution)/shard_map/ppermute | solution.py:601
  50.9 1.0 %collective-permute-start.6 = (bf16[432,128]{1,0:T(8,128)(2,1)S(1)}, bf16[432,128]{1,0:T(8,128)(2,1)S(1)}, u32[]{:S(2)}, u32[]{:S(2)}) collective-permute-start(bf16[432,128]{1,0:T(8,128)(2,1)S(1)} %slice_bitcast_fusion), channel_id=1, source_target_pairs={{0,16},{8,24},{16,0},{24,8},{1,17},{9,25},{17,1},{25,9},{2,18},{10... | collective-permute-start | bytes 331784 | tf_op jit(solution)/shard_map/ppermute | solution.py:601
  52.0 5.5 %all-to-all-start.1 = ((bf16[8,2,32,256]{3,2,1,0:T(8,128)(2,1)}), bf16[8,2,32,256]{3,2,1,0:T(8,128)(2,1)S(1)}, u32[]{:S(2)}, u32[]{:S(2)}) async-start(bf16[8,2,32,256]{3,2,1,0:T(8,128)(2,1)} %get-tuple-element.41), calls=%async_computation.1 | async-start | bytes 524288 | tf_op jit(solution)/shard_map/all_to_all | solution.py:722
  57.5 2.1 %collective-permute-start.7 = (bf16[432,128]{1,0:T(8,128)(2,1)S(1)}, bf16[432,128]{1,0:T(8,128)(2,1)S(1)}, u32[]{:S(2)}, u32[]{:S(2)}) collective-permute-start(bf16[432,128]{1,0:T(8,128)(2,1)S(1)} %fusion), channel_id=1, source_target_pairs={{0,1},{1,0},{2,3},{3,2},{4,5},{5,4},{6,7},{7,6},{8,9},{9,8},{10,11... | collective-permute-start | bytes 331784 | tf_op jit(solution)/shard_map/ppermute | solution.py:601
  59.6 5.0 %collective-permute-done.7 = bf16[432,128]{1,0:T(8,128)(2,1)S(1)} collective-permute-done((bf16[432,128]{1,0:T(8,128)(2,1)S(1)}, bf16[432,128]{1,0:T(8,128)(2,1)S(1)}, u32[]{:S(2)}, u32[]{:S(2)}) %collective-permute-start.7) | collective-permute-done | bytes 110624 | tf_op jit(solution)/shard_map/ppermute | solution.py:601
  64.6 1.8 %collective-permute-start.8 = (bf16[432,128]{1,0:T(8,128)(2,1)S(1)}, bf16[432,128]{1,0:T(8,128)(2,1)S(1)}, u32[]{:S(2)}, u32[]{:S(2)}) collective-permute-start(bf16[432,128]{1,0:T(8,128)(2,1)S(1)} %add_convert_fusion.2), channel_id=1, source_target_pairs={{0,2},{1,3},{2,0},{3,1},{4,6},{5,7},{6,4},{7,5},{8,10},{9,11},{10,... | collective-permute-start | bytes 331784 | tf_op jit(solution)/shard_map/ppermute | solution.py:601
  66.6 1.4 %project.1.n0 = f32[72,256]{1,0:T(8,128)S(1)} custom-call(bf16[8,2,32,256]{3,2,1,0:T(8,128)(2,1)S(1)} %all-to-all-done.1.prov_ref, f32[256,256]{1,0:T(8,128)S(1)} %get-tuple-element.42.tx_ref, f32[256,256]{1,0:T(8,128)S(1)} %get-tuple-element.43.ty_ref, f32[256,256]{1,0:T(8,128)S(1)} %get-tuple-element.44.back_ref, ...), custom_call_target="tpu_custom_call" | custom-call | flops 2147483648 | bytes 4194304 | tf_op jit(solution)/shard_map/project/pallas_call | solution.py:726
  68.0 1.5 %collective-permute-start.11 = (f32[72,256]{1,0:T(8,128)S(1)}, f32[72,256]{1,0:T(8,128)S(1)}, u32[]{:S(2)}, u32[]{:S(2)}) collective-permute-start(f32[72,256]{1,0:T(8,128)S(1)} %project.1.n0), channel_id=1, source_target_pairs={{0,16},{8,24},{16,0},{24,8},{1,17},{9,25},{17,1},{25,9},{2,18},{10... | collective-permute-start | bytes 221192 | tf_op jit(solution)/shard_map/ppermute | solution.py:601
  69.5 2.8 %collective-permute-start.9 = (bf16[432,128]{1,0:T(8,128)(2,1)S(1)}, bf16[432,128]{1,0:T(8,128)(2,1)S(1)}, u32[]{:S(2)}, u32[]{:S(2)}) collective-permute-start(bf16[432,128]{1,0:T(8,128)(2,1)S(1)} %add_convert_fusion.1.low_ref), channel_id=1, source_target_pairs={{0,4},{1,5},{2,6},{3,7},{4,0},{5,1},{6,2},{7,3},{8,12},{9,13},{10,... | collective-permute-start | bytes 331784 | tf_op jit(solution)/shard_map/ppermute | solution.py:601
  72.4 0.5 collective-permute-start.12
  72.9 0.6 copy.26
  73.8 1.5 %collective-permute-done.9.other_ref = bf16[432,128]{1,0:T(8,128)(2,1)S(1)} collective-permute-done((bf16[432,128]{1,0:T(8,128)(2,1)S(1)}, bf16[432,128]{1,0:T(8,128)(2,1)S(1)}, u32[]{:S(2)}, u32[]{:S(2)}) %collective-permute-start.9) | collective-permute-done | bytes 110624 | tf_op jit(solution)/shard_map/ppermute | solution.py:601
  75.3 0.9 %finish.1 = (f32[2,4,32,256]{3,2,1,0:T(8,128)}, f32[3,3,2,16]{3,2,1,0:T(2,128)}, f32[1,16]{1,0:T(1,128)}, f32[5,3,3,16,64]{4,3,2,1,0:T(8,128)}, f32[5,16]{1,0:T(...) custom-call(bf16[432,128]{1,0:T(8,128)(2,1)S(1)} %add_convert_fusion.1.low_ref, ...), custom_call_target="tpu_custom_call" | custom-call | tf_op jit(solution)/shard_map/finish/pallas_call | solution.py:747
  (20 shorter events, 1.2 us)
Async XLA Ops:
  0.6 1.0 %copy-start = (f32[2,4,32,256]{3,2,1,0:T(8,128)S(1)}, f32[2,4,32,256]{3,2,1,0:T(8,128)}, u32[]{:S(2)}) copy-start(f32[2,4,32,256]{3,2,1,0:T(8,128)} %param.24) | copy-start | bytes 786436
  2.3 18.3 %all-to-all-start = ((bf16[8,2,32,256]{3,2,1,0:T(8,128)(2,1)}), bf16[8,2,32,256]{3,2,1,0:T(8,128)(2,1)S(1)}, u32[]{:S(2)}, u32[]{:S(2)}) async-start(bf16[8,2,32,256]{3,2,1,0:T(8,128)(2,1)} %broadcast_in_dim.17), calls=%async_computation | async-start | bytes 524288 | tf_op jit(solution)/shard_map/all_to_all | solution.py:680
  11.0 8.6 %collective-permute-start.4 = (bf16[304,256]{1,0:T(8,128)(2,1)S(1)}, bf16[304,256]{1,0:T(8,128)(2,1)S(1)}, u32[]{:S(2)}, u32[]{:S(2)}) collective-permute-start(bf16[304,256]{1,0:T(8,128)(2,1)S(1)} %get-tuple-element.37.w0), channel_id=1, source_target_pairs={{0,24},{8,16},{16,8},{24,0},{1,25},{9,17},{17,9},{25,1},{2,26},{10... | collective-permute-start | bytes 466952 | tf_op jit(solution)/shard_map/ppermute | solution.py:601
  11.7 9.0 %collective-permute-start.3 = (bf16[304,256]{1,0:T(8,128)(2,1)S(1)}, bf16[304,256]{1,0:T(8,128)(2,1)S(1)}, u32[]{:S(2)}, u32[]{:S(2)}) collective-permute-start(bf16[304,256]{1,0:T(8,128)(2,1)S(1)} %get-tuple-element.37.w0), channel_id=1, source_target_pairs={{0,16},{8,24},{16,0},{24,8},{1,17},{9,25},{17,1},{25,9},{2,18},{10... | collective-permute-start | bytes 466952 | tf_op jit(solution)/shard_map/ppermute | solution.py:601
  12.6 8.1 %collective-permute-start.2 = (bf16[304,256]{1,0:T(8,128)(2,1)S(1)}, bf16[304,256]{1,0:T(8,128)(2,1)S(1)}, u32[]{:S(2)}, u32[]{:S(2)}) collective-permute-start(bf16[304,256]{1,0:T(8,128)(2,1)S(1)} %get-tuple-element.37.w0), channel_id=1, source_target_pairs={{0,8},{8,0},{16,24},{24,16},{1,9},{9,1},{17,25},{25,17},{2,10},{10... | collective-permute-start | bytes 466952 | tf_op jit(solution)/shard_map/ppermute | solution.py:601
  12.9 6.7 %collective-permute-start = (f32[2,16,256]{2,1,0:T(8,128)S(1)}, f32[2,16,256]{2,1,0:T(8,128)S(1)}, u32[]{:S(2)}, u32[]{:S(2)}) collective-permute-start(f32[2,16,256]{2,1,0:T(8,128)S(1)} %get-tuple-element.35), channel_id=1, source_target_pairs={{0,1},{1,2},{2,3},{3,4},{4,5},{5,6},{6,7},{7,0},{8,9},{9,10},{10,1... | collective-permute-start | bytes 98312 | tf_op jit(solution)/shard_map/ppermute | solution.py:596
  14.9 4.7 %collective-permute-start.1 = (f32[2,16,256]{2,1,0:T(8,128)S(1)}, f32[2,16,256]{2,1,0:T(8,128)S(1)}, u32[]{:S(2)}, u32[]{:S(2)}) collective-permute-start(f32[2,16,256]{2,1,0:T(8,128)S(1)} %get-tuple-element.36), channel_id=1, source_target_pairs={{0,7},{1,0},{2,1},{3,2},{4,3},{5,4},{6,5},{7,6},{8,15},{9,8},{10,9... | collective-permute-start | bytes 98312 | tf_op jit(solution)/shard_map/ppermute | solution.py:596
  49.3 1.5 %collective-permute-start.5 = (bf16[2,432,128]{2,1,0:T(8,128)(2,1)S(1)}, bf16[2,432,128]{2,1,0:T(8,128)(2,1)S(1)}, u32[]{:S(2)}, u32[]{:S(2)}) collective-permute-start(bf16[2,432,128]{2,1,0:T(8,128)(2,1)S(1)} %get-tuple-element.40), channel_id=1, source_target_pairs={{0,8},{8,0},{16,24},{24,16},{1,9},{9,1},{17,25},{25,17},{2,10},{10... | collective-permute-start | bytes 663560 | tf_op jit(solution)/shard_map/ppermute | solution.py:601
  50.9 6.5 %collective-permute-start.6 = (bf16[432,128]{1,0:T(8,128)(2,1)S(1)}, bf16[432,128]{1,0:T(8,128)(2,1)S(1)}, u32[]{:S(2)}, u32[]{:S(2)}) collective-permute-start(bf16[432,128]{1,0:T(8,128)(2,1)S(1)} %slice_bitcast_fusion), channel_id=1, source_target_pairs={{0,16},{8,24},{16,0},{24,8},{1,17},{9,25},{17,1},{25,9},{2,18},{10... | collective-permute-start | bytes 331784 | tf_op jit(solution)/shard_map/ppermute | solution.py:601
  52.0 14.7 %all-to-all-start.1 = ((bf16[8,2,32,256]{3,2,1,0:T(8,128)(2,1)}), bf16[8,2,32,256]{3,2,1,0:T(8,128)(2,1)S(1)}, u32[]{:S(2)}, u32[]{:S(2)}) async-start(bf16[8,2,32,256]{3,2,1,0:T(8,128)(2,1)} %get-tuple-element.41), calls=%async_computation.1 | async-start | bytes 524288 | tf_op jit(solution)/shard_map/all_to_all | solution.py:722
  57.5 7.1 %collective-permute-start.7 = (bf16[432,128]{1,0:T(8,128)(2,1)S(1)}, bf16[432,128]{1,0:T(8,128)(2,1)S(1)}, u32[]{:S(2)}, u32[]{:S(2)}) collective-permute-start(bf16[432,128]{1,0:T(8,128)(2,1)S(1)} %fusion), channel_id=1, source_target_pairs={{0,1},{1,0},{2,3},{3,2},{4,5},{5,4},{6,7},{7,6},{8,9},{9,8},{10,11... | collective-permute-start | bytes 331784 | tf_op jit(solution)/shard_map/ppermute | solution.py:601
  64.6 4.9 %collective-permute-start.8 = (bf16[432,128]{1,0:T(8,128)(2,1)S(1)}, bf16[432,128]{1,0:T(8,128)(2,1)S(1)}, u32[]{:S(2)}, u32[]{:S(2)}) collective-permute-start(bf16[432,128]{1,0:T(8,128)(2,1)S(1)} %add_convert_fusion.2), channel_id=1, source_target_pairs={{0,2},{1,3},{2,0},{3,1},{4,6},{5,7},{6,4},{7,5},{8,10},{9,11},{10,... | collective-permute-start | bytes 331784 | tf_op jit(solution)/shard_map/ppermute | solution.py:601
  68.0 4.4 %collective-permute-start.11 = (f32[72,256]{1,0:T(8,128)S(1)}, f32[72,256]{1,0:T(8,128)S(1)}, u32[]{:S(2)}, u32[]{:S(2)}) collective-permute-start(f32[72,256]{1,0:T(8,128)S(1)} %project.1.n0), channel_id=1, source_target_pairs={{0,16},{8,24},{16,0},{24,8},{1,17},{9,25},{17,1},{25,9},{2,18},{10... | collective-permute-start | bytes 221192 | tf_op jit(solution)/shard_map/ppermute | solution.py:601
  69.5 5.7 %collective-permute-start.9 = (bf16[432,128]{1,0:T(8,128)(2,1)S(1)}, bf16[432,128]{1,0:T(8,128)(2,1)S(1)}, u32[]{:S(2)}, u32[]{:S(2)}) collective-permute-start(bf16[432,128]{1,0:T(8,128)(2,1)S(1)} %add_convert_fusion.1.low_ref), channel_id=1, source_target_pairs={{0,4},{1,5},{2,6},{3,7},{4,0},{5,1},{6,2},{7,3},{8,12},{9,13},{10,... | collective-permute-start | bytes 331784 | tf_op jit(solution)/shard_map/ppermute | solution.py:601
  72.4 1.3 %collective-permute-start.10 = (f32[72,256]{1,0:T(8,128)S(1)}, f32[72,256]{1,0:T(8,128)S(1)}, u32[]{:S(2)}, u32[]{:S(2)}) collective-permute-start(f32[72,256]{1,0:T(8,128)S(1)} %project.1.n0), channel_id=1, source_target_pairs={{0,8},{8,0},{16,24},{24,16},{1,9},{9,1},{17,25},{25,17},{2,10},{10... | collective-permute-start | bytes 221192 | tf_op jit(solution)/shard_map/ppermute | solution.py:601
  72.4 1.4 %collective-permute-start.12 = (f32[72,256]{1,0:T(8,128)S(1)}, f32[72,256]{1,0:T(8,128)S(1)}, u32[]{:S(2)}, u32[]{:S(2)}) collective-permute-start(f32[72,256]{1,0:T(8,128)S(1)} %collective-permute-done.11.n2), channel_id=1, source_target_pairs={{0,8},{8,0},{16,24},{24,16},{1,9},{9,1},{17,25},{25,17},{2,10},{10... | collective-permute-start | bytes 221192 | tf_op jit(solution)/shard_map/ppermute | solution.py:601
